TPU v7x, 32 devices: a whole 2x2x4 slice. The times are simulated.
32 devices in a mesh: row: 4 (over x, core), col: 2 (over y), seq: 4 (over z).
Axes of the slice: x: 2, y: 2, z: 4, core: 2. Of those that a mesh axis runs over, the one named last changes fastest.
Arguments:
- left_piece: bfloat16 [512, 32, 256], P('seq', None, 'row'), may hold values from -6 to 6
- right_piece: bfloat16 [512, 32, 256], P('seq', 'row', 'col'), may hold values from -6 to 6
- proj_weight: bfloat16 [1024, 128], replicated, may hold values from -4 to 4
- proj_bias: float32 [128], replicated, may hold values from -3 to 3
- pair_rep: bfloat16 [256, 256, 128], P(('row', 'seq'), 'col'), may hold values from -6 to 6
- norm_gain: float32 [128], replicated, may hold values from 0.5 to 1.5
- up_weight: bfloat16 [128, 512], replicated, may hold values from -0.5 to 0.5
- up_bias: float32 [512], replicated, may hold values from -3 to 3
- down_weight: bfloat16 [512, 128], replicated, may hold values from -0.25 to 0.25
- down_bias: float32 [128], replicated, may hold values from -3 to 3
Outputs:
- refined: bfloat16 [256, 256, 128], P(('row', 'seq'), 'col')
All inputs are finite; a program needn't handle non-finite values.
Results may differ from a plain program's by a relative error of at most 0.0085.
Values may be sent and summed in bfloat16 or wider, within the bound.
No kernel may reach another device: no remote copies, remote signals or barrier semaphores. Data moves between devices by JAX's collectives and lax.ppermute only.
A program may use at most 64 MiB of HBM per device.

v0:
```python
import functools

import jax
import jax.numpy as jnp
from jax import lax
from jax.experimental import pallas as pl
from jax.experimental.pallas import tpu as pltpu
from jax.sharding import PartitionSpec as P

epsilon = 1e-05
axes = ("row", "col", "seq")


def update_kernel(places, shares, low, last, scale, *refs):
    blocks, data_count, right_places, share_rows, source_rows, group_len, run = places
    groups = len(right_places)
    sources = len(right_places[0])
    refs = list(refs)
    place_ref = refs.pop(0)
    left_refs = [refs.pop(0) for _ in range(2 * blocks if last else 1)]
    data_refs = [refs.pop(0) for _ in range(data_count)]
    bias_ref, weight_ref = refs.pop(0), refs.pop(0)
    first_ref = refs.pop(0) if last else None
    update_ref = refs.pop() if last else refs[0]
    outer_ref = refs.pop()
    lhs_ref = refs.pop() if last else left_refs[0]
    out_refs = refs
    row_count, _, lanes = outer_ref.shape
    low = groups // 2
    channels = share_rows * blocks // row_count
    share = share_rows // channels
    per = source_rows // group_len
    half = lanes // 2
    pair_channels = weight_ref.shape[0] // 2
    lane_low = lax.broadcasted_iota(jnp.int32, (pair_channels, lanes), 1) < half
    for block in range(blocks if last else 0):
        for dz in range(groups):
            lhs_ref[
                block * share_rows : (block + 1) * share_rows,
                dz * group_len : (dz + 1) * group_len,
            ] = left_refs[2 * block + dz // low][
                dz % low * share_rows : (dz % low + 1) * share_rows
            ]

    def right_tile(item):
        source, rest = divmod(item, per)
        tiles = []
        for dz in range(groups):
            operand, first = right_places[dz][source]
            first += rest * group_len
            tiles.append(data_refs[operand][first : first + group_len])
        return jnp.concatenate(tiles, axis=0)

    for pair in range(sources * per // 2):
        right = jnp.concatenate([right_tile(2 * pair), right_tile(2 * pair + 1)], axis=1)
        outer = jnp.dot(lhs_ref[...], right, preferred_element_type=jnp.float32)
        outer = outer.astype(jnp.bfloat16)
        for part in range(2):
            item = 2 * pair + part
            outer_ref[:, item * channels : (item + 1) * channels, :] = outer[
                :, part * lanes : (part + 1) * lanes
            ].reshape(row_count, channels, lanes)

    unroll = min(4, row_count // 2)

    @pl.loop(0, row_count // (2 * unroll))
    def _(step):
        for two in range(unroll):
            index = step * unroll + two
            both = jnp.concatenate([outer_ref[2 * index], outer_ref[2 * index + 1]], axis=1)
            proj = jnp.dot(weight_ref[...], both, preferred_element_type=jnp.float32)
            a0 = proj[:pair_channels, :lanes]
            a1 = proj[:pair_channels, lanes:]
            b0 = proj[pair_channels:, :lanes]
            b1 = proj[pair_channels:, lanes:]
            cell = jnp.where(lane_low, a0, b1) + pltpu.roll(
                jnp.where(lane_low, a1, b0), half, 1
            )
            cell = (cell * scale + bias_ref[...]).astype(jnp.bfloat16)
            begin = 2 * index
            if last:
                begin = (place_ref[2] ^ (1 + begin // share)) * share + begin % share
            update_ref[pl.ds(begin, 2)] = cell.T.reshape(2, half, pair_channels)

    if last:
        update_ref[pl.ds(place_ref[2] * share, share)] = first_ref[...]
        core, z_low, z_high = place_ref[0], place_ref[1], place_ref[3]
        out_refs[0][...] = update_ref[pl.ds(z_high * run, run)]
        out_refs[1][...] = update_ref[pl.ds((1 - z_high) * run, run)]
        for dz in range(low):
            for flip in range(2):
                begin = (core ^ flip) * (half // 2) + (z_low ^ dz) * run
                out_refs[2 + 2 * dz + flip][...] = update_ref[
                    :, pl.ds(pl.multiple_of(begin, run), run), :
                ]


def pack_kernel(*refs):
    rows = refs[0].shape[0]
    for index, ref in enumerate(refs[:-1]):
        refs[-1][index * rows : (index + 1) * rows] = ref[...]


def pack(*values):
    rows, lanes = values[0].shape
    return pl.pallas_call(
        pack_kernel,
        out_shape=jax.ShapeDtypeStruct((len(values) * rows, lanes), values[0].dtype),
        in_specs=[pl.BlockSpec(memory_space=pltpu.VMEM)] * len(values),
        out_specs=pl.BlockSpec(memory_space=pltpu.VMEM),
        compiler_params=pltpu.CompilerParams(vmem_limit_bytes=4 * 1024 * 1024),
        name="pack",
    )(*values)


def arrange_kernel(near_ref, far_ref, out_ref):
    rows, lanes = out_ref.shape[0], near_ref.shape[1]
    count = near_ref.shape[0] // rows
    for index in range(2 * count):
        ref = near_ref if index < count else far_ref
        begin = index % count * rows
        out_ref[:, index * lanes : (index + 1) * lanes] = ref[begin : begin + rows]


def arrange(lefts, groups):
    rows, lanes = lefts[0].shape
    rows //= groups // 2
    return pl.pallas_call(
        arrange_kernel,
        out_shape=jax.ShapeDtypeStruct((rows, groups * lanes), lefts[0].dtype),
        in_specs=[pl.BlockSpec(memory_space=pltpu.VMEM)] * 2,
        out_specs=pl.BlockSpec(memory_space=pltpu.VMEM),
        compiler_params=pltpu.CompilerParams(vmem_limit_bytes=4 * 1024 * 1024),
        cost_estimate=pl.CostEstimate(
            flops=rows * groups * lanes * 8 * lanes * groups * 1,
            bytes_accessed=4 * rows * groups * lanes,
            transcendentals=0,
        ),
        name="arrange",
    )(*lefts)


def finish_kernel(low, other, *refs):
    place_ref, pair_ref, direct_ref = refs[:3]
    mirror_refs = refs[3 : 3 + 2 * low]
    up_ref, down_ref, vector_ref, swap_ref = refs[3 + 2 * low : 7 + 2 * low]
    out_ref, done_ref, sems = refs[-3:]
    run, columns, pair_channels = pair_ref.shape
    half = columns // 2
    core, z_low, part = place_ref[0], place_ref[1], place_ref[3] ^ other
    cells = run * run
    gain = vector_ref[:, :pair_channels]
    down_bias = vector_ref[:, pair_channels : 2 * pair_channels]
    up_bias = vector_ref[:, 2 * pair_channels :]
    ones = jnp.full((2 * pair_channels, pair_channels), 1.0 / pair_channels, jnp.bfloat16)
    copies = []
    for dz in range(low):
        middles = []
        begins = []
        for flip in range(2):
            local = (core ^ flip) * (half // 2) + (z_low ^ dz) * run
            local = pl.multiple_of(local, run)
            begin = (core ^ flip) * half + (part * low + (z_low ^ dz)) * run
            begin = pl.multiple_of(begin, run)
            begins.append(begin)
            piece = mirror_refs[2 * dz + flip][pl.ds(part * run, run)]
            mirrored = jnp.dot(
                swap_ref[...],
                piece.reshape(cells, pair_channels),
                preferred_element_type=jnp.float32,
            )
            direct = direct_ref[:, pl.ds(local, run), :].reshape(cells, pair_channels)
            residual = pair_ref[:, pl.ds(begin, run), :].reshape(cells, pair_channels)
            middles.append(
                (
                    residual.astype(jnp.float32) + 0.5 * (direct.astype(jnp.float32) + mirrored)
                ).astype(jnp.bfloat16)
            )
        middle = jnp.concatenate(middles, axis=0)
        values = middle.astype(jnp.float32)
        center = jnp.dot(middle, ones[:pair_channels], preferred_element_type=jnp.float32)
        moved = values - center
        square = jnp.square(moved)
        high = square.astype(jnp.bfloat16)
        rest = (square - high.astype(jnp.float32)).astype(jnp.bfloat16)
        spread = jnp.dot(
            jnp.concatenate([high, rest], axis=1), ones, preferred_element_type=jnp.float32
        )
        normed = moved * lax.rsqrt(spread + epsilon) * gain
        hidden = jnp.dot(
            normed.astype(jnp.bfloat16), up_ref[...], preferred_element_type=jnp.float32
        )
        hidden = jnp.maximum(hidden + up_bias, 0.0).astype(jnp.bfloat16)
        result = jnp.dot(hidden, down_ref[...], preferred_element_type=jnp.float32)
        result = (values + result + down_bias).astype(jnp.bfloat16)
        for flip in range(2):
            index = 2 * dz + flip
            done_ref[index] = result[flip * cells : (flip + 1) * cells].reshape(
                run, run, pair_channels
            )
            copy = pltpu.make_async_copy(
                done_ref.at[index], out_ref.at[:, pl.ds(begins[flip], run), :], sems.at[index]
            )
            copy.start()
            copies.append(copy)
    for copy in copies:
        copy.wait()


def on_device(
    left_piece,
    right_piece,
    proj_weight,
    proj_bias,
    pair_rep,
    norm_gain,
    up_weight,
    up_bias,
    down_weight,
    down_bias,
):
    rows = lax.axis_size("row")
    cols = lax.axis_size("col")
    groups = lax.axis_size("seq")
    xs = rows // 2
    low = groups // 2
    row, col, seq = (lax.axis_index(name) for name in axes)
    core, z_low, z_high = row % 2, seq % low, seq // low
    run, columns, pair_channels = pair_rep.shape
    group_len, channels, _ = left_piece.shape
    e1 = right_piece.shape[1] // 2
    half = columns // 2
    bf16 = jnp.bfloat16

    def pick(value, index, axis=0):
        return lax.dynamic_index_in_dim(value, index, axis, False)

    def swap(value, name, size, flip):
        return lax.ppermute(value, name, [(i, i ^ flip) for i in range(size)])

    right = right_piece.reshape(group_len, e1, 2, 2, 2, half // 2).transpose(4, 1, 0, 2, 3, 5)
    source_rows = e1 * group_len
    right = right.reshape(2, source_rows, 2 * half)
    share_rows = 2 * run // cols * channels
    left = left_piece.transpose(2, 1, 0).reshape(2, low, run, channels, group_len)
    left = left.transpose(1, 0, 2, 3, 4).reshape(low, cols, share_rows, group_len)
    left = pick(left, col, 1)

    def after(value, *earlier):
        return lax.optimization_barrier((value, earlier))[0] if earlier else value

    mine, theirs = pick(right, z_high), pick(right, 1 - z_high)
    own, crossing = pick(left, z_low), pick(left, 1 - z_low)
    near = swap(crossing, "seq", groups, 1)
    blocks = {0: mine}
    blocks[low + 1] = swap(theirs, "seq", groups, low + 1)
    blocks[1] = swap(mine, "seq", groups, 1)
    blocks[low] = swap(blocks[low + 1], "seq", groups, 1)
    lefts = [pack(own, near)]
    lefts.append(swap(lefts[0], "seq", groups, low))
    shares = [[swap(lefts[0], "col", cols, dy)] for dy in range(1, cols)]
    first_lhs = arrange(lefts, groups)
    data = []
    right_places = {dz: [] for dz in range(groups)}
    order = (0, 1, low + 1, low)
    crosses = {dz: [blocks[dz]] for dz in order}
    last = ()
    for dz in order:
        for dx in range(1, xs):
            behind = last + (tuple(map(tuple, shares)) if dz == low else ())
            crosses[dz].append(swap(after(blocks[dz], *behind), "row", rows, 2 * dx))
            last = (crosses[dz][-1],)
    for position in range(xs):
        values = [crosses[dz][position] for dz in order]
        for dz, value in zip(order, values):
            right_places[dz].append((len(data), 0))
            data.append(value)
        count = len(order) if position == 0 else len(order) - 1
        exchanged = swap(pack(*values[:count]), "row", rows, 1)
        for index, dz in enumerate(order[:count]):
            right_places[dz].append((len(data), index * source_rows))
        data.append(exchanged)
        if count < len(order):
            right_places[low].append((len(data), 0))
            data.append(swap(after(values[-1], first_lhs), "row", rows, 1))
    for dy in range(1, cols):
        shares[dy - 1].append(swap(lefts[1], "col", cols, dy))
    right_places = [right_places[dz] for dz in range(groups)]
    last_lefts = [value for pair in shares for value in pair]

    weight = proj_weight.reshape(channels, rows, e1, 2, pair_channels)
    weight = weight.transpose(1, 3, 4, 2, 0)
    weight = jnp.stack([pick(weight, row ^ m) for m in range(rows)], axis=2)
    weight = weight.reshape(2 * pair_channels, channels * channels // 2)

    place = jnp.stack([core, z_low, col, z_high]).astype(jnp.int32)
    vmem = pl.BlockSpec(memory_space=pltpu.VMEM)
    smem = pl.BlockSpec(memory_space=pltpu.SMEM)
    params = pltpu.CompilerParams(vmem_limit_bytes=40 * 1024 * 1024)
    scale = 1.0 / (group_len * groups)
    bias = jnp.broadcast_to(proj_bias[:, None], (pair_channels, 2 * half))
    share = share_rows // channels

    def update_call(last, left_values, extra, out_shape, out_specs, scratch):
        blocks = max(len(left_values) // 2, 1)
        row_count = share * blocks
        outer_size = row_count * channels * channels * half
        places = (blocks, len(data), right_places, share_rows, source_rows, group_len, run)
        return pl.pallas_call(
            functools.partial(update_kernel, places, cols, low, last, scale),
            out_shape=out_shape,
            in_specs=[smem] + [vmem] * (len(left_values) + len(data) + 2 + len(extra)),
            out_specs=out_specs,
            scratch_shapes=scratch[:-1]
            + [
                pltpu.VMEM((row_count, channels * channels // 2, 2 * half), bf16),
            ]
            + scratch[-1:],
            compiler_params=params,
            cost_estimate=pl.CostEstimate(
                flops=2 * outer_size * (groups * group_len + 2 * pair_channels),
                bytes_accessed=2 * outer_size,
                transcendentals=0,
            ),
            name="update_last" if last else "update_first",
        )(place, *left_values, *data, bias, weight, *extra)

    first = update_call(
        False, [first_lhs], [], jax.ShapeDtypeStruct((share, half, pair_channels), bf16), vmem, []
    )
    outs = update_call(
        True,
        last_lefts,
        [first],
        [jax.ShapeDtypeStruct((run, half, pair_channels), bf16)] * 2
        + [jax.ShapeDtypeStruct((2 * run, run, pair_channels), bf16)] * (2 * low),
        [vmem] * (2 + 2 * low),
        [
            pltpu.VMEM(((2 * run - share) * channels, groups * group_len), bf16),
            pltpu.VMEM((2 * run, half, pair_channels), bf16),
        ],
    )

    mirrors = []
    for dz in range(low):
        for flip in range(2):
            pairs = []
            for r in range(rows):
                for c in range(cols):
                    for q in range(groups):
                        source = (r * cols + c) * groups + q
                        target = 2 * c + (r % 2 ^ flip)
                        target = (target * cols + r // 2) * groups + (q ^ dz)
                        pairs.append((source, target))
            mirrors.append(lax.ppermute(outs[2 + 2 * dz + flip], axes, pairs))
    update_other = swap(outs[1], "seq", groups, low)

    vectors = jnp.concatenate([norm_gain, down_bias, up_bias]).reshape(1, -1)
    cell = jnp.arange(run * run)
    mirror_cell = cell % run * run + cell // run
    swap_cells = (mirror_cell[:, None] == cell[None, :]).astype(bf16)
    anywhere = pl.BlockSpec(memory_space=pl.ANY)
    result = None
    for other in range(2):
        operands = [
            place,
            pair_rep,
            update_other if other else outs[0],
            *mirrors,
            up_weight,
            down_weight,
            vectors,
            swap_cells,
        ]
        extra = [] if result is None else [result]
        result = pl.pallas_call(
            functools.partial(finish_kernel, low, other),
            out_shape=jax.ShapeDtypeStruct(pair_rep.shape, bf16),
            in_specs=[smem] + [vmem] * (len(operands) - 1) + [anywhere] * len(extra),
            out_specs=anywhere,
            scratch_shapes=[
                pltpu.VMEM((2 * low, run, run, pair_channels), bf16),
                pltpu.SemaphoreType.DMA((2 * low,)),
            ],
            input_output_aliases={len(operands): 0} if extra else {},
            compiler_params=params,
            name="finish",
        )(*operands, *extra)
    return result


def solution(mesh):
    in_specs = (
        P("seq", None, "row"),
        P("seq", "row", "col"),
        P(),
        P(),
        P(("row", "seq"), "col", None),
        P(),
        P(),
        P(),
        P(),
        P(),
    )
    out_specs = P(("row", "seq"), "col", None)
    return jax.shard_map(
        on_device, mesh=mesh, in_specs=in_specs, out_specs=out_specs, check_vma=False
    )
```

profile of v0, /device:TPU:3, one launch (start us, length us, event | category | flops | bytes accessed | tf_op | source)
XLA Modules:
  0.0 68.8 jit_solution(18097503417100810449)
XLA Ops:
  0.0 1.1 %copy.19 = bf16[128,8,128]{0,2,1:T(8,128)(2,1)S(1)} copy(bf16[128,8,128]{2,1,0:T(8,128)(2,1)} %param.11) | data formatting | bytes 524288 | tf_op args[1]
  1.2 0.2 copy.20
  1.4 0.1 reshape.55
  1.5 0.1 copy.21
  1.7 1.4 %collective-permute-start.4 = (bf16[512,128]{1,0:T(8,128)(2,1)S(1)}, bf16[512,128]{1,0:T(8,128)(2,1)S(1)}, u32[]{:S(2)}, u32[]{:S(2)}) collective-permute-start(bf16[512,128]{1,0:T(8,128)(2,1)S(1)} %bitcast.45), channel_id=1, source_target_pairs={{0,1},{1,0},{2,3},{3,2},{4,5},{5,4},{6,7},{7,6},{8,9},{9,8},{10,11... | collective-permute-start | bytes 393224 | tf_op jit(solution)/shard_map/ppermute | solution.py:239
  3.0 0.3 collective-permute-start.8
  3.3 0.3 copy.18
  3.7 0.6 collective-permute-start
  4.3 0.1 copy.22
  4.4 3.0 %collective-permute-start.5 = (bf16[512,128]{1,0:T(8,128)(2,1)S(1)}, bf16[512,128]{1,0:T(8,128)(2,1)S(1)}, u32[]{:S(2)}, u32[]{:S(2)}) collective-permute-start(bf16[512,128]{1,0:T(8,128)(2,1)S(1)} %bitcast.56), channel_id=1, source_target_pairs={{0,3},{1,2},{2,1},{3,0},{4,7},{5,6},{6,5},{7,4},{8,11},{9,10},{10,... | collective-permute-start | bytes 393224 | tf_op jit(solution)/shard_map/ppermute | solution.py:239
  7.4 0.2 constant_dynamic-slice_fusion.3
  7.6 1.3 %collective-permute-start.9 = (bf16[512,128]{1,0:T(8,128)(2,1)S(1)}, bf16[512,128]{1,0:T(8,128)(2,1)S(1)}, u32[]{:S(2)}, u32[]{:S(2)}) collective-permute-start(bf16[512,128]{1,0:T(8,128)(2,1)S(1)} %collective-permute-done.4.refs_1_.refs_3_.refs_4_), channel_id=1, source_target_pairs={{0,16},{8,24},{16,0},{24,8},{1,17},{9,25},{17,1},{25,9},{2,18},{10... | collective-permute-start | bytes 393224 | tf_op jit(solution)/shard_map/ppermute | solution.py:239
  8.9 0.2 collective-permute-done.refs_1_
  9.1 1.3 %collective-permute-start.1 = (bf16[1024,128]{1,0:T(8,128)(2,1)S(1)}, bf16[1024,128]{1,0:T(8,128)(2,1)S(1)}, u32[]{:S(2)}, u32[]{:S(2)}) collective-permute-start(bf16[1024,128]{1,0:T(8,128)(2,1)S(1)} %pack.3.near_ref), channel_id=1, source_target_pairs={{0,4},{4,0},{1,5},{5,1},{2,6},{6,2},{3,7},{7,3},{8,12},{12,8},{9,1... | collective-permute-start | bytes 786440 | tf_op jit(solution)/shard_map/ppermute | solution.py:239
  10.4 3.5 %collective-permute-done.5.refs_2_.refs_4_.refs_5_ = bf16[512,128]{1,0:T(8,128)(2,1)S(1)} collective-permute-done((bf16[512,128]{1,0:T(8,128)(2,1)S(1)}, bf16[512,128]{1,0:T(8,128)(2,1)S(1)}, u32[]{:S(2)}, u32[]{:S(2)}) %collective-permute-start.5) | collective-permute-done | bytes 131104 | tf_op jit(solution)/shard_map/ppermute | solution.py:239
  13.9 0.1 copy_bitcast_fusion.1
  14.0 1.2 %collective-permute-start.2 = (bf16[1024,128]{1,0:T(8,128)(2,1)S(1)}, bf16[1024,128]{1,0:T(8,128)(2,1)S(1)}, u32[]{:S(2)}, u32[]{:S(2)}) collective-permute-start(bf16[1024,128]{1,0:T(8,128)(2,1)S(1)} %pack.3.near_ref), channel_id=1, source_target_pairs={{0,2},{1,3},{2,0},{3,1},{4,6},{5,7},{6,4},{7,5},{8,10},{9,11},{10,... | collective-permute-start | bytes 786440 | tf_op jit(solution)/shard_map/ppermute | solution.py:239
  15.2 4.2 %collective-permute-done.6.refs_3_.refs_5_.refs_6_ = bf16[512,128]{1,0:T(8,128)(2,1)S(1)} collective-permute-done((bf16[512,128]{1,0:T(8,128)(2,1)S(1)}, bf16[512,128]{1,0:T(8,128)(2,1)S(1)}, u32[]{:S(2)}, u32[]{:S(2)}) %collective-permute-start.6) | collective-permute-done | bytes 131104 | tf_op jit(solution)/shard_map/ppermute | solution.py:239
  19.5 2.6 %collective-permute-start.7 = (bf16[2048,128]{1,0:T(8,128)(2,1)S(1)}, bf16[2048,128]{1,0:T(8,128)(2,1)S(1)}, u32[]{:S(2)}, u32[]{:S(2)}) collective-permute-start(bf16[2048,128]{1,0:T(8,128)(2,1)S(1)} %pack.4), channel_id=1, source_target_pairs={{0,8},{8,0},{16,24},{24,16},{1,9},{9,1},{17,25},{25,17},{2,10},{10... | collective-permute-start | bytes 1572872 | tf_op jit(solution)/shard_map/ppermute | solution.py:239
  22.0 0.1 copy_bitcast_fusion.3
  22.2 0.1 collective-permute-start.11
  22.3 2.0 %collective-permute-start.12 = (bf16[1536,128]{1,0:T(8,128)(2,1)S(1)}, bf16[1536,128]{1,0:T(8,128)(2,1)S(1)}, u32[]{:S(2)}, u32[]{:S(2)}) collective-permute-start(bf16[1536,128]{1,0:T(8,128)(2,1)S(1)} %pack.5), channel_id=1, source_target_pairs={{0,8},{8,0},{16,24},{24,16},{1,9},{9,1},{17,25},{25,17},{2,10},{10... | collective-permute-start | bytes 1179656 | tf_op jit(solution)/shard_map/ppermute | solution.py:239
  24.3 0.5 pad_maximum_fusion
  24.8 2.6 %collective-permute-done.2.far_ref = bf16[1024,128]{1,0:T(8,128)(2,1)S(1)} collective-permute-done((bf16[1024,128]{1,0:T(8,128)(2,1)S(1)}, bf16[1024,128]{1,0:T(8,128)(2,1)S(1)}, u32[]{:S(2)}, u32[]{:S(2)}) %collective-permute-start.2) | collective-permute-done | bytes 262176 | tf_op jit(solution)/shard_map/ppermute | solution.py:239
  27.4 0.1 arrange.1.refs_1_
  27.5 0.8 %copy-done.3 = bf16[512,512]{1,0:T(8,128)(2,1)} copy-done((bf16[512,512]{1,0:T(8,128)(2,1)}, bf16[512,512]{1,0:T(8,128)(2,1)S(1)}, u32[]{:S(2)}) %copy-start.3) | copy-done | bytes 524312
  28.3 2.0 %collective-permute-start.13 = (bf16[512,128]{1,0:T(8,128)(2,1)}, bf16[512,128]{1,0:T(8,128)(2,1)}, u32[]{:S(2)}, u32[]{:S(2)}) collective-permute-start(bf16[512,128]{1,0:T(8,128)(2,1)} %collective-permute-done.11.refs_10_.refs_11_), channel_id=1, source_target_pairs={{0,8},{8,0},{16,24},{24,16},{1,9},{9,1},{17,25},{25,17},{2,10},{10... | collective-permute-start | bytes 393224 | tf_op jit(solution)/shard_map/ppermute | solution.py:239
  30.3 0.7 %copy.39 = bf16[64,8,2,128]{3,1,2,0:T(8,128)(2,1)} copy(bf16[64,8,2,128]{3,2,1,0:T(2,128)(2,1)S(1)} %bitcast.51) | data formatting | bytes 524288
  31.0 1.1 %copy.28.refs_14_.refs_15_ = bf16[256,512]{1,0:T(8,128)(2,1)S(1)} copy(bf16[256,512]{0,1:T(8,128)(2,1)} %bitcast.52) | data formatting | bytes 524288 | tf_op jit(solution)/shard_map/reshape | solution.py:294
  32.1 1.3 %collective-permute-start.3 = (bf16[1024,128]{1,0:T(8,128)(2,1)S(1)}, bf16[1024,128]{1,0:T(8,128)(2,1)S(1)}, u32[]{:S(2)}, u32[]{:S(2)}) collective-permute-start(bf16[1024,128]{1,0:T(8,128)(2,1)S(1)} %collective-permute-done.2.far_ref), channel_id=1, source_target_pairs={{0,4},{4,0},{1,5},{5,1},{2,6},{6,2},{3,7},{7,3},{8,12},{12,8},{9,1... | collective-permute-start | bytes 786440 | tf_op jit(solution)/shard_map/ppermute | solution.py:239
  33.4 0.1 pad_add_fusion.refs_0_
  33.5 0.6 copy-done.8
  34.1 0.1 broadcast_in_dim.2.refs_13_.refs_14_
  34.1 1.0 %copy-done.4 = bf16[512,512]{1,0:T(8,128)(2,1)S(1)} copy-done((bf16[512,512]{1,0:T(8,128)(2,1)S(1)}, bf16[512,512]{1,0:T(8,128)(2,1)}, u32[]{:S(2)}) %copy-start.4) | copy-done | bytes 524312
  35.2 3.4 %update_first.1.refs_16_ = bf16[16,64,128]{2,1,0:T(8,128)(2,1)S(1)} custom-call(s32[4]{0:T(128)S(1)} %pad_add_fusion.refs_0_, bf16[512,512]{1,0:T(8,128)(2,1)S(1)} %copy-done.4, bf16[512,128]{1,0:T(8,128)(2,1)S(1)} %bitcast.48, bf16[512,128]{1,0:T(8,128)(2,1)S(1)} %collective-permute-done.4.refs_1_.refs_3_.refs_4_, ...), custom_call_target="tpu_custom_call" | custom-call | flops 1610612736 | bytes 2097152 | tf_op jit(solution)/shard_map/update_first/pallas_call | solution.py:309
  38.6 1.5 %collective-permute-done.3.refs_2_ = bf16[1024,128]{1,0:T(8,128)(2,1)S(1)} collective-permute-done((bf16[1024,128]{1,0:T(8,128)(2,1)S(1)}, bf16[1024,128]{1,0:T(8,128)(2,1)S(1)}, u32[]{:S(2)}, u32[]{:S(2)}) %collective-permute-start.3) | collective-permute-done | bytes 262176 | tf_op jit(solution)/shard_map/ppermute | solution.py:239
  40.1 3.6 %update_last.1 = (bf16[16,64,128]{2,1,0:T(8,128)(2,1)S(1)}, bf16[16,64,128]{2,1,0:T(8,128)(2,1)S(1)}, bf16[32,16,128]{2,1,0:T(8,128)(2,1)S(1)}, bf16[32,16,128]{...) custom-call(s32[4]{0:T(128)S(1)} %pad_add_fusion.refs_0_, ...), custom_call_target="tpu_custom_call" | custom-call | flops 1610612736 | bytes 2097152 | tf_op jit(solution)/shard_map/update_last/pallas_call | solution.py:309
  43.7 0.1 collective-permute-start.14
  43.8 2.2 %collective-permute-start.15 = (bf16[32,16,128]{2,1,0:T(8,128)(2,1)S(1)}, bf16[32,16,128]{2,1,0:T(8,128)(2,1)S(1)}, u32[]{:S(2)}, u32[]{:S(2)}) collective-permute-start(bf16[32,16,128]{2,1,0:T(8,128)(2,1)S(1)} %get-tuple-element.20), channel_id=1, source_target_pairs={{0,0},{1,1},{2,2},{3,3},{4,16},{5,17},{6,18},{7,19},{8,8},{9,9},{1... | collective-permute-start | bytes 393224 | tf_op jit(solution)/shard_map/ppermute | solution.py:355
  46.0 3.1 %collective-permute-start.16 = (bf16[32,16,128]{2,1,0:T(8,128)(2,1)S(1)}, bf16[32,16,128]{2,1,0:T(8,128)(2,1)S(1)}, u32[]{:S(2)}, u32[]{:S(2)}) collective-permute-start(bf16[32,16,128]{2,1,0:T(8,128)(2,1)S(1)} %get-tuple-element.21), channel_id=1, source_target_pairs={{0,8},{1,9},{2,10},{3,11},{4,24},{5,25},{6,26},{7,27},{8,0},{9,1},... | collective-permute-start | bytes 393224 | tf_op jit(solution)/shard_map/ppermute | solution.py:355
  49.1 1.9 %collective-permute-start.17 = (bf16[32,16,128]{2,1,0:T(8,128)(2,1)S(1)}, bf16[32,16,128]{2,1,0:T(8,128)(2,1)S(1)}, u32[]{:S(2)}, u32[]{:S(2)}) collective-permute-start(bf16[32,16,128]{2,1,0:T(8,128)(2,1)S(1)} %get-tuple-element.22), channel_id=1, source_target_pairs={{0,1},{1,0},{2,3},{3,2},{4,17},{5,16},{6,19},{7,18},{8,9},{9,8},{1... | collective-permute-start | bytes 393224 | tf_op jit(solution)/shard_map/ppermute | solution.py:355
  51.1 0.9 %collective-permute-start.18 = (bf16[32,16,128]{2,1,0:T(8,128)(2,1)S(1)}, bf16[32,16,128]{2,1,0:T(8,128)(2,1)S(1)}, u32[]{:S(2)}, u32[]{:S(2)}) collective-permute-start(bf16[32,16,128]{2,1,0:T(8,128)(2,1)S(1)} %get-tuple-element.23), channel_id=1, source_target_pairs={{0,9},{1,8},{2,11},{3,10},{4,25},{5,24},{6,27},{7,26},{8,1},{9,0},... | collective-permute-start | bytes 393224 | tf_op jit(solution)/shard_map/ppermute | solution.py:355
  52.0 0.1 fusion.refs_10_
  52.1 2.9 %collective-permute-done.16.refs_4_ = bf16[32,16,128]{2,1,0:T(8,128)(2,1)S(1)} collective-permute-done((bf16[32,16,128]{2,1,0:T(8,128)(2,1)S(1)}, bf16[32,16,128]{2,1,0:T(8,128)(2,1)S(1)}, u32[]{:S(2)}, u32[]{:S(2)}) %collective-permute-start.16) | collective-permute-done | bytes 131104 | tf_op jit(solution)/shard_map/ppermute | solution.py:355
  55.0 5.7 %collective-permute-done.17.refs_5_ = bf16[32,16,128]{2,1,0:T(8,128)(2,1)S(1)} collective-permute-done((bf16[32,16,128]{2,1,0:T(8,128)(2,1)S(1)}, bf16[32,16,128]{2,1,0:T(8,128)(2,1)S(1)}, u32[]{:S(2)}, u32[]{:S(2)}) %collective-permute-start.17) | collective-permute-done | bytes 131104 | tf_op jit(solution)/shard_map/ppermute | solution.py:355
  60.7 2.8 %collective-permute-done.18.refs_6_ = bf16[32,16,128]{2,1,0:T(8,128)(2,1)S(1)} collective-permute-done((bf16[32,16,128]{2,1,0:T(8,128)(2,1)S(1)}, bf16[32,16,128]{2,1,0:T(8,128)(2,1)S(1)}, u32[]{:S(2)}, u32[]{:S(2)}) %collective-permute-start.18) | collective-permute-done | bytes 131104 | tf_op jit(solution)/shard_map/ppermute | solution.py:355
  63.5 2.6 %finish.2.refs_11_ = bf16[16,128,128]{2,1,0:T(8,128)(2,1)} custom-call(s32[4]{0:T(128)S(1)} %pad_add_fusion.refs_0_, bf16[16,128,128]{2,1,0:T(8,128)(2,1)S(1)} %copy-done, bf16[16,64,128]{2,1,0:T(8,128)(2,1)S(1)} %get-tuple-element.24.refs_2_, bf16[32,16,128]{2,1,0:T(8,128)(2,1)S(1)} %collective-permute-done.15.refs_3_, ...), custom_call_target="tpu_custom_call" | custom-call | tf_op jit(solution)/shard_map/finish/pallas_call | solution.py:376
  66.2 2.7 %finish.3 = bf16[16,128,128]{2,1,0:T(8,128)(2,1)} custom-call(s32[4]{0:T(128)S(1)} %pad_add_fusion.refs_0_, bf16[16,128,128]{2,1,0:T(8,128)(2,1)S(1)} %copy-done, bf16[16,64,128]{2,1,0:T(8,128)(2,1)S(1)} %collective-permute-done.14.refs_2_, bf16[32,16,128]{2,1,0:T(8,128)(2,1)S(1)} %collective-permute-done.15.refs_3_, ...), custom_call_target="tpu_custom_call", output_to_operand_aliasing={{}: (11, {})} | custom-call | tf_op jit(solution)/shard_map/finish/pallas_call | solution.py:376
  (40 shorter events, 0.2 us)
Async XLA Ops:
  1.5 1.8 %copy-start.5 = (bf16[128,32,64]{0,2,1:T(8,128)(2,1)S(1)}, bf16[128,32,64]{0,2,1:T(8,128)(2,1)}, u32[]{:S(2)}) copy-start(bf16[128,32,64]{0,2,1:T(8,128)(2,1)} %param.10) | copy-start | bytes 1572868
  1.7 6.0 %collective-permute-start.4 = (bf16[512,128]{1,0:T(8,128)(2,1)S(1)}, bf16[512,128]{1,0:T(8,128)(2,1)S(1)}, u32[]{:S(2)}, u32[]{:S(2)}) collective-permute-start(bf16[512,128]{1,0:T(8,128)(2,1)S(1)} %bitcast.45), channel_id=1, source_target_pairs={{0,1},{1,0},{2,3},{3,2},{4,5},{5,4},{6,7},{7,6},{8,9},{9,8},{10,11... | collective-permute-start | bytes 393224 | tf_op jit(solution)/shard_map/ppermute | solution.py:239
  3.0 4.6 %collective-permute-start.8 = (bf16[512,128]{1,0:T(8,128)(2,1)S(1)}, bf16[512,128]{1,0:T(8,128)(2,1)S(1)}, u32[]{:S(2)}, u32[]{:S(2)}) collective-permute-start(bf16[512,128]{1,0:T(8,128)(2,1)S(1)} %bitcast.46), channel_id=1, source_target_pairs={{0,16},{8,24},{16,0},{24,8},{1,17},{9,25},{17,1},{25,9},{2,18},{10... | collective-permute-start | bytes 393224 | tf_op jit(solution)/shard_map/ppermute | solution.py:239
  3.7 3.8 %copy-start.6 = (bf16[1024,128]{1,0:T(8,128)(2,1)S(1)}, bf16[1024,128]{1,0:T(8,128)(2,1)}, u32[]{:S(2)}) copy-start(bf16[1024,128]{1,0:T(8,128)(2,1)} %param.12) | copy-start | bytes 786436
  3.7 5.4 %collective-permute-start = (bf16[512,128]{1,0:T(8,128)(2,1)S(1)}, bf16[512,128]{1,0:T(8,128)(2,1)S(1)}, u32[]{:S(2)}, u32[]{:S(2)}) collective-permute-start(bf16[512,128]{1,0:T(8,128)(2,1)S(1)} %get-tuple-element.25), channel_id=1, source_target_pairs={{0,1},{1,0},{2,3},{3,2},{4,5},{5,4},{6,7},{7,6},{8,9},{9,8},{10,11... | collective-permute-start | bytes 393224 | tf_op jit(solution)/shard_map/ppermute | solution.py:239
  4.4 9.5 %collective-permute-start.5 = (bf16[512,128]{1,0:T(8,128)(2,1)S(1)}, bf16[512,128]{1,0:T(8,128)(2,1)S(1)}, u32[]{:S(2)}, u32[]{:S(2)}) collective-permute-start(bf16[512,128]{1,0:T(8,128)(2,1)S(1)} %bitcast.56), channel_id=1, source_target_pairs={{0,3},{1,2},{2,1},{3,0},{4,7},{5,6},{6,5},{7,4},{8,11},{9,10},{10,... | collective-permute-start | bytes 393224 | tf_op jit(solution)/shard_map/ppermute | solution.py:239
  7.6 7.6 %collective-permute-start.9 = (bf16[512,128]{1,0:T(8,128)(2,1)S(1)}, bf16[512,128]{1,0:T(8,128)(2,1)S(1)}, u32[]{:S(2)}, u32[]{:S(2)}) collective-permute-start(bf16[512,128]{1,0:T(8,128)(2,1)S(1)} %collective-permute-done.4.refs_1_.refs_3_.refs_4_), channel_id=1, source_target_pairs={{0,16},{8,24},{16,0},{24,8},{1,17},{9,25},{17,1},{25,9},{2,18},{10... | collective-permute-start | bytes 393224 | tf_op jit(solution)/shard_map/ppermute | solution.py:239
  9.1 13.1 %collective-permute-start.1 = (bf16[1024,128]{1,0:T(8,128)(2,1)S(1)}, bf16[1024,128]{1,0:T(8,128)(2,1)S(1)}, u32[]{:S(2)}, u32[]{:S(2)}) collective-permute-start(bf16[1024,128]{1,0:T(8,128)(2,1)S(1)} %pack.3.near_ref), channel_id=1, source_target_pairs={{0,4},{4,0},{1,5},{5,1},{2,6},{6,2},{3,7},{7,3},{8,12},{12,8},{9,1... | collective-permute-start | bytes 786440 | tf_op jit(solution)/shard_map/ppermute | solution.py:239
  13.9 5.5 %collective-permute-start.6 = (bf16[512,128]{1,0:T(8,128)(2,1)S(1)}, bf16[512,128]{1,0:T(8,128)(2,1)S(1)}, u32[]{:S(2)}, u32[]{:S(2)}) collective-permute-start(bf16[512,128]{1,0:T(8,128)(2,1)S(1)} %collective-permute-done.5.refs_2_.refs_4_.refs_5_), channel_id=1, source_target_pairs={{0,1},{1,0},{2,3},{3,2},{4,5},{5,4},{6,7},{7,6},{8,9},{9,8},{10,11... | collective-permute-start | bytes 393224 | tf_op jit(solution)/shard_map/ppermute | solution.py:239
  14.0 13.4 %collective-permute-start.2 = (bf16[1024,128]{1,0:T(8,128)(2,1)S(1)}, bf16[1024,128]{1,0:T(8,128)(2,1)S(1)}, u32[]{:S(2)}, u32[]{:S(2)}) collective-permute-start(bf16[1024,128]{1,0:T(8,128)(2,1)S(1)} %pack.3.near_ref), channel_id=1, source_target_pairs={{0,2},{1,3},{2,0},{3,1},{4,6},{5,7},{6,4},{7,5},{8,10},{9,11},{10,... | collective-permute-start | bytes 786440 | tf_op jit(solution)/shard_map/ppermute | solution.py:239
  15.2 6.9 %collective-permute-start.10 = (bf16[512,128]{1,0:T(8,128)(2,1)S(1)}, bf16[512,128]{1,0:T(8,128)(2,1)S(1)}, u32[]{:S(2)}, u32[]{:S(2)}) collective-permute-start(bf16[512,128]{1,0:T(8,128)(2,1)S(1)} %collective-permute-done.5.refs_2_.refs_4_.refs_5_), channel_id=1, source_target_pairs={{0,16},{8,24},{16,0},{24,8},{1,17},{9,25},{17,1},{25,9},{2,18},{10... | collective-permute-start | bytes 393224 | tf_op jit(solution)/shard_map/ppermute | solution.py:239
  19.5 14.0 %collective-permute-start.7 = (bf16[2048,128]{1,0:T(8,128)(2,1)S(1)}, bf16[2048,128]{1,0:T(8,128)(2,1)S(1)}, u32[]{:S(2)}, u32[]{:S(2)}) collective-permute-start(bf16[2048,128]{1,0:T(8,128)(2,1)S(1)} %pack.4), channel_id=1, source_target_pairs={{0,8},{8,0},{16,24},{24,16},{1,9},{9,1},{17,25},{25,17},{2,10},{10... | collective-permute-start | bytes 1572872 | tf_op jit(solution)/shard_map/ppermute | solution.py:239
  22.2 6.1 %collective-permute-start.11 = (bf16[512,128]{1,0:T(8,128)(2,1)S(1)}, bf16[512,128]{1,0:T(8,128)(2,1)}, u32[]{:S(2)}, u32[]{:S(2)}) collective-permute-start(bf16[512,128]{1,0:T(8,128)(2,1)S(1)} %collective-permute-done.6.refs_3_.refs_5_.refs_6_), channel_id=1, source_target_pairs={{0,16},{8,24},{16,0},{24,8},{1,17},{9,25},{17,1},{25,9},{2,18},{10... | collective-permute-start | bytes 393224 | tf_op jit(solution)/shard_map/ppermute | solution.py:239
  22.3 11.2 %collective-permute-start.12 = (bf16[1536,128]{1,0:T(8,128)(2,1)S(1)}, bf16[1536,128]{1,0:T(8,128)(2,1)S(1)}, u32[]{:S(2)}, u32[]{:S(2)}) collective-permute-start(bf16[1536,128]{1,0:T(8,128)(2,1)S(1)} %pack.5), channel_id=1, source_target_pairs={{0,8},{8,0},{16,24},{24,16},{1,9},{9,1},{17,25},{25,17},{2,10},{10... | collective-permute-start | bytes 1179656 | tf_op jit(solution)/shard_map/ppermute | solution.py:239
  24.7 5.5 %copy-start.7 = (f32[512]{0:T(512)S(1)}, f32[512]{0:T(512)}, u32[]{:S(2)}) copy-start(f32[512]{0:T(512)} %param.17) | copy-start | bytes 6148
  24.7 5.5 %copy-start.9 = (f32[128]{0:T(128)S(1)}, f32[128]{0:T(128)}, u32[]{:S(2)}) copy-start(f32[128]{0:T(128)} %param.19) | copy-start | bytes 1540
  24.8 5.5 %copy-start.10 = (f32[128]{0:T(128)S(1)}, f32[128]{0:T(128)}, u32[]{:S(2)}) copy-start(f32[128]{0:T(128)} %param.15) | copy-start | bytes 1540
  27.5 0.8 %copy-start.3 = (bf16[512,512]{1,0:T(8,128)(2,1)}, bf16[512,512]{1,0:T(8,128)(2,1)S(1)}, u32[]{:S(2)}) copy-start(bf16[512,512]{1,0:T(8,128)(2,1)S(1)} %arrange.1.refs_1_) | copy-start | bytes 1572868
  28.3 5.2 %collective-permute-start.13 = (bf16[512,128]{1,0:T(8,128)(2,1)}, bf16[512,128]{1,0:T(8,128)(2,1)}, u32[]{:S(2)}, u32[]{:S(2)}) collective-permute-start(bf16[512,128]{1,0:T(8,128)(2,1)} %collective-permute-done.11.refs_10_.refs_11_), channel_id=1, source_target_pairs={{0,8},{8,0},{16,24},{24,16},{1,9},{9,1},{17,25},{25,17},{2,10},{10... | collective-permute-start | bytes 393224 | tf_op jit(solution)/shard_map/ppermute | solution.py:239
  32.1 8.0 %collective-permute-start.3 = (bf16[1024,128]{1,0:T(8,128)(2,1)S(1)}, bf16[1024,128]{1,0:T(8,128)(2,1)S(1)}, u32[]{:S(2)}, u32[]{:S(2)}) collective-permute-start(bf16[1024,128]{1,0:T(8,128)(2,1)S(1)} %collective-permute-done.2.far_ref), channel_id=1, source_target_pairs={{0,4},{4,0},{1,5},{5,1},{2,6},{6,2},{3,7},{7,3},{8,12},{12,8},{9,1... | collective-permute-start | bytes 786440 | tf_op jit(solution)/shard_map/ppermute | solution.py:239
  33.4 0.7 copy-start.8
  34.1 1.1 %copy-start.4 = (bf16[512,512]{1,0:T(8,128)(2,1)S(1)}, bf16[512,512]{1,0:T(8,128)(2,1)}, u32[]{:S(2)}) copy-start(bf16[512,512]{1,0:T(8,128)(2,1)} %copy-done.3) | copy-start | bytes 1572868
  38.6 24.9 %copy-start = (bf16[16,128,128]{2,1,0:T(8,128)(2,1)S(1)}, bf16[16,128,128]{2,1,0:T(8,128)(2,1)}, u32[]{:S(2)}) copy-start(bf16[16,128,128]{2,1,0:T(8,128)(2,1)} %refs_1_.3) | copy-start | bytes 1572868
  40.1 23.4 %copy-start.2 = (bf16[512,128]{1,0:T(8,128)(2,1)S(1)}, bf16[512,128]{1,0:T(8,128)(2,1)}, u32[]{:S(2)}) copy-start(bf16[512,128]{1,0:T(8,128)(2,1)} %refs_8_.3) | copy-start | bytes 393220
  43.7 19.8 %copy-start.1 = (bf16[128,512]{1,0:T(8,128)(2,1)S(1)}, bf16[128,512]{1,0:T(8,128)(2,1)}, u32[]{:S(2)}) copy-start(bf16[128,512]{1,0:T(8,128)(2,1)} %refs_7_.3) | copy-start | bytes 393220
  43.7 22.5 %collective-permute-start.14 = (bf16[16,64,128]{2,1,0:T(8,128)(2,1)S(1)}, bf16[16,64,128]{2,1,0:T(8,128)(2,1)S(1)}, u32[]{:S(2)}, u32[]{:S(2)}) collective-permute-start(bf16[16,64,128]{2,1,0:T(8,128)(2,1)S(1)} %get-tuple-element.19), channel_id=1, source_target_pairs={{0,2},{1,3},{2,0},{3,1},{4,6},{5,7},{6,4},{7,5},{8,10},{9,11},{10,... | collective-permute-start | bytes 786440 | tf_op jit(solution)/shard_map/ppermute | solution.py:239
  43.8 8.3 %collective-permute-start.15 = (bf16[32,16,128]{2,1,0:T(8,128)(2,1)S(1)}, bf16[32,16,128]{2,1,0:T(8,128)(2,1)S(1)}, u32[]{:S(2)}, u32[]{:S(2)}) collective-permute-start(bf16[32,16,128]{2,1,0:T(8,128)(2,1)S(1)} %get-tuple-element.20), channel_id=1, source_target_pairs={{0,0},{1,1},{2,2},{3,3},{4,16},{5,17},{6,18},{7,19},{8,8},{9,9},{1... | collective-permute-start | bytes 393224 | tf_op jit(solution)/shard_map/ppermute | solution.py:355
  46.0 9.0 %collective-permute-start.16 = (bf16[32,16,128]{2,1,0:T(8,128)(2,1)S(1)}, bf16[32,16,128]{2,1,0:T(8,128)(2,1)S(1)}, u32[]{:S(2)}, u32[]{:S(2)}) collective-permute-start(bf16[32,16,128]{2,1,0:T(8,128)(2,1)S(1)} %get-tuple-element.21), channel_id=1, source_target_pairs={{0,8},{1,9},{2,10},{3,11},{4,24},{5,25},{6,26},{7,27},{8,0},{9,1},... | collective-permute-start | bytes 393224 | tf_op jit(solution)/shard_map/ppermute | solution.py:355
  49.1 11.6 %collective-permute-start.17 = (bf16[32,16,128]{2,1,0:T(8,128)(2,1)S(1)}, bf16[32,16,128]{2,1,0:T(8,128)(2,1)S(1)}, u32[]{:S(2)}, u32[]{:S(2)}) collective-permute-start(bf16[32,16,128]{2,1,0:T(8,128)(2,1)S(1)} %get-tuple-element.22), channel_id=1, source_target_pairs={{0,1},{1,0},{2,3},{3,2},{4,17},{5,16},{6,19},{7,18},{8,9},{9,8},{1... | collective-permute-start | bytes 393224 | tf_op jit(solution)/shard_map/ppermute | solution.py:355
  51.1 12.4 %collective-permute-start.18 = (bf16[32,16,128]{2,1,0:T(8,128)(2,1)S(1)}, bf16[32,16,128]{2,1,0:T(8,128)(2,1)S(1)}, u32[]{:S(2)}, u32[]{:S(2)}) collective-permute-start(bf16[32,16,128]{2,1,0:T(8,128)(2,1)S(1)} %get-tuple-element.23), channel_id=1, source_target_pairs={{0,9},{1,8},{2,11},{3,10},{4,25},{5,24},{6,27},{7,26},{8,1},{9,0},... | collective-permute-start | bytes 393224 | tf_op jit(solution)/shard_map/ppermute | solution.py:355
where the time goes:
time: 69.5 us; the launch traced here: 68.8 us
  starting transfers between devices  25.2 us (36%)
  waiting for transfers between devices  23.4 us (34%)
  Pallas kernels  12.4 us (18%)
  local copies, waits for them, and re-layouts  6.79 us (10%)
    ppermute x15, starting transfers between devices, swap(): return lax.ppermute(value, name, [(i, i ^ flip) for i in range(size)])  17 us
    ppermute x15, waiting for transfers between devices, swap(): return lax.ppermute(value, name, [(i, i ^ flip) for i in range(size)])  12 us
    ppermute x4, waiting for transfers between devices, on_device(): mirrors.append(lax.ppermute(outs[2 + 2 * dz + flip], axes, pairs))  11.4 us
    ppermute x4, starting transfers between devices, on_device(): mirrors.append(lax.ppermute(outs[2 + 2 * dz + flip], axes, pairs))  8.16 us
    pallas_call x2, Pallas kernels, update_call(): pl.pallas_call(functools.partial(update_kernel, places, cols, low, last,...  6.97 us
    pallas_call x2, Pallas kernels, on_device(): pl.pallas_call(functools.partial(finish_kernel, low, other), out_shape=ja...  5.31 us
    unnamed x24, local copies, waits for them, and re-layouts  4.32 us
  transfers between devices with their start and end apart: 19, of which 8 were waited for; matrix products, arithmetic and copies ran while one was open for 5% of the time, Pallas kernels for 9%

commit v1 on v0

--- a/solution.py
+++ b/solution.py
@@ -17,7 +17,7 @@
     sources = len(right_places[0])
     refs = list(refs)
     place_ref = refs.pop(0)
-    left_refs = [refs.pop(0) for _ in range(2 * blocks if last else 1)]
+    left_refs = [refs.pop(0) for _ in range(3 * blocks if last else 1)]
     data_refs = [refs.pop(0) for _ in range(data_count)]
     bias_ref, weight_ref = refs.pop(0), refs.pop(0)
     first_ref = refs.pop(0) if last else None
@@ -35,12 +35,12 @@
     lane_low = lax.broadcasted_iota(jnp.int32, (pair_channels, lanes), 1) < half
     for block in range(blocks if last else 0):
         for dz in range(groups):
+            index = 3 * block + max(0, dz - low + 1)
+            begin = dz * share_rows if dz < low else 0
             lhs_ref[
                 block * share_rows : (block + 1) * share_rows,
                 dz * group_len : (dz + 1) * group_len,
-            ] = left_refs[2 * block + dz // low][
-                dz % low * share_rows : (dz % low + 1) * share_rows
-            ]
+            ] = left_refs[index][begin : begin + share_rows]
 
     def right_tile(item):
         source, rest = divmod(item, per)
@@ -113,26 +113,27 @@
     )(*values)
 
 
-def arrange_kernel(near_ref, far_ref, out_ref):
-    rows, lanes = out_ref.shape[0], near_ref.shape[1]
-    count = near_ref.shape[0] // rows
-    for index in range(2 * count):
-        ref = near_ref if index < count else far_ref
-        begin = index % count * rows
-        out_ref[:, index * lanes : (index + 1) * lanes] = ref[begin : begin + rows]
+def arrange_kernel(*refs):
+    out_ref = refs[-1]
+    rows, lanes = out_ref.shape[0], refs[0].shape[1]
+    index = 0
+    for ref in refs[:-1]:
+        for begin in range(0, ref.shape[0], rows):
+            out_ref[:, index * lanes : (index + 1) * lanes] = ref[begin : begin + rows]
+            index += 1
 
 
 def arrange(lefts, groups):
-    rows, lanes = lefts[0].shape
-    rows //= groups // 2
+    lanes = lefts[0].shape[1]
+    rows = sum(value.shape[0] for value in lefts) // groups
     return pl.pallas_call(
         arrange_kernel,
         out_shape=jax.ShapeDtypeStruct((rows, groups * lanes), lefts[0].dtype),
-        in_specs=[pl.BlockSpec(memory_space=pltpu.VMEM)] * 2,
+        in_specs=[pl.BlockSpec(memory_space=pltpu.VMEM)] * len(lefts),
         out_specs=pl.BlockSpec(memory_space=pltpu.VMEM),
         compiler_params=pltpu.CompilerParams(vmem_limit_bytes=4 * 1024 * 1024),
         cost_estimate=pl.CostEstimate(
-            flops=rows * groups * lanes * 8 * lanes * groups * 1,
+            flops=rows * groups * lanes * 8 * lanes * groups * 4,
             bytes_accessed=4 * rows * groups * lanes,
             transcendentals=0,
         ),
@@ -256,10 +257,26 @@
     blocks[low + 1] = swap(theirs, "seq", groups, low + 1)
     blocks[1] = swap(mine, "seq", groups, 1)
     blocks[low] = swap(blocks[low + 1], "seq", groups, 1)
+    weight = proj_weight.reshape(channels, rows, e1, 2, pair_channels)
+    weight = weight.transpose(1, 3, 4, 2, 0)
+    weight = jnp.stack([pick(weight, row ^ m) for m in range(rows)], axis=2)
+    weight = weight.reshape(2 * pair_channels, channels * channels // 2)
+    bias = jnp.broadcast_to(proj_bias[:, None], (pair_channels, 2 * half))
+    vectors = jnp.concatenate([norm_gain, down_bias, up_bias]).reshape(1, -1)
+    cell = jnp.arange(run * run)
+    mirror_cell = cell % run * run + cell // run
+    swap_cells = (mirror_cell[:, None] == cell[None, :]).astype(bf16)
+    weight, bias, vectors, swap_cells = constants = lax.optimization_barrier(
+        (weight, bias, vectors, swap_cells)
+    )
     lefts = [pack(own, near)]
-    lefts.append(swap(lefts[0], "seq", groups, low))
+    fars = [swap(own, "seq", groups, low), swap(near, "seq", groups, low)]
     shares = [[swap(lefts[0], "col", cols, dy)] for dy in range(1, cols)]
-    first_lhs = arrange(lefts, groups)
+    near_shares = [pair[0] for pair in shares]
+    for dy in range(1, cols):
+        shares[dy - 1] += [swap(value, "col", cols, dy) for value in fars]
+    far_shares = [pair[1] for pair in shares]
+    first_lhs = arrange([lefts[0]] + fars, groups)
     data = []
     right_places = {dz: [] for dz in range(groups)}
     order = (0, 1, low + 1, low)
@@ -267,7 +284,7 @@
     last = ()
     for dz in order:
         for dx in range(1, xs):
-            behind = last + (tuple(map(tuple, shares)) if dz == low else ())
+            behind = last + ((near_shares, constants) if dz == low else ())
             crosses[dz].append(swap(after(blocks[dz], *behind), "row", rows, 2 * dx))
             last = (crosses[dz][-1],)
     for position in range(xs):
@@ -282,27 +299,19 @@
         data.append(exchanged)
         if count < len(order):
             right_places[low].append((len(data), 0))
-            data.append(swap(after(values[-1], first_lhs), "row", rows, 1))
-    for dy in range(1, cols):
-        shares[dy - 1].append(swap(lefts[1], "col", cols, dy))
+            data.append(swap(after(values[-1], first_lhs, far_shares), "row", rows, 1))
     right_places = [right_places[dz] for dz in range(groups)]
     last_lefts = [value for pair in shares for value in pair]
-
-    weight = proj_weight.reshape(channels, rows, e1, 2, pair_channels)
-    weight = weight.transpose(1, 3, 4, 2, 0)
-    weight = jnp.stack([pick(weight, row ^ m) for m in range(rows)], axis=2)
-    weight = weight.reshape(2 * pair_channels, channels * channels // 2)
 
     place = jnp.stack([core, z_low, col, z_high]).astype(jnp.int32)
     vmem = pl.BlockSpec(memory_space=pltpu.VMEM)
     smem = pl.BlockSpec(memory_space=pltpu.SMEM)
-    params = pltpu.CompilerParams(vmem_limit_bytes=40 * 1024 * 1024)
+    params = pltpu.CompilerParams(vmem_limit_bytes=16 * 1024 * 1024)
     scale = 1.0 / (group_len * groups)
-    bias = jnp.broadcast_to(proj_bias[:, None], (pair_channels, 2 * half))
     share = share_rows // channels
 
     def update_call(last, left_values, extra, out_shape, out_specs, scratch):
-        blocks = max(len(left_values) // 2, 1)
+        blocks = max(len(left_values) // 3, 1)
         row_count = share * blocks
         outer_size = row_count * channels * channels * half
         places = (blocks, len(data), right_places, share_rows, source_rows, group_len, run)
@@ -355,10 +364,6 @@
             mirrors.append(lax.ppermute(outs[2 + 2 * dz + flip], axes, pairs))
     update_other = swap(outs[1], "seq", groups, low)
 
-    vectors = jnp.concatenate([norm_gain, down_bias, up_bias]).reshape(1, -1)
-    cell = jnp.arange(run * run)
-    mirror_cell = cell % run * run + cell // run
-    swap_cells = (mirror_cell[:, None] == cell[None, :]).astype(bf16)
     anywhere = pl.BlockSpec(memory_space=pl.ANY)
     result = None
     for other in range(2):

time: 69.5 us -> 69.5 us (level)
  waiting for transfers between devices: 23.4 us -> 21.7 us
  starting transfers between devices: 25.2 us -> 26.7 us
    ppermute x15 -> x17, waiting for transfers between devices: 12 us -> 9.29 us  [swap(): return lax.ppermute(value, name, [(i, i ^ flip) for i in range(size)])]
    ppermute x15 -> x17, starting transfers between devices: 17 us -> 18.6 us  [swap(): return lax.ppermute(value, name, [(i, i ^ flip) for i in range(size)])]
    optimization_barrier x0 -> x1, local copies, waits for them, and re-layouts: none -> 1.09 us  [on_device(): lax.optimization_barrier((weight, bias, vectors, swap_cells))]
    reshape x1 -> x0, local copies, waits for them, and re-layouts: 1.09 us -> none  [on_device(): weight = weight.reshape(2 * pair_channels, channels * channels // 2)]
    ppermute x4, waiting for transfers between devices: 11.4 us -> 12.4 us  [on_device(): mirrors.append(lax.ppermute(outs[2 + 2 * dz + flip], axes, pairs))]
    unnamed x24 -> x30, local copies, waits for them, and re-layouts: 4.32 us -> 5 us
  transfers between devices with their start and end apart: 19 -> 21, of which waited for: 8 -> 7; matrix products, arithmetic and copies ran while one was open for 5% -> 5% of each run, Pallas kernels for 9% -> 9%
where the time goes in v1:
time: 69.5 us; the launch traced here: 69.3 us
  starting transfers between devices  26.7 us (38%)
  waiting for transfers between devices  21.7 us (31%)
  Pallas kernels  12.4 us (18%)
  local copies, waits for them, and re-layouts  7.48 us (11%)
    ppermute x17, starting transfers between devices, swap(): return lax.ppermute(value, name, [(i, i ^ flip) for i in range(size)])  18.6 us
    ppermute x4, waiting for transfers between devices, on_device(): mirrors.append(lax.ppermute(outs[2 + 2 * dz + flip], axes, pairs))  12.4 us
    ppermute x17, waiting for transfers between devices, swap(): return lax.ppermute(value, name, [(i, i ^ flip) for i in range(size)])  9.29 us
    ppermute x4, starting transfers between devices, on_device(): mirrors.append(lax.ppermute(outs[2 + 2 * dz + flip], axes, pairs))  8.15 us
    pallas_call x2, Pallas kernels, update_call(): pl.pallas_call(functools.partial(update_kernel, places, cols, low, last,...  6.96 us
    pallas_call x2, Pallas kernels, on_device(): pl.pallas_call(functools.partial(finish_kernel, low, other), out_shape=ja...  5.31 us
    unnamed x30, local copies, waits for them, and re-layouts  5 us
  transfers between devices with their start and end apart: 21, of which 7 were waited for; matrix products, arithmetic and copies ran while one was open for 5% of the time, Pallas kernels for 9%

profile of v1, /device:TPU:3, one launch (start us, length us, event | category | flops | bytes accessed | tf_op | source)
XLA Modules:
  0.0 69.3 jit_solution(18233921576144483063)
XLA Ops:
  0.0 1.1 %copy.19 = bf16[128,8,128]{0,2,1:T(8,128)(2,1)S(1)} copy(bf16[128,8,128]{2,1,0:T(8,128)(2,1)} %param.11) | data formatting | bytes 524288 | tf_op args[1]
  1.2 0.2 copy.20
  1.4 0.1 reshape.55
  1.5 0.1 copy.21
  1.7 1.5 %collective-permute-start.6 = (bf16[512,128]{1,0:T(8,128)(2,1)S(1)}, bf16[512,128]{1,0:T(8,128)(2,1)S(1)}, u32[]{:S(2)}, u32[]{:S(2)}) collective-permute-start(bf16[512,128]{1,0:T(8,128)(2,1)S(1)} %bitcast.46), channel_id=1, source_target_pairs={{0,1},{1,0},{2,3},{3,2},{4,5},{5,4},{6,7},{7,6},{8,9},{9,8},{10,11... | collective-permute-start | bytes 393224 | tf_op jit(solution)/shard_map/ppermute | solution.py:240
  3.3 0.1 copy.22
  3.4 2.3 %collective-permute-start.7 = (bf16[512,128]{1,0:T(8,128)(2,1)S(1)}, bf16[512,128]{1,0:T(8,128)(2,1)S(1)}, u32[]{:S(2)}, u32[]{:S(2)}) collective-permute-start(bf16[512,128]{1,0:T(8,128)(2,1)S(1)} %bitcast.56), channel_id=1, source_target_pairs={{0,3},{1,2},{2,1},{3,0},{4,7},{5,6},{6,5},{7,4},{8,11},{9,10},{10,... | collective-permute-start | bytes 393224 | tf_op jit(solution)/shard_map/ppermute | solution.py:240
  5.7 0.3 copy.18
  6.0 0.5 collective-permute-start
  6.5 1.0 %collective-permute-start.2 = (bf16[512,128]{1,0:T(8,128)(2,1)S(1)}, bf16[512,128]{1,0:T(8,128)(2,1)S(1)}, u32[]{:S(2)}, u32[]{:S(2)}) collective-permute-start(bf16[512,128]{1,0:T(8,128)(2,1)S(1)} %get-tuple-element.34.refs_0_), channel_id=1, source_target_pairs={{0,2},{1,3},{2,0},{3,1},{4,6},{5,7},{6,4},{7,5},{8,10},{9,11},{10,... | collective-permute-start | bytes 393224 | tf_op jit(solution)/shard_map/ppermute | solution.py:240
  7.5 0.2 constant_dynamic-slice_fusion.3
  7.7 0.1 copy_bitcast_fusion.3
  7.8 0.1 copy_bitcast_fusion.1
  7.9 0.5 pad_maximum_fusion
  8.4 1.3 %collective-permute-start.11 = (bf16[512,128]{1,0:T(8,128)(2,1)S(1)}, bf16[512,128]{1,0:T(8,128)(2,1)S(1)}, u32[]{:S(2)}, u32[]{:S(2)}) collective-permute-start(bf16[512,128]{1,0:T(8,128)(2,1)S(1)} %collective-permute-done.6.refs_1_.refs_3_.refs_5_), channel_id=1, source_target_pairs={{0,16},{8,24},{16,0},{24,8},{1,17},{9,25},{17,1},{25,9},{2,18},{10... | collective-permute-start | bytes 393224 | tf_op jit(solution)/shard_map/ppermute | solution.py:240
  9.7 5.0 %collective-permute-done.refs_1_ = bf16[512,128]{1,0:T(8,128)(2,1)S(1)} collective-permute-done((bf16[512,128]{1,0:T(8,128)(2,1)S(1)}, bf16[512,128]{1,0:T(8,128)(2,1)S(1)}, u32[]{:S(2)}, u32[]{:S(2)}) %collective-permute-start) | collective-permute-done | bytes 131104 | tf_op jit(solution)/shard_map/ppermute | solution.py:240
  14.7 1.3 %collective-permute-start.1 = (bf16[1024,128]{1,0:T(8,128)(2,1)S(1)}, bf16[1024,128]{1,0:T(8,128)(2,1)S(1)}, u32[]{:S(2)}, u32[]{:S(2)}) collective-permute-start(bf16[1024,128]{1,0:T(8,128)(2,1)S(1)} %pack.3.refs_0_), channel_id=1, source_target_pairs={{0,4},{4,0},{1,5},{5,1},{2,6},{6,2},{3,7},{7,3},{8,12},{12,8},{9,1... | collective-permute-start | bytes 786440 | tf_op jit(solution)/shard_map/ppermute | solution.py:240
  16.0 0.7 %copy.39 = bf16[64,8,2,128]{3,1,2,0:T(8,128)(2,1)} copy(bf16[64,8,2,128]{3,2,1,0:T(2,128)(2,1)S(1)} %bitcast.52) | data formatting | bytes 524288
  16.8 2.0 %collective-permute-start.8 = (bf16[512,128]{1,0:T(8,128)(2,1)S(1)}, bf16[512,128]{1,0:T(8,128)(2,1)S(1)}, u32[]{:S(2)}, u32[]{:S(2)}) collective-permute-start(bf16[512,128]{1,0:T(8,128)(2,1)S(1)} %collective-permute-done.7.refs_2_.refs_4_.refs_6_), channel_id=1, source_target_pairs={{0,1},{1,0},{2,3},{3,2},{4,5},{5,4},{6,7},{7,6},{8,9},{9,8},{10,11... | collective-permute-start | bytes 393224 | tf_op jit(solution)/shard_map/ppermute | solution.py:240
  18.8 1.2 %collective-permute-start.12 = (bf16[512,128]{1,0:T(8,128)(2,1)S(1)}, bf16[512,128]{1,0:T(8,128)(2,1)S(1)}, u32[]{:S(2)}, u32[]{:S(2)}) collective-permute-start(bf16[512,128]{1,0:T(8,128)(2,1)S(1)} %collective-permute-done.7.refs_2_.refs_4_.refs_6_), channel_id=1, source_target_pairs={{0,16},{8,24},{16,0},{24,8},{1,17},{9,25},{17,1},{25,9},{2,18},{10... | collective-permute-start | bytes 393224 | tf_op jit(solution)/shard_map/ppermute | solution.py:240
  20.0 0.1 fusion.refs_10_
  20.2 0.3 collective-permute-start.3
  20.5 2.2 %collective-permute-done.8.refs_3_.refs_5_.refs_7_ = bf16[512,128]{1,0:T(8,128)(2,1)S(1)} collective-permute-done((bf16[512,128]{1,0:T(8,128)(2,1)S(1)}, bf16[512,128]{1,0:T(8,128)(2,1)S(1)}, u32[]{:S(2)}, u32[]{:S(2)}) %collective-permute-start.8) | collective-permute-done | bytes 131104 | tf_op jit(solution)/shard_map/ppermute | solution.py:240
  22.8 3.6 %collective-permute-start.9 = (bf16[2048,128]{1,0:T(8,128)(2,1)S(1)}, bf16[2048,128]{1,0:T(8,128)(2,1)S(1)}, u32[]{:S(2)}, u32[]{:S(2)}) collective-permute-start(bf16[2048,128]{1,0:T(8,128)(2,1)S(1)} %pack.4), channel_id=1, source_target_pairs={{0,8},{8,0},{16,24},{24,16},{1,9},{9,1},{17,25},{25,17},{2,10},{10... | collective-permute-start | bytes 1572872 | tf_op jit(solution)/shard_map/ppermute | solution.py:240
  26.4 0.1 collective-permute-start.14
  26.5 1.3 %collective-permute-start.13 = (bf16[512,128]{1,0:T(8,128)(2,1)S(1)}, bf16[512,128]{1,0:T(8,128)(2,1)}, u32[]{:S(2)}, u32[]{:S(2)}) collective-permute-start(bf16[512,128]{1,0:T(8,128)(2,1)S(1)} %collective-permute-done.8.refs_3_.refs_5_.refs_7_), channel_id=1, source_target_pairs={{0,16},{8,24},{16,0},{24,8},{1,17},{9,25},{17,1},{25,9},{2,18},{10... | collective-permute-start | bytes 393224 | tf_op jit(solution)/shard_map/ppermute | solution.py:240
  27.7 0.1 arrange.1.refs_1_
  27.8 0.6 copy-done.3
  28.4 0.8 %copy-done.6 = bf16[512,512]{1,0:T(8,128)(2,1)} copy-done((bf16[512,512]{1,0:T(8,128)(2,1)}, bf16[512,512]{1,0:T(8,128)(2,1)S(1)}, u32[]{:S(2)}) %copy-start.6) | copy-done | bytes 524312
  29.2 0.7 copy-done.4
  29.9 1.4 %collective-permute-done.13.refs_10_.refs_12_ = bf16[512,128]{1,0:T(8,128)(2,1)} collective-permute-done((bf16[512,128]{1,0:T(8,128)(2,1)S(1)}, bf16[512,128]{1,0:T(8,128)(2,1)}, u32[]{:S(2)}, u32[]{:S(2)}) %collective-permute-start.13) | collective-permute-done | bytes 131104 | tf_op jit(solution)/shard_map/ppermute | solution.py:240
  31.3 1.3 %collective-permute-start.15 = (bf16[512,128]{1,0:T(8,128)(2,1)}, bf16[512,128]{1,0:T(8,128)(2,1)}, u32[]{:S(2)}, u32[]{:S(2)}) collective-permute-start(bf16[512,128]{1,0:T(8,128)(2,1)} %collective-permute-done.13.refs_10_.refs_12_), channel_id=1, source_target_pairs={{0,8},{8,0},{16,24},{24,16},{1,9},{9,1},{17,25},{25,17},{2,10},{10... | collective-permute-start | bytes 393224 | tf_op jit(solution)/shard_map/ppermute | solution.py:240
  32.5 1.1 %copy.28.refs_14_.refs_16_ = bf16[256,512]{1,0:T(8,128)(2,1)S(1)} copy(bf16[256,512]{0,1:T(8,128)(2,1)} %bitcast.51) | data formatting | bytes 524288 | tf_op jit(solution)/shard_map/optimization_barrier | solution.py:269
  33.7 0.2 collective-permute-start.5
  34.0 1.0 %copy-done.7 = bf16[512,512]{1,0:T(8,128)(2,1)S(1)} copy-done((bf16[512,512]{1,0:T(8,128)(2,1)S(1)}, bf16[512,512]{1,0:T(8,128)(2,1)}, u32[]{:S(2)}) %copy-start.7) | copy-done | bytes 524312
  35.0 3.4 %update_first.1.refs_17_ = bf16[16,64,128]{2,1,0:T(8,128)(2,1)S(1)} custom-call(s32[4]{0:T(128)S(1)} %pad_add_fusion.refs_0_, bf16[512,512]{1,0:T(8,128)(2,1)S(1)} %copy-done.7, bf16[512,128]{1,0:T(8,128)(2,1)S(1)} %bitcast.48, bf16[512,128]{1,0:T(8,128)(2,1)S(1)} %collective-permute-done.6.refs_1_.refs_3_.refs_5_, ...), custom_call_target="tpu_custom_call" | custom-call | flops 1610612736 | bytes 2097152 | tf_op jit(solution)/shard_map/update_first/pallas_call | solution.py:318
  38.5 0.6 collective-permute-done.5.refs_3_
  39.1 3.6 %update_last.1 = (bf16[16,64,128]{2,1,0:T(8,128)(2,1)S(1)}, bf16[16,64,128]{2,1,0:T(8,128)(2,1)S(1)}, bf16[32,16,128]{2,1,0:T(8,128)(2,1)S(1)}, bf16[32,16,128]{...) custom-call(s32[4]{0:T(128)S(1)} %pad_add_fusion.refs_0_, ...), custom_call_target="tpu_custom_call" | custom-call | flops 1610612736 | bytes 2097152 | tf_op jit(solution)/shard_map/update_last/pallas_call | solution.py:318
  42.6 0.8 %collective-permute-start.16 = (bf16[16,64,128]{2,1,0:T(8,128)(2,1)S(1)}, bf16[16,64,128]{2,1,0:T(8,128)(2,1)S(1)}, u32[]{:S(2)}, u32[]{:S(2)}) collective-permute-start(bf16[16,64,128]{2,1,0:T(8,128)(2,1)S(1)} %get-tuple-element.27), channel_id=1, source_target_pairs={{0,2},{1,3},{2,0},{3,1},{4,6},{5,7},{6,4},{7,5},{8,10},{9,11},{10,... | collective-permute-start | bytes 786440 | tf_op jit(solution)/shard_map/ppermute | solution.py:240
  43.4 3.5 %collective-permute-start.17 = (bf16[32,16,128]{2,1,0:T(8,128)(2,1)S(1)}, bf16[32,16,128]{2,1,0:T(8,128)(2,1)S(1)}, u32[]{:S(2)}, u32[]{:S(2)}) collective-permute-start(bf16[32,16,128]{2,1,0:T(8,128)(2,1)S(1)} %get-tuple-element.28), channel_id=1, source_target_pairs={{0,0},{1,1},{2,2},{3,3},{4,16},{5,17},{6,18},{7,19},{8,8},{9,9},{1... | collective-permute-start | bytes 393224 | tf_op jit(solution)/shard_map/ppermute | solution.py:364
  47.0 2.0 %collective-permute-start.18 = (bf16[32,16,128]{2,1,0:T(8,128)(2,1)S(1)}, bf16[32,16,128]{2,1,0:T(8,128)(2,1)S(1)}, u32[]{:S(2)}, u32[]{:S(2)}) collective-permute-start(bf16[32,16,128]{2,1,0:T(8,128)(2,1)S(1)} %get-tuple-element.29), channel_id=1, source_target_pairs={{0,8},{1,9},{2,10},{3,11},{4,24},{5,25},{6,26},{7,27},{8,0},{9,1},... | collective-permute-start | bytes 393224 | tf_op jit(solution)/shard_map/ppermute | solution.py:364
  49.0 2.5 %collective-permute-start.19 = (bf16[32,16,128]{2,1,0:T(8,128)(2,1)S(1)}, bf16[32,16,128]{2,1,0:T(8,128)(2,1)S(1)}, u32[]{:S(2)}, u32[]{:S(2)}) collective-permute-start(bf16[32,16,128]{2,1,0:T(8,128)(2,1)S(1)} %get-tuple-element.30), channel_id=1, source_target_pairs={{0,1},{1,0},{2,3},{3,2},{4,17},{5,16},{6,19},{7,18},{8,9},{9,8},{1... | collective-permute-start | bytes 393224 | tf_op jit(solution)/shard_map/ppermute | solution.py:364
  51.5 0.1 collective-permute-start.20
  51.6 3.3 %collective-permute-done.18.refs_4_ = bf16[32,16,128]{2,1,0:T(8,128)(2,1)S(1)} collective-permute-done((bf16[32,16,128]{2,1,0:T(8,128)(2,1)S(1)}, bf16[32,16,128]{2,1,0:T(8,128)(2,1)S(1)}, u32[]{:S(2)}, u32[]{:S(2)}) %collective-permute-start.18) | collective-permute-done | bytes 131104 | tf_op jit(solution)/shard_map/ppermute | solution.py:364
  54.9 6.5 %collective-permute-done.19.refs_5_ = bf16[32,16,128]{2,1,0:T(8,128)(2,1)S(1)} collective-permute-done((bf16[32,16,128]{2,1,0:T(8,128)(2,1)S(1)}, bf16[32,16,128]{2,1,0:T(8,128)(2,1)S(1)}, u32[]{:S(2)}, u32[]{:S(2)}) %collective-permute-start.19) | collective-permute-done | bytes 131104 | tf_op jit(solution)/shard_map/ppermute | solution.py:364
  61.4 2.6 %collective-permute-done.20.refs_6_ = bf16[32,16,128]{2,1,0:T(8,128)(2,1)S(1)} collective-permute-done((bf16[32,16,128]{2,1,0:T(8,128)(2,1)S(1)}, bf16[32,16,128]{2,1,0:T(8,128)(2,1)S(1)}, u32[]{:S(2)}, u32[]{:S(2)}) %collective-permute-start.20) | collective-permute-done | bytes 131104 | tf_op jit(solution)/shard_map/ppermute | solution.py:364
  64.0 2.7 %finish.2.refs_11_ = bf16[16,128,128]{2,1,0:T(8,128)(2,1)} custom-call(s32[4]{0:T(128)S(1)} %pad_add_fusion.refs_0_, bf16[16,128,128]{2,1,0:T(8,128)(2,1)S(1)} %copy-done, bf16[16,64,128]{2,1,0:T(8,128)(2,1)S(1)} %get-tuple-element.32.refs_2_, bf16[32,16,128]{2,1,0:T(8,128)(2,1)S(1)} %collective-permute-done.17.refs_3_, ...), custom_call_target="tpu_custom_call" | custom-call | tf_op jit(solution)/shard_map/finish/pallas_call | solution.py:381
  66.6 2.7 %finish.3 = bf16[16,128,128]{2,1,0:T(8,128)(2,1)} custom-call(s32[4]{0:T(128)S(1)} %pad_add_fusion.refs_0_, bf16[16,128,128]{2,1,0:T(8,128)(2,1)S(1)} %copy-done, bf16[16,64,128]{2,1,0:T(8,128)(2,1)S(1)} %collective-permute-done.16.refs_2_, bf16[32,16,128]{2,1,0:T(8,128)(2,1)S(1)} %collective-permute-done.17.refs_3_, ...), custom_call_target="tpu_custom_call", output_to_operand_aliasing={{}: (11, {})} | custom-call | tf_op jit(solution)/shard_map/finish/pallas_call | solution.py:381
  (50 shorter events, 0.5 us)
Async XLA Ops:
  1.5 4.2 %copy-start.8 = (bf16[128,32,64]{0,2,1:T(8,128)(2,1)S(1)}, bf16[128,32,64]{0,2,1:T(8,128)(2,1)}, u32[]{:S(2)}) copy-start(bf16[128,32,64]{0,2,1:T(8,128)(2,1)} %param.10) | copy-start | bytes 1572868
  1.7 6.7 %collective-permute-start.10 = (bf16[512,128]{1,0:T(8,128)(2,1)S(1)}, bf16[512,128]{1,0:T(8,128)(2,1)S(1)}, u32[]{:S(2)}, u32[]{:S(2)}) collective-permute-start(bf16[512,128]{1,0:T(8,128)(2,1)S(1)} %bitcast.45), channel_id=1, source_target_pairs={{0,16},{8,24},{16,0},{24,8},{1,17},{9,25},{17,1},{25,9},{2,18},{10... | collective-permute-start | bytes 393224 | tf_op jit(solution)/shard_map/ppermute | solution.py:240
  1.7 6.7 %collective-permute-start.6 = (bf16[512,128]{1,0:T(8,128)(2,1)S(1)}, bf16[512,128]{1,0:T(8,128)(2,1)S(1)}, u32[]{:S(2)}, u32[]{:S(2)}) collective-permute-start(bf16[512,128]{1,0:T(8,128)(2,1)S(1)} %bitcast.46), channel_id=1, source_target_pairs={{0,1},{1,0},{2,3},{3,2},{4,5},{5,4},{6,7},{7,6},{8,9},{9,8},{10,11... | collective-permute-start | bytes 393224 | tf_op jit(solution)/shard_map/ppermute | solution.py:240
  3.4 13.4 %collective-permute-start.7 = (bf16[512,128]{1,0:T(8,128)(2,1)S(1)}, bf16[512,128]{1,0:T(8,128)(2,1)S(1)}, u32[]{:S(2)}, u32[]{:S(2)}) collective-permute-start(bf16[512,128]{1,0:T(8,128)(2,1)S(1)} %bitcast.56), channel_id=1, source_target_pairs={{0,3},{1,2},{2,1},{3,0},{4,7},{5,6},{6,5},{7,4},{8,11},{9,10},{10,... | collective-permute-start | bytes 393224 | tf_op jit(solution)/shard_map/ppermute | solution.py:240
  6.0 1.5 %copy-start.9 = (bf16[1024,128]{1,0:T(8,128)(2,1)S(1)}, bf16[1024,128]{1,0:T(8,128)(2,1)}, u32[]{:S(2)}) copy-start(bf16[1024,128]{1,0:T(8,128)(2,1)} %param.12) | copy-start | bytes 786436
  6.0 8.6 %collective-permute-start = (bf16[512,128]{1,0:T(8,128)(2,1)S(1)}, bf16[512,128]{1,0:T(8,128)(2,1)S(1)}, u32[]{:S(2)}, u32[]{:S(2)}) collective-permute-start(bf16[512,128]{1,0:T(8,128)(2,1)S(1)} %get-tuple-element.33), channel_id=1, source_target_pairs={{0,1},{1,0},{2,3},{3,2},{4,5},{5,4},{6,7},{7,6},{8,9},{9,8},{10,11... | collective-permute-start | bytes 393224 | tf_op jit(solution)/shard_map/ppermute | solution.py:240
  6.5 13.7 %collective-permute-start.2 = (bf16[512,128]{1,0:T(8,128)(2,1)S(1)}, bf16[512,128]{1,0:T(8,128)(2,1)S(1)}, u32[]{:S(2)}, u32[]{:S(2)}) collective-permute-start(bf16[512,128]{1,0:T(8,128)(2,1)S(1)} %get-tuple-element.34.refs_0_), channel_id=1, source_target_pairs={{0,2},{1,3},{2,0},{3,1},{4,6},{5,7},{6,4},{7,5},{8,10},{9,11},{10,... | collective-permute-start | bytes 393224 | tf_op jit(solution)/shard_map/ppermute | solution.py:240
  7.9 1.8 %copy-start.10 = (f32[512]{0:T(512)S(1)}, f32[512]{0:T(512)}, u32[]{:S(2)}) copy-start(f32[512]{0:T(512)} %param.17) | copy-start | bytes 6148
  7.9 1.8 %copy-start.12 = (f32[128]{0:T(128)S(1)}, f32[128]{0:T(128)}, u32[]{:S(2)}) copy-start(f32[128]{0:T(128)} %param.19) | copy-start | bytes 1540
  7.9 1.8 %copy-start.13 = (f32[128]{0:T(128)S(1)}, f32[128]{0:T(128)}, u32[]{:S(2)}) copy-start(f32[128]{0:T(128)} %param.15) | copy-start | bytes 1540
  8.4 10.4 %collective-permute-start.11 = (bf16[512,128]{1,0:T(8,128)(2,1)S(1)}, bf16[512,128]{1,0:T(8,128)(2,1)S(1)}, u32[]{:S(2)}, u32[]{:S(2)}) collective-permute-start(bf16[512,128]{1,0:T(8,128)(2,1)S(1)} %collective-permute-done.6.refs_1_.refs_3_.refs_5_), channel_id=1, source_target_pairs={{0,16},{8,24},{16,0},{24,8},{1,17},{9,25},{17,1},{25,9},{2,18},{10... | collective-permute-start | bytes 393224 | tf_op jit(solution)/shard_map/ppermute | solution.py:240
  14.7 11.8 %collective-permute-start.1 = (bf16[1024,128]{1,0:T(8,128)(2,1)S(1)}, bf16[1024,128]{1,0:T(8,128)(2,1)S(1)}, u32[]{:S(2)}, u32[]{:S(2)}) collective-permute-start(bf16[1024,128]{1,0:T(8,128)(2,1)S(1)} %pack.3.refs_0_), channel_id=1, source_target_pairs={{0,4},{4,0},{1,5},{5,1},{2,6},{6,2},{3,7},{7,3},{8,12},{12,8},{9,1... | collective-permute-start | bytes 786440 | tf_op jit(solution)/shard_map/ppermute | solution.py:240
  16.8 3.3 %copy-start.11 = (f32[128]{0:T(128)S(1)}, f32[128]{0:T(128)}, u32[]{:S(2)}) copy-start(f32[128]{0:T(128)} %param.13) | copy-start | bytes 1540
  16.8 11.0 %collective-permute-start.4 = (bf16[512,128]{1,0:T(8,128)(2,1)S(1)}, bf16[512,128]{1,0:T(8,128)(2,1)S(1)}, u32[]{:S(2)}, u32[]{:S(2)}) collective-permute-start(bf16[512,128]{1,0:T(8,128)(2,1)S(1)} %collective-permute-done.refs_1_), channel_id=1, source_target_pairs={{0,2},{1,3},{2,0},{3,1},{4,6},{5,7},{6,4},{7,5},{8,10},{9,11},{10,... | collective-permute-start | bytes 393224 | tf_op jit(solution)/shard_map/ppermute | solution.py:240
  16.8 6.0 %collective-permute-start.8 = (bf16[512,128]{1,0:T(8,128)(2,1)S(1)}, bf16[512,128]{1,0:T(8,128)(2,1)S(1)}, u32[]{:S(2)}, u32[]{:S(2)}) collective-permute-start(bf16[512,128]{1,0:T(8,128)(2,1)S(1)} %collective-permute-done.7.refs_2_.refs_4_.refs_6_), channel_id=1, source_target_pairs={{0,1},{1,0},{2,3},{3,2},{4,5},{5,4},{6,7},{7,6},{8,9},{9,8},{10,11... | collective-permute-start | bytes 393224 | tf_op jit(solution)/shard_map/ppermute | solution.py:240
  18.8 7.6 %collective-permute-start.12 = (bf16[512,128]{1,0:T(8,128)(2,1)S(1)}, bf16[512,128]{1,0:T(8,128)(2,1)S(1)}, u32[]{:S(2)}, u32[]{:S(2)}) collective-permute-start(bf16[512,128]{1,0:T(8,128)(2,1)S(1)} %collective-permute-done.7.refs_2_.refs_4_.refs_6_), channel_id=1, source_target_pairs={{0,16},{8,24},{16,0},{24,8},{1,17},{9,25},{17,1},{25,9},{2,18},{10... | collective-permute-start | bytes 393224 | tf_op jit(solution)/shard_map/ppermute | solution.py:240
  20.2 9.0 %collective-permute-start.3 = (bf16[512,128]{1,0:T(8,128)(2,1)S(1)}, bf16[512,128]{1,0:T(8,128)(2,1)S(1)}, u32[]{:S(2)}, u32[]{:S(2)}) collective-permute-start(bf16[512,128]{1,0:T(8,128)(2,1)S(1)} %collective-permute-done.2.refs_1_), channel_id=1, source_target_pairs={{0,4},{4,0},{1,5},{5,1},{2,6},{6,2},{3,7},{7,3},{8,12},{12,8},{9,1... | collective-permute-start | bytes 393224 | tf_op jit(solution)/shard_map/ppermute | solution.py:240
  22.8 11.2 %collective-permute-start.9 = (bf16[2048,128]{1,0:T(8,128)(2,1)S(1)}, bf16[2048,128]{1,0:T(8,128)(2,1)S(1)}, u32[]{:S(2)}, u32[]{:S(2)}) collective-permute-start(bf16[2048,128]{1,0:T(8,128)(2,1)S(1)} %pack.4), channel_id=1, source_target_pairs={{0,8},{8,0},{16,24},{24,16},{1,9},{9,1},{17,25},{25,17},{2,10},{10... | collective-permute-start | bytes 1572872 | tf_op jit(solution)/shard_map/ppermute | solution.py:240
  26.4 7.6 %collective-permute-start.14 = (bf16[1536,128]{1,0:T(8,128)(2,1)S(1)}, bf16[1536,128]{1,0:T(8,128)(2,1)S(1)}, u32[]{:S(2)}, u32[]{:S(2)}) collective-permute-start(bf16[1536,128]{1,0:T(8,128)(2,1)S(1)} %pack.5), channel_id=1, source_target_pairs={{0,8},{8,0},{16,24},{24,16},{1,9},{9,1},{17,25},{25,17},{2,10},{10... | collective-permute-start | bytes 1179656 | tf_op jit(solution)/shard_map/ppermute | solution.py:240
  26.5 4.8 %collective-permute-start.13 = (bf16[512,128]{1,0:T(8,128)(2,1)S(1)}, bf16[512,128]{1,0:T(8,128)(2,1)}, u32[]{:S(2)}, u32[]{:S(2)}) collective-permute-start(bf16[512,128]{1,0:T(8,128)(2,1)S(1)} %collective-permute-done.8.refs_3_.refs_5_.refs_7_), channel_id=1, source_target_pairs={{0,16},{8,24},{16,0},{24,8},{1,17},{9,25},{17,1},{25,9},{2,18},{10... | collective-permute-start | bytes 393224 | tf_op jit(solution)/shard_map/ppermute | solution.py:240
  27.7 0.7 copy-start.3
  28.4 0.8 %copy-start.6 = (bf16[512,512]{1,0:T(8,128)(2,1)}, bf16[512,512]{1,0:T(8,128)(2,1)S(1)}, u32[]{:S(2)}) copy-start(bf16[512,512]{1,0:T(8,128)(2,1)S(1)} %arrange.1.refs_1_) | copy-start | bytes 1572868
  29.2 0.7 copy-start.4
  31.3 2.7 %collective-permute-start.15 = (bf16[512,128]{1,0:T(8,128)(2,1)}, bf16[512,128]{1,0:T(8,128)(2,1)}, u32[]{:S(2)}, u32[]{:S(2)}) collective-permute-start(bf16[512,128]{1,0:T(8,128)(2,1)} %collective-permute-done.13.refs_10_.refs_12_), channel_id=1, source_target_pairs={{0,8},{8,0},{16,24},{24,16},{1,9},{9,1},{17,25},{25,17},{2,10},{10... | collective-permute-start | bytes 393224 | tf_op jit(solution)/shard_map/ppermute | solution.py:240
  33.7 5.4 %copy-start.5 = (bf16[512,128]{1,0:T(8,128)(2,1)S(1)}, bf16[512,128]{1,0:T(8,128)(2,1)}, u32[]{:S(2)}) copy-start(bf16[512,128]{1,0:T(8,128)(2,1)} %copy-done.4) | copy-start | bytes 393220
  33.7 5.4 %collective-permute-start.5 = (bf16[512,128]{1,0:T(8,128)(2,1)}, bf16[512,128]{1,0:T(8,128)(2,1)S(1)}, u32[]{:S(2)}, u32[]{:S(2)}) collective-permute-start(bf16[512,128]{1,0:T(8,128)(2,1)} %copy-done.3), channel_id=1, source_target_pairs={{0,4},{4,0},{1,5},{5,1},{2,6},{6,2},{3,7},{7,3},{8,12},{12,8},{9,1... | collective-permute-start | bytes 393224 | tf_op jit(solution)/shard_map/ppermute | solution.py:240
  34.0 1.0 %copy-start.7 = (bf16[512,512]{1,0:T(8,128)(2,1)S(1)}, bf16[512,512]{1,0:T(8,128)(2,1)}, u32[]{:S(2)}) copy-start(bf16[512,512]{1,0:T(8,128)(2,1)} %copy-done.6) | copy-start | bytes 1572868
  38.4 25.5 %copy-start = (bf16[16,128,128]{2,1,0:T(8,128)(2,1)S(1)}, bf16[16,128,128]{2,1,0:T(8,128)(2,1)}, u32[]{:S(2)}) copy-start(bf16[16,128,128]{2,1,0:T(8,128)(2,1)} %refs_1_.3) | copy-start | bytes 1572868
  38.5 25.5 %copy-start.1 = (bf16[128,512]{1,0:T(8,128)(2,1)S(1)}, bf16[128,512]{1,0:T(8,128)(2,1)}, u32[]{:S(2)}) copy-start(bf16[128,512]{1,0:T(8,128)(2,1)} %refs_7_.3) | copy-start | bytes 393220
  38.5 25.5 %copy-start.2 = (bf16[512,128]{1,0:T(8,128)(2,1)S(1)}, bf16[512,128]{1,0:T(8,128)(2,1)}, u32[]{:S(2)}) copy-start(bf16[512,128]{1,0:T(8,128)(2,1)} %refs_8_.3) | copy-start | bytes 393220
  42.6 24.0 %collective-permute-start.16 = (bf16[16,64,128]{2,1,0:T(8,128)(2,1)S(1)}, bf16[16,64,128]{2,1,0:T(8,128)(2,1)S(1)}, u32[]{:S(2)}, u32[]{:S(2)}) collective-permute-start(bf16[16,64,128]{2,1,0:T(8,128)(2,1)S(1)} %get-tuple-element.27), channel_id=1, source_target_pairs={{0,2},{1,3},{2,0},{3,1},{4,6},{5,7},{6,4},{7,5},{8,10},{9,11},{10,... | collective-permute-start | bytes 786440 | tf_op jit(solution)/shard_map/ppermute | solution.py:240
  43.4 8.2 %collective-permute-start.17 = (bf16[32,16,128]{2,1,0:T(8,128)(2,1)S(1)}, bf16[32,16,128]{2,1,0:T(8,128)(2,1)S(1)}, u32[]{:S(2)}, u32[]{:S(2)}) collective-permute-start(bf16[32,16,128]{2,1,0:T(8,128)(2,1)S(1)} %get-tuple-element.28), channel_id=1, source_target_pairs={{0,0},{1,1},{2,2},{3,3},{4,16},{5,17},{6,18},{7,19},{8,8},{9,9},{1... | collective-permute-start | bytes 393224 | tf_op jit(solution)/shard_map/ppermute | solution.py:364
  47.0 7.9 %collective-permute-start.18 = (bf16[32,16,128]{2,1,0:T(8,128)(2,1)S(1)}, bf16[32,16,128]{2,1,0:T(8,128)(2,1)S(1)}, u32[]{:S(2)}, u32[]{:S(2)}) collective-permute-start(bf16[32,16,128]{2,1,0:T(8,128)(2,1)S(1)} %get-tuple-element.29), channel_id=1, source_target_pairs={{0,8},{1,9},{2,10},{3,11},{4,24},{5,25},{6,26},{7,27},{8,0},{9,1},... | collective-permute-start | bytes 393224 | tf_op jit(solution)/shard_map/ppermute | solution.py:364
  49.0 12.4 %collective-permute-start.19 = (bf16[32,16,128]{2,1,0:T(8,128)(2,1)S(1)}, bf16[32,16,128]{2,1,0:T(8,128)(2,1)S(1)}, u32[]{:S(2)}, u32[]{:S(2)}) collective-permute-start(bf16[32,16,128]{2,1,0:T(8,128)(2,1)S(1)} %get-tuple-element.30), channel_id=1, source_target_pairs={{0,1},{1,0},{2,3},{3,2},{4,17},{5,16},{6,19},{7,18},{8,9},{9,8},{1... | collective-permute-start | bytes 393224 | tf_op jit(solution)/shard_map/ppermute | solution.py:364
  51.5 12.5 %collective-permute-start.20 = (bf16[32,16,128]{2,1,0:T(8,128)(2,1)S(1)}, bf16[32,16,128]{2,1,0:T(8,128)(2,1)S(1)}, u32[]{:S(2)}, u32[]{:S(2)}) collective-permute-start(bf16[32,16,128]{2,1,0:T(8,128)(2,1)S(1)} %get-tuple-element.31), channel_id=1, source_target_pairs={{0,9},{1,8},{2,11},{3,10},{4,25},{5,24},{6,27},{7,26},{8,1},{9,0},... | collective-permute-start | bytes 393224 | tf_op jit(solution)/shard_map/ppermute | solution.py:364

commit v2 on v1

--- a/solution.py
+++ b/solution.py
@@ -266,9 +266,6 @@
     cell = jnp.arange(run * run)
     mirror_cell = cell % run * run + cell // run
     swap_cells = (mirror_cell[:, None] == cell[None, :]).astype(bf16)
-    weight, bias, vectors, swap_cells = constants = lax.optimization_barrier(
-        (weight, bias, vectors, swap_cells)
-    )
     lefts = [pack(own, near)]
     fars = [swap(own, "seq", groups, low), swap(near, "seq", groups, low)]
     shares = [[swap(lefts[0], "col", cols, dy)] for dy in range(1, cols)]
@@ -284,22 +281,22 @@
     last = ()
     for dz in order:
         for dx in range(1, xs):
-            behind = last + ((near_shares, constants) if dz == low else ())
+            behind = last + ((near_shares,) if dz == low else ())
             crosses[dz].append(swap(after(blocks[dz], *behind), "row", rows, 2 * dx))
             last = (crosses[dz][-1],)
     for position in range(xs):
         values = [crosses[dz][position] for dz in order]
-        for dz, value in zip(order, values):
-            right_places[dz].append((len(data), 0))
+        count = len(order) if position == 0 else len(order) - 1
+        packed = pack(*values[:count])
+        for value in (packed, swap(packed, "row", rows, 1)):
+            for index, dz in enumerate(order[:count]):
+                right_places[dz].append((len(data), index * source_rows))
             data.append(value)
-        count = len(order) if position == 0 else len(order) - 1
-        exchanged = swap(pack(*values[:count]), "row", rows, 1)
-        for index, dz in enumerate(order[:count]):
-            right_places[dz].append((len(data), index * source_rows))
-        data.append(exchanged)
         if count < len(order):
-            right_places[low].append((len(data), 0))
-            data.append(swap(after(values[-1], first_lhs, far_shares), "row", rows, 1))
+            exchanged = swap(after(values[-1], first_lhs, far_shares), "row", rows, 1)
+            for value in (values[-1], exchanged):
+                right_places[low].append((len(data), 0))
+                data.append(value)
     right_places = [right_places[dz] for dz in range(groups)]
     last_lefts = [value for pair in shares for value in pair]
 

time: 69.5 us -> 67.6 us (0.973)
  local copies, waits for them, and re-layouts: 7.48 us -> 5.2 us
  Pallas kernels: 12.4 us -> 11.5 us
  waiting for transfers between devices: 21.7 us -> 22.5 us
    unnamed x30 -> x24, local copies, waits for them, and re-layouts: 5 us -> 3.67 us
    ppermute x17, waiting for transfers between devices: 9.29 us -> 10.4 us  [swap(): return lax.ppermute(value, name, [(i, i ^ flip) for i in range(size)])]
    optimization_barrier x1 -> x0, local copies, waits for them, and re-layouts: 1.09 us -> none  [on_device(): lax.optimization_barrier((weight, bias, vectors, swap_cells))]
    pallas_call x2, Pallas kernels: 6.96 us -> 6.06 us  [update_call(): pl.pallas_call(functools.partial(update_kernel, places, cols, low, last,...]
  transfers between devices with their start and end apart: 21 -> 21, of which waited for: 7 -> 7; matrix products, arithmetic and copies ran while one was open for 5% -> 3% of each run, Pallas kernels for 9% -> 9%
where the time goes in v2:
time: 67.6 us; the launch traced here: 67.3 us
  starting transfers between devices  27.1 us (40%)
  waiting for transfers between devices  22.5 us (33%)
  Pallas kernels  11.5 us (17%)
  local copies, waits for them, and re-layouts  5.2 us (8%)
    ppermute x17, starting transfers between devices, swap(): return lax.ppermute(value, name, [(i, i ^ flip) for i in range(size)])  18.8 us
    ppermute x4, waiting for transfers between devices, on_device(): mirrors.append(lax.ppermute(outs[2 + 2 * dz + flip], axes, pairs))  12.1 us
    ppermute x17, waiting for transfers between devices, swap(): return lax.ppermute(value, name, [(i, i ^ flip) for i in range(size)])  10.4 us
    ppermute x4, starting transfers between devices, on_device(): mirrors.append(lax.ppermute(outs[2 + 2 * dz + flip], axes, pairs))  8.35 us
    pallas_call x2, Pallas kernels, update_call(): pl.pallas_call(functools.partial(update_kernel, places, cols, low, last,...  6.06 us
    pallas_call x2, Pallas kernels, on_device(): pl.pallas_call(functools.partial(finish_kernel, low, other), out_shape=ja...  5.31 us
    unnamed x24, local copies, waits for them, and re-layouts  3.67 us
  transfers between devices with their start and end apart: 21, of which 7 were waited for; matrix products, arithmetic and copies ran while one was open for 3% of the time, Pallas kernels for 9%

profile of v2, /device:TPU:3, one launch (start us, length us, event | category | flops | bytes accessed | tf_op | source)
XLA Modules:
  0.0 67.3 jit_solution(14945633476397214503)
XLA Ops:
  0.0 1.1 %copy.19 = bf16[128,8,128]{0,2,1:T(8,128)(2,1)S(1)} copy(bf16[128,8,128]{2,1,0:T(8,128)(2,1)} %param.11) | data formatting | bytes 524288 | tf_op args[1]
  1.2 0.2 copy.20
  1.4 0.1 reshape.55
  1.5 0.1 copy.21
  1.7 1.5 %collective-permute-start.6 = (bf16[512,128]{1,0:T(8,128)(2,1)S(1)}, bf16[512,128]{1,0:T(8,128)(2,1)S(1)}, u32[]{:S(2)}, u32[]{:S(2)}) collective-permute-start(bf16[512,128]{1,0:T(8,128)(2,1)S(1)} %bitcast.46), channel_id=1, source_target_pairs={{0,1},{1,0},{2,3},{3,2},{4,5},{5,4},{6,7},{7,6},{8,9},{9,8},{10,11... | collective-permute-start | bytes 393224 | tf_op jit(solution)/shard_map/ppermute | solution.py:240
  3.3 0.1 copy.22
  3.4 2.3 %collective-permute-start.7 = (bf16[512,128]{1,0:T(8,128)(2,1)S(1)}, bf16[512,128]{1,0:T(8,128)(2,1)S(1)}, u32[]{:S(2)}, u32[]{:S(2)}) collective-permute-start(bf16[512,128]{1,0:T(8,128)(2,1)S(1)} %bitcast.54), channel_id=1, source_target_pairs={{0,3},{1,2},{2,1},{3,0},{4,7},{5,6},{6,5},{7,4},{8,11},{9,10},{10,... | collective-permute-start | bytes 393224 | tf_op jit(solution)/shard_map/ppermute | solution.py:240
  5.7 0.3 copy.18
  6.0 0.5 collective-permute-start
  6.5 1.0 %collective-permute-start.2 = (bf16[512,128]{1,0:T(8,128)(2,1)S(1)}, bf16[512,128]{1,0:T(8,128)(2,1)S(1)}, u32[]{:S(2)}, u32[]{:S(2)}) collective-permute-start(bf16[512,128]{1,0:T(8,128)(2,1)S(1)} %get-tuple-element.26.refs_0_), channel_id=1, source_target_pairs={{0,2},{1,3},{2,0},{3,1},{4,6},{5,7},{6,4},{7,5},{8,10},{9,11},{10,... | collective-permute-start | bytes 393224 | tf_op jit(solution)/shard_map/ppermute | solution.py:240
  7.5 0.2 constant_dynamic-slice_fusion.3
  7.7 1.3 %collective-permute-start.11 = (bf16[512,128]{1,0:T(8,128)(2,1)S(1)}, bf16[512,128]{1,0:T(8,128)(2,1)S(1)}, u32[]{:S(2)}, u32[]{:S(2)}) collective-permute-start(bf16[512,128]{1,0:T(8,128)(2,1)S(1)} %collective-permute-done.6.refs_1_), channel_id=1, source_target_pairs={{0,16},{8,24},{16,0},{24,8},{1,17},{9,25},{17,1},{25,9},{2,18},{10... | collective-permute-start | bytes 393224 | tf_op jit(solution)/shard_map/ppermute | solution.py:240
  9.0 0.1 copy_bitcast_fusion.1
  9.1 5.6 %collective-permute-done.refs_1_ = bf16[512,128]{1,0:T(8,128)(2,1)S(1)} collective-permute-done((bf16[512,128]{1,0:T(8,128)(2,1)S(1)}, bf16[512,128]{1,0:T(8,128)(2,1)S(1)}, u32[]{:S(2)}, u32[]{:S(2)}) %collective-permute-start) | collective-permute-done | bytes 131104 | tf_op jit(solution)/shard_map/ppermute | solution.py:240
  14.7 1.3 %collective-permute-start.1 = (bf16[1024,128]{1,0:T(8,128)(2,1)S(1)}, bf16[1024,128]{1,0:T(8,128)(2,1)S(1)}, u32[]{:S(2)}, u32[]{:S(2)}) collective-permute-start(bf16[1024,128]{1,0:T(8,128)(2,1)S(1)} %pack.3.refs_0_), channel_id=1, source_target_pairs={{0,4},{4,0},{1,5},{5,1},{2,6},{6,2},{3,7},{7,3},{8,12},{12,8},{9,1... | collective-permute-start | bytes 786440 | tf_op jit(solution)/shard_map/ppermute | solution.py:240
  16.0 2.0 %collective-permute-start.8 = (bf16[512,128]{1,0:T(8,128)(2,1)S(1)}, bf16[512,128]{1,0:T(8,128)(2,1)S(1)}, u32[]{:S(2)}, u32[]{:S(2)}) collective-permute-start(bf16[512,128]{1,0:T(8,128)(2,1)S(1)} %collective-permute-done.7.refs_2_), channel_id=1, source_target_pairs={{0,1},{1,0},{2,3},{3,2},{4,5},{5,4},{6,7},{7,6},{8,9},{9,8},{10,11... | collective-permute-start | bytes 393224 | tf_op jit(solution)/shard_map/ppermute | solution.py:240
  18.0 1.2 %collective-permute-start.12 = (bf16[512,128]{1,0:T(8,128)(2,1)S(1)}, bf16[512,128]{1,0:T(8,128)(2,1)S(1)}, u32[]{:S(2)}, u32[]{:S(2)}) collective-permute-start(bf16[512,128]{1,0:T(8,128)(2,1)S(1)} %collective-permute-done.7.refs_2_), channel_id=1, source_target_pairs={{0,16},{8,24},{16,0},{24,8},{1,17},{9,25},{17,1},{25,9},{2,18},{10... | collective-permute-start | bytes 393224 | tf_op jit(solution)/shard_map/ppermute | solution.py:240
  19.2 0.1 copy_bitcast_fusion.3
  19.3 0.5 pad_maximum_fusion
  19.8 0.3 collective-permute-start.3
  20.1 1.8 %collective-permute-done.8.refs_3_ = bf16[512,128]{1,0:T(8,128)(2,1)S(1)} collective-permute-done((bf16[512,128]{1,0:T(8,128)(2,1)S(1)}, bf16[512,128]{1,0:T(8,128)(2,1)S(1)}, u32[]{:S(2)}, u32[]{:S(2)}) %collective-permute-start.8) | collective-permute-done | bytes 131104 | tf_op jit(solution)/shard_map/ppermute | solution.py:240
  22.0 3.6 %collective-permute-start.9 = (bf16[2048,128]{1,0:T(8,128)(2,1)S(1)}, bf16[2048,128]{1,0:T(8,128)(2,1)S(1)}, u32[]{:S(2)}, u32[]{:S(2)}) collective-permute-start(bf16[2048,128]{1,0:T(8,128)(2,1)S(1)} %pack.4.refs_2_.refs_4_), channel_id=1, source_target_pairs={{0,8},{8,0},{16,24},{24,16},{1,9},{9,1},{17,25},{25,17},{2,10},{10... | collective-permute-start | bytes 1572872 | tf_op jit(solution)/shard_map/ppermute | solution.py:240
  25.6 1.2 %collective-permute-start.14 = (bf16[512,128]{1,0:T(8,128)(2,1)S(1)}, bf16[512,128]{1,0:T(8,128)(2,1)S(1)}, u32[]{:S(2)}, u32[]{:S(2)}) collective-permute-start(bf16[512,128]{1,0:T(8,128)(2,1)S(1)} %collective-permute-done.8.refs_3_), channel_id=1, source_target_pairs={{0,16},{8,24},{16,0},{24,8},{1,17},{9,25},{17,1},{25,9},{2,18},{10... | collective-permute-start | bytes 393224 | tf_op jit(solution)/shard_map/ppermute | solution.py:240
  26.8 0.4 collective-permute-start.13
  27.3 0.1 arrange.1.refs_1_
  27.4 0.8 %copy-done.3 = bf16[512,512]{1,0:T(8,128)(2,1)} copy-done((bf16[512,512]{1,0:T(8,128)(2,1)}, bf16[512,512]{1,0:T(8,128)(2,1)S(1)}, u32[]{:S(2)}) %copy-start.3) | copy-done | bytes 524312
  28.2 2.5 %collective-permute-done.14.refs_6_.refs_8_ = bf16[512,128]{1,0:T(8,128)(2,1)S(1)} collective-permute-done((bf16[512,128]{1,0:T(8,128)(2,1)S(1)}, bf16[512,128]{1,0:T(8,128)(2,1)S(1)}, u32[]{:S(2)}, u32[]{:S(2)}) %collective-permute-start.14) | collective-permute-done | bytes 131104 | tf_op jit(solution)/shard_map/ppermute | solution.py:240
  30.7 0.9 %collective-permute-start.15 = (bf16[512,128]{1,0:T(8,128)(2,1)S(1)}, bf16[512,128]{1,0:T(8,128)(2,1)S(1)}, u32[]{:S(2)}, u32[]{:S(2)}) collective-permute-start(bf16[512,128]{1,0:T(8,128)(2,1)S(1)} %collective-permute-done.14.refs_6_.refs_8_), channel_id=1, source_target_pairs={{0,8},{8,0},{16,24},{24,16},{1,9},{9,1},{17,25},{25,17},{2,10},{10... | collective-permute-start | bytes 393224 | tf_op jit(solution)/shard_map/ppermute | solution.py:240
  31.5 0.1 pad_add_fusion.refs_0_
  31.7 0.1 copy.28.refs_9_.refs_11_
  31.8 0.5 copy-done.7
  32.3 0.5 collective-permute-start.5
  32.9 0.1 copy-done.8
  33.0 0.1 broadcast_in_dim.2.refs_8_.refs_10_
  33.1 1.0 %copy-done.4 = bf16[512,512]{1,0:T(8,128)(2,1)S(1)} copy-done((bf16[512,512]{1,0:T(8,128)(2,1)S(1)}, bf16[512,512]{1,0:T(8,128)(2,1)}, u32[]{:S(2)}) %copy-start.4) | copy-done | bytes 524312
  34.1 3.0 %update_first.1.refs_12_ = bf16[16,64,128]{2,1,0:T(8,128)(2,1)S(1)} custom-call(s32[4]{0:T(128)S(1)} %pad_add_fusion.refs_0_, bf16[512,512]{1,0:T(8,128)(2,1)S(1)} %copy-done.4, bf16[2048,128]{1,0:T(8,128)(2,1)S(1)} %pack.4.refs_2_.refs_4_, bf16[2048,128]{1,0:T(8,128)(2,1)S(1)} %collective-permute-done.9.refs_3_.refs_5_, ...), custom_call_target="tpu_custom_call" | custom-call | flops 1610612736 | bytes 2097152 | tf_op jit(solution)/shard_map/update_first/pallas_call | solution.py:315
  37.1 0.4 collective-permute-done.5.refs_3_
  37.5 3.1 %update_last.1 = (bf16[16,64,128]{2,1,0:T(8,128)(2,1)S(1)}, bf16[16,64,128]{2,1,0:T(8,128)(2,1)S(1)}, bf16[32,16,128]{2,1,0:T(8,128)(2,1)S(1)}, bf16[32,16,128]{...) custom-call(s32[4]{0:T(128)S(1)} %pad_add_fusion.refs_0_, ...), custom_call_target="tpu_custom_call" | custom-call | flops 1610612736 | bytes 2097152 | tf_op jit(solution)/shard_map/update_last/pallas_call | solution.py:315
  40.7 0.8 %collective-permute-start.16 = (bf16[16,64,128]{2,1,0:T(8,128)(2,1)S(1)}, bf16[16,64,128]{2,1,0:T(8,128)(2,1)S(1)}, u32[]{:S(2)}, u32[]{:S(2)}) collective-permute-start(bf16[16,64,128]{2,1,0:T(8,128)(2,1)S(1)} %get-tuple-element.19), channel_id=1, source_target_pairs={{0,2},{1,3},{2,0},{3,1},{4,6},{5,7},{6,4},{7,5},{8,10},{9,11},{10,... | collective-permute-start | bytes 786440 | tf_op jit(solution)/shard_map/ppermute | solution.py:240
  41.4 3.3 %collective-permute-start.17 = (bf16[32,16,128]{2,1,0:T(8,128)(2,1)S(1)}, bf16[32,16,128]{2,1,0:T(8,128)(2,1)S(1)}, u32[]{:S(2)}, u32[]{:S(2)}) collective-permute-start(bf16[32,16,128]{2,1,0:T(8,128)(2,1)S(1)} %get-tuple-element.20), channel_id=1, source_target_pairs={{0,0},{1,1},{2,2},{3,3},{4,16},{5,17},{6,18},{7,19},{8,8},{9,9},{1... | collective-permute-start | bytes 393224 | tf_op jit(solution)/shard_map/ppermute | solution.py:361
  44.8 2.2 %collective-permute-start.18 = (bf16[32,16,128]{2,1,0:T(8,128)(2,1)S(1)}, bf16[32,16,128]{2,1,0:T(8,128)(2,1)S(1)}, u32[]{:S(2)}, u32[]{:S(2)}) collective-permute-start(bf16[32,16,128]{2,1,0:T(8,128)(2,1)S(1)} %get-tuple-element.21), channel_id=1, source_target_pairs={{0,8},{1,9},{2,10},{3,11},{4,24},{5,25},{6,26},{7,27},{8,0},{9,1},... | collective-permute-start | bytes 393224 | tf_op jit(solution)/shard_map/ppermute | solution.py:361
  47.0 2.8 %collective-permute-start.19 = (bf16[32,16,128]{2,1,0:T(8,128)(2,1)S(1)}, bf16[32,16,128]{2,1,0:T(8,128)(2,1)S(1)}, u32[]{:S(2)}, u32[]{:S(2)}) collective-permute-start(bf16[32,16,128]{2,1,0:T(8,128)(2,1)S(1)} %get-tuple-element.22), channel_id=1, source_target_pairs={{0,1},{1,0},{2,3},{3,2},{4,17},{5,16},{6,19},{7,18},{8,9},{9,8},{1... | collective-permute-start | bytes 393224 | tf_op jit(solution)/shard_map/ppermute | solution.py:361
  49.8 0.1 fusion.refs_10_
  49.9 2.8 %collective-permute-done.18.refs_4_ = bf16[32,16,128]{2,1,0:T(8,128)(2,1)S(1)} collective-permute-done((bf16[32,16,128]{2,1,0:T(8,128)(2,1)S(1)}, bf16[32,16,128]{2,1,0:T(8,128)(2,1)S(1)}, u32[]{:S(2)}, u32[]{:S(2)}) %collective-permute-start.18) | collective-permute-done | bytes 131104 | tf_op jit(solution)/shard_map/ppermute | solution.py:361
  52.8 6.4 %collective-permute-done.19.refs_5_ = bf16[32,16,128]{2,1,0:T(8,128)(2,1)S(1)} collective-permute-done((bf16[32,16,128]{2,1,0:T(8,128)(2,1)S(1)}, bf16[32,16,128]{2,1,0:T(8,128)(2,1)S(1)}, u32[]{:S(2)}, u32[]{:S(2)}) %collective-permute-start.19) | collective-permute-done | bytes 131104 | tf_op jit(solution)/shard_map/ppermute | solution.py:361
  59.2 2.8 %collective-permute-done.20.refs_6_ = bf16[32,16,128]{2,1,0:T(8,128)(2,1)S(1)} collective-permute-done((bf16[32,16,128]{2,1,0:T(8,128)(2,1)S(1)}, bf16[32,16,128]{2,1,0:T(8,128)(2,1)S(1)}, u32[]{:S(2)}, u32[]{:S(2)}) %collective-permute-start.20) | collective-permute-done | bytes 131104 | tf_op jit(solution)/shard_map/ppermute | solution.py:361
  62.0 2.7 %finish.2.refs_11_ = bf16[16,128,128]{2,1,0:T(8,128)(2,1)} custom-call(s32[4]{0:T(128)S(1)} %pad_add_fusion.refs_0_, bf16[16,128,128]{2,1,0:T(8,128)(2,1)S(1)} %copy-done, bf16[16,64,128]{2,1,0:T(8,128)(2,1)S(1)} %get-tuple-element.24.refs_2_, bf16[32,16,128]{2,1,0:T(8,128)(2,1)S(1)} %collective-permute-done.17.refs_3_, ...), custom_call_target="tpu_custom_call" | custom-call | tf_op jit(solution)/shard_map/finish/pallas_call | solution.py:378
  64.7 2.7 %finish.3 = bf16[16,128,128]{2,1,0:T(8,128)(2,1)} custom-call(s32[4]{0:T(128)S(1)} %pad_add_fusion.refs_0_, bf16[16,128,128]{2,1,0:T(8,128)(2,1)S(1)} %copy-done, bf16[16,64,128]{2,1,0:T(8,128)(2,1)S(1)} %collective-permute-done.16.refs_2_, bf16[32,16,128]{2,1,0:T(8,128)(2,1)S(1)} %collective-permute-done.17.refs_3_, ...), custom_call_target="tpu_custom_call", output_to_operand_aliasing={{}: (11, {})} | custom-call | tf_op jit(solution)/shard_map/finish/pallas_call | solution.py:378
  (44 shorter events, 0.4 us)
Async XLA Ops:
  1.5 4.2 %copy-start.5 = (bf16[128,32,64]{0,2,1:T(8,128)(2,1)S(1)}, bf16[128,32,64]{0,2,1:T(8,128)(2,1)}, u32[]{:S(2)}) copy-start(bf16[128,32,64]{0,2,1:T(8,128)(2,1)} %param.10) | copy-start | bytes 1572868
  1.7 6.0 %collective-permute-start.10 = (bf16[512,128]{1,0:T(8,128)(2,1)S(1)}, bf16[512,128]{1,0:T(8,128)(2,1)S(1)}, u32[]{:S(2)}, u32[]{:S(2)}) collective-permute-start(bf16[512,128]{1,0:T(8,128)(2,1)S(1)} %bitcast.45), channel_id=1, source_target_pairs={{0,16},{8,24},{16,0},{24,8},{1,17},{9,25},{17,1},{25,9},{2,18},{10... | collective-permute-start | bytes 393224 | tf_op jit(solution)/shard_map/ppermute | solution.py:240
  1.7 5.9 %collective-permute-start.6 = (bf16[512,128]{1,0:T(8,128)(2,1)S(1)}, bf16[512,128]{1,0:T(8,128)(2,1)S(1)}, u32[]{:S(2)}, u32[]{:S(2)}) collective-permute-start(bf16[512,128]{1,0:T(8,128)(2,1)S(1)} %bitcast.46), channel_id=1, source_target_pairs={{0,1},{1,0},{2,3},{3,2},{4,5},{5,4},{6,7},{7,6},{8,9},{9,8},{10,11... | collective-permute-start | bytes 393224 | tf_op jit(solution)/shard_map/ppermute | solution.py:240
  3.4 12.6 %collective-permute-start.7 = (bf16[512,128]{1,0:T(8,128)(2,1)S(1)}, bf16[512,128]{1,0:T(8,128)(2,1)S(1)}, u32[]{:S(2)}, u32[]{:S(2)}) collective-permute-start(bf16[512,128]{1,0:T(8,128)(2,1)S(1)} %bitcast.54), channel_id=1, source_target_pairs={{0,3},{1,2},{2,1},{3,0},{4,7},{5,6},{6,5},{7,4},{8,11},{9,10},{10,... | collective-permute-start | bytes 393224 | tf_op jit(solution)/shard_map/ppermute | solution.py:240
  6.0 1.5 %copy-start.6 = (bf16[1024,128]{1,0:T(8,128)(2,1)S(1)}, bf16[1024,128]{1,0:T(8,128)(2,1)}, u32[]{:S(2)}) copy-start(bf16[1024,128]{1,0:T(8,128)(2,1)} %param.12) | copy-start | bytes 786436
  6.0 8.6 %collective-permute-start = (bf16[512,128]{1,0:T(8,128)(2,1)S(1)}, bf16[512,128]{1,0:T(8,128)(2,1)S(1)}, u32[]{:S(2)}, u32[]{:S(2)}) collective-permute-start(bf16[512,128]{1,0:T(8,128)(2,1)S(1)} %get-tuple-element.25), channel_id=1, source_target_pairs={{0,1},{1,0},{2,3},{3,2},{4,5},{5,4},{6,7},{7,6},{8,9},{9,8},{10,11... | collective-permute-start | bytes 393224 | tf_op jit(solution)/shard_map/ppermute | solution.py:240
  6.5 13.3 %collective-permute-start.2 = (bf16[512,128]{1,0:T(8,128)(2,1)S(1)}, bf16[512,128]{1,0:T(8,128)(2,1)S(1)}, u32[]{:S(2)}, u32[]{:S(2)}) collective-permute-start(bf16[512,128]{1,0:T(8,128)(2,1)S(1)} %get-tuple-element.26.refs_0_), channel_id=1, source_target_pairs={{0,2},{1,3},{2,0},{3,1},{4,6},{5,7},{6,4},{7,5},{8,10},{9,11},{10,... | collective-permute-start | bytes 393224 | tf_op jit(solution)/shard_map/ppermute | solution.py:240
  7.7 10.3 %collective-permute-start.11 = (bf16[512,128]{1,0:T(8,128)(2,1)S(1)}, bf16[512,128]{1,0:T(8,128)(2,1)S(1)}, u32[]{:S(2)}, u32[]{:S(2)}) collective-permute-start(bf16[512,128]{1,0:T(8,128)(2,1)S(1)} %collective-permute-done.6.refs_1_), channel_id=1, source_target_pairs={{0,16},{8,24},{16,0},{24,8},{1,17},{9,25},{17,1},{25,9},{2,18},{10... | collective-permute-start | bytes 393224 | tf_op jit(solution)/shard_map/ppermute | solution.py:240
  14.7 10.9 %collective-permute-start.1 = (bf16[1024,128]{1,0:T(8,128)(2,1)S(1)}, bf16[1024,128]{1,0:T(8,128)(2,1)S(1)}, u32[]{:S(2)}, u32[]{:S(2)}) collective-permute-start(bf16[1024,128]{1,0:T(8,128)(2,1)S(1)} %pack.3.refs_0_), channel_id=1, source_target_pairs={{0,4},{4,0},{1,5},{5,1},{2,6},{6,2},{3,7},{7,3},{8,12},{12,8},{9,1... | collective-permute-start | bytes 786440 | tf_op jit(solution)/shard_map/ppermute | solution.py:240
  16.0 11.3 %collective-permute-start.4 = (bf16[512,128]{1,0:T(8,128)(2,1)S(1)}, bf16[512,128]{1,0:T(8,128)(2,1)S(1)}, u32[]{:S(2)}, u32[]{:S(2)}) collective-permute-start(bf16[512,128]{1,0:T(8,128)(2,1)S(1)} %collective-permute-done.refs_1_), channel_id=1, source_target_pairs={{0,2},{1,3},{2,0},{3,1},{4,6},{5,7},{6,4},{7,5},{8,10},{9,11},{10,... | collective-permute-start | bytes 393224 | tf_op jit(solution)/shard_map/ppermute | solution.py:240
  16.0 6.0 %collective-permute-start.8 = (bf16[512,128]{1,0:T(8,128)(2,1)S(1)}, bf16[512,128]{1,0:T(8,128)(2,1)S(1)}, u32[]{:S(2)}, u32[]{:S(2)}) collective-permute-start(bf16[512,128]{1,0:T(8,128)(2,1)S(1)} %collective-permute-done.7.refs_2_), channel_id=1, source_target_pairs={{0,1},{1,0},{2,3},{3,2},{4,5},{5,4},{6,7},{7,6},{8,9},{9,8},{10,11... | collective-permute-start | bytes 393224 | tf_op jit(solution)/shard_map/ppermute | solution.py:240
  18.0 7.6 %collective-permute-start.12 = (bf16[512,128]{1,0:T(8,128)(2,1)S(1)}, bf16[512,128]{1,0:T(8,128)(2,1)S(1)}, u32[]{:S(2)}, u32[]{:S(2)}) collective-permute-start(bf16[512,128]{1,0:T(8,128)(2,1)S(1)} %collective-permute-done.7.refs_2_), channel_id=1, source_target_pairs={{0,16},{8,24},{16,0},{24,8},{1,17},{9,25},{17,1},{25,9},{2,18},{10... | collective-permute-start | bytes 393224 | tf_op jit(solution)/shard_map/ppermute | solution.py:240
  19.8 8.3 %collective-permute-start.3 = (bf16[512,128]{1,0:T(8,128)(2,1)S(1)}, bf16[512,128]{1,0:T(8,128)(2,1)S(1)}, u32[]{:S(2)}, u32[]{:S(2)}) collective-permute-start(bf16[512,128]{1,0:T(8,128)(2,1)S(1)} %collective-permute-done.2.refs_1_), channel_id=1, source_target_pairs={{0,4},{4,0},{1,5},{5,1},{2,6},{6,2},{3,7},{7,3},{8,12},{12,8},{9,1... | collective-permute-start | bytes 393224 | tf_op jit(solution)/shard_map/ppermute | solution.py:240
  22.0 10.9 %collective-permute-start.9 = (bf16[2048,128]{1,0:T(8,128)(2,1)S(1)}, bf16[2048,128]{1,0:T(8,128)(2,1)S(1)}, u32[]{:S(2)}, u32[]{:S(2)}) collective-permute-start(bf16[2048,128]{1,0:T(8,128)(2,1)S(1)} %pack.4.refs_2_.refs_4_), channel_id=1, source_target_pairs={{0,8},{8,0},{16,24},{24,16},{1,9},{9,1},{17,25},{25,17},{2,10},{10... | collective-permute-start | bytes 1572872 | tf_op jit(solution)/shard_map/ppermute | solution.py:240
  25.6 5.1 %collective-permute-start.14 = (bf16[512,128]{1,0:T(8,128)(2,1)S(1)}, bf16[512,128]{1,0:T(8,128)(2,1)S(1)}, u32[]{:S(2)}, u32[]{:S(2)}) collective-permute-start(bf16[512,128]{1,0:T(8,128)(2,1)S(1)} %collective-permute-done.8.refs_3_), channel_id=1, source_target_pairs={{0,16},{8,24},{16,0},{24,8},{1,17},{9,25},{17,1},{25,9},{2,18},{10... | collective-permute-start | bytes 393224 | tf_op jit(solution)/shard_map/ppermute | solution.py:240
  26.8 6.0 %collective-permute-start.13 = (bf16[1536,128]{1,0:T(8,128)(2,1)S(1)}, bf16[1536,128]{1,0:T(8,128)(2,1)S(1)}, u32[]{:S(2)}, u32[]{:S(2)}) collective-permute-start(bf16[1536,128]{1,0:T(8,128)(2,1)S(1)} %pack.5.refs_4_.refs_6_), channel_id=1, source_target_pairs={{0,8},{8,0},{16,24},{24,16},{1,9},{9,1},{17,25},{25,17},{2,10},{10... | collective-permute-start | bytes 1179656 | tf_op jit(solution)/shard_map/ppermute | solution.py:240
  27.4 0.8 %copy-start.3 = (bf16[512,512]{1,0:T(8,128)(2,1)}, bf16[512,512]{1,0:T(8,128)(2,1)S(1)}, u32[]{:S(2)}) copy-start(bf16[512,512]{1,0:T(8,128)(2,1)S(1)} %arrange.1.refs_1_) | copy-start | bytes 1572868
  30.7 2.2 %collective-permute-start.15 = (bf16[512,128]{1,0:T(8,128)(2,1)S(1)}, bf16[512,128]{1,0:T(8,128)(2,1)S(1)}, u32[]{:S(2)}, u32[]{:S(2)}) collective-permute-start(bf16[512,128]{1,0:T(8,128)(2,1)S(1)} %collective-permute-done.14.refs_6_.refs_8_), channel_id=1, source_target_pairs={{0,8},{8,0},{16,24},{24,16},{1,9},{9,1},{17,25},{25,17},{2,10},{10... | collective-permute-start | bytes 393224 | tf_op jit(solution)/shard_map/ppermute | solution.py:240
  31.6 0.7 %copy-start.7 = (f32[512]{0:T(512)S(1)}, f32[512]{0:T(512)}, u32[]{:S(2)}) copy-start(f32[512]{0:T(512)} %param.17) | copy-start | bytes 6148
  31.6 0.7 %copy-start.9 = (f32[128]{0:T(128)S(1)}, f32[128]{0:T(128)}, u32[]{:S(2)}) copy-start(f32[128]{0:T(128)} %param.19) | copy-start | bytes 1540
  31.7 0.7 copy-start.10
  32.3 0.7 copy-start.8
  32.3 5.2 %collective-permute-start.5 = (bf16[512,128]{1,0:T(8,128)(2,1)S(1)}, bf16[512,128]{1,0:T(8,128)(2,1)S(1)}, u32[]{:S(2)}, u32[]{:S(2)}) collective-permute-start(bf16[512,128]{1,0:T(8,128)(2,1)S(1)} %collective-permute-done.4.refs_2_), channel_id=1, source_target_pairs={{0,4},{4,0},{1,5},{5,1},{2,6},{6,2},{3,7},{7,3},{8,12},{12,8},{9,1... | collective-permute-start | bytes 393224 | tf_op jit(solution)/shard_map/ppermute | solution.py:240
  33.1 1.1 %copy-start.4 = (bf16[512,512]{1,0:T(8,128)(2,1)S(1)}, bf16[512,512]{1,0:T(8,128)(2,1)}, u32[]{:S(2)}) copy-start(bf16[512,512]{1,0:T(8,128)(2,1)} %copy-done.3) | copy-start | bytes 1572868
  37.1 24.9 %copy-start = (bf16[16,128,128]{2,1,0:T(8,128)(2,1)S(1)}, bf16[16,128,128]{2,1,0:T(8,128)(2,1)}, u32[]{:S(2)}) copy-start(bf16[16,128,128]{2,1,0:T(8,128)(2,1)} %refs_1_.3) | copy-start | bytes 1572868
  37.5 24.5 %copy-start.2 = (bf16[512,128]{1,0:T(8,128)(2,1)S(1)}, bf16[512,128]{1,0:T(8,128)(2,1)}, u32[]{:S(2)}) copy-start(bf16[512,128]{1,0:T(8,128)(2,1)} %refs_8_.3) | copy-start | bytes 393220
  40.6 21.4 %copy-start.1 = (bf16[128,512]{1,0:T(8,128)(2,1)S(1)}, bf16[128,512]{1,0:T(8,128)(2,1)}, u32[]{:S(2)}) copy-start(bf16[128,512]{1,0:T(8,128)(2,1)} %refs_7_.3) | copy-start | bytes 393220
  40.7 24.0 %collective-permute-start.16 = (bf16[16,64,128]{2,1,0:T(8,128)(2,1)S(1)}, bf16[16,64,128]{2,1,0:T(8,128)(2,1)S(1)}, u32[]{:S(2)}, u32[]{:S(2)}) collective-permute-start(bf16[16,64,128]{2,1,0:T(8,128)(2,1)S(1)} %get-tuple-element.19), channel_id=1, source_target_pairs={{0,2},{1,3},{2,0},{3,1},{4,6},{5,7},{6,4},{7,5},{8,10},{9,11},{10,... | collective-permute-start | bytes 786440 | tf_op jit(solution)/shard_map/ppermute | solution.py:240
  41.4 8.5 %collective-permute-start.17 = (bf16[32,16,128]{2,1,0:T(8,128)(2,1)S(1)}, bf16[32,16,128]{2,1,0:T(8,128)(2,1)S(1)}, u32[]{:S(2)}, u32[]{:S(2)}) collective-permute-start(bf16[32,16,128]{2,1,0:T(8,128)(2,1)S(1)} %get-tuple-element.20), channel_id=1, source_target_pairs={{0,0},{1,1},{2,2},{3,3},{4,16},{5,17},{6,18},{7,19},{8,8},{9,9},{1... | collective-permute-start | bytes 393224 | tf_op jit(solution)/shard_map/ppermute | solution.py:361
  44.8 8.0 %collective-permute-start.18 = (bf16[32,16,128]{2,1,0:T(8,128)(2,1)S(1)}, bf16[32,16,128]{2,1,0:T(8,128)(2,1)S(1)}, u32[]{:S(2)}, u32[]{:S(2)}) collective-permute-start(bf16[32,16,128]{2,1,0:T(8,128)(2,1)S(1)} %get-tuple-element.21), channel_id=1, source_target_pairs={{0,8},{1,9},{2,10},{3,11},{4,24},{5,25},{6,26},{7,27},{8,0},{9,1},... | collective-permute-start | bytes 393224 | tf_op jit(solution)/shard_map/ppermute | solution.py:361
  47.0 12.2 %collective-permute-start.19 = (bf16[32,16,128]{2,1,0:T(8,128)(2,1)S(1)}, bf16[32,16,128]{2,1,0:T(8,128)(2,1)S(1)}, u32[]{:S(2)}, u32[]{:S(2)}) collective-permute-start(bf16[32,16,128]{2,1,0:T(8,128)(2,1)S(1)} %get-tuple-element.22), channel_id=1, source_target_pairs={{0,1},{1,0},{2,3},{3,2},{4,17},{5,16},{6,19},{7,18},{8,9},{9,8},{1... | collective-permute-start | bytes 393224 | tf_op jit(solution)/shard_map/ppermute | solution.py:361
  49.8 12.2 %collective-permute-start.20 = (bf16[32,16,128]{2,1,0:T(8,128)(2,1)S(1)}, bf16[32,16,128]{2,1,0:T(8,128)(2,1)S(1)}, u32[]{:S(2)}, u32[]{:S(2)}) collective-permute-start(bf16[32,16,128]{2,1,0:T(8,128)(2,1)S(1)} %get-tuple-element.23), channel_id=1, source_target_pairs={{0,9},{1,8},{2,11},{3,10},{4,25},{5,24},{6,27},{7,26},{8,1},{9,0},... | collective-permute-start | bytes 393224 | tf_op jit(solution)/shard_map/ppermute | solution.py:361

commit v3 on v2

--- a/solution.py
+++ b/solution.py
@@ -17,13 +17,13 @@
     sources = len(right_places[0])
     refs = list(refs)
     place_ref = refs.pop(0)
-    left_refs = [refs.pop(0) for _ in range(3 * blocks if last else 1)]
+    left_refs = [refs.pop(0) for _ in range(3 * blocks)]
     data_refs = [refs.pop(0) for _ in range(data_count)]
     bias_ref, weight_ref = refs.pop(0), refs.pop(0)
-    first_ref = refs.pop(0) if last else None
+    first_ref = refs.pop(0)
     update_ref = refs.pop() if last else refs[0]
     outer_ref = refs.pop()
-    lhs_ref = refs.pop() if last else left_refs[0]
+    lhs_ref = refs.pop()
     out_refs = refs
     row_count, _, lanes = outer_ref.shape
     low = groups // 2
@@ -33,7 +33,7 @@
     half = lanes // 2
     pair_channels = weight_ref.shape[0] // 2
     lane_low = lax.broadcasted_iota(jnp.int32, (pair_channels, lanes), 1) < half
-    for block in range(blocks if last else 0):
+    for block in range(blocks):
         for dz in range(groups):
             index = 3 * block + max(0, dz - low + 1)
             begin = dz * share_rows if dz < low else 0
@@ -86,13 +86,29 @@
         update_ref[pl.ds(place_ref[2] * share, share)] = first_ref[...]
         core, z_low, z_high = place_ref[0], place_ref[1], place_ref[3]
         out_refs[0][...] = update_ref[pl.ds(z_high * run, run)]
-        out_refs[1][...] = update_ref[pl.ds((1 - z_high) * run, run)]
+        quarter = half // 2
+
+        def mirrored(slot, dz, flip):
+            begin = (core ^ flip) * quarter + (z_low ^ dz) * run
+            out_refs[1 + slot][...] = update_ref[:, pl.ds(pl.multiple_of(begin, run), run), :]
+
+        def direct(slot, part):
+            for index in range(low):
+                begin = part * quarter + index * run
+                out_refs[1 + slot][index * run : (index + 1) * run] = update_ref[
+                    pl.ds((1 - z_high) * run, run), begin : begin + run, :
+                ]
+
+        for side in range(2):
+
+            @pl.when(core == side)
+            def _():
+                for dz in range(2):
+                    mirrored(2 * dz + side, dz, 0)
+                    direct(2 * dz + 1 - side, dz)
+
         for dz in range(low):
-            for flip in range(2):
-                begin = (core ^ flip) * (half // 2) + (z_low ^ dz) * run
-                out_refs[2 + 2 * dz + flip][...] = update_ref[
-                    :, pl.ds(pl.multiple_of(begin, run), run), :
-                ]
+            mirrored(4 + dz, dz, 1)
 
 
 def pack_kernel(*refs):
@@ -113,49 +129,47 @@
     )(*values)
 
 
-def arrange_kernel(*refs):
-    out_ref = refs[-1]
-    rows, lanes = out_ref.shape[0], refs[0].shape[1]
-    index = 0
-    for ref in refs[:-1]:
-        for begin in range(0, ref.shape[0], rows):
-            out_ref[:, index * lanes : (index + 1) * lanes] = ref[begin : begin + rows]
-            index += 1
-
-
-def arrange(lefts, groups):
-    lanes = lefts[0].shape[1]
-    rows = sum(value.shape[0] for value in lefts) // groups
+def arrived_kernel(first_ref, second_ref, out_ref):
+    rows = out_ref.shape[0] // 2
+    out_ref[:rows] = first_ref[:rows]
+    out_ref[rows:] = second_ref[:rows]
+
+
+def arrived(first, second, flops):
     return pl.pallas_call(
-        arrange_kernel,
-        out_shape=jax.ShapeDtypeStruct((rows, groups * lanes), lefts[0].dtype),
-        in_specs=[pl.BlockSpec(memory_space=pltpu.VMEM)] * len(lefts),
+        arrived_kernel,
+        out_shape=jax.ShapeDtypeStruct((32, first.shape[1]), first.dtype),
+        in_specs=[pl.BlockSpec(memory_space=pltpu.VMEM)] * 2,
         out_specs=pl.BlockSpec(memory_space=pltpu.VMEM),
         compiler_params=pltpu.CompilerParams(vmem_limit_bytes=4 * 1024 * 1024),
         cost_estimate=pl.CostEstimate(
-            flops=rows * groups * lanes * 8 * lanes * groups * 4,
-            bytes_accessed=4 * rows * groups * lanes,
-            transcendentals=0,
+            flops=flops, bytes_accessed=4 * first.size, transcendentals=0
         ),
-        name="arrange",
-    )(*lefts)
-
-
-def finish_kernel(low, other, *refs):
-    place_ref, pair_ref, direct_ref = refs[:3]
-    mirror_refs = refs[3 : 3 + 2 * low]
-    up_ref, down_ref, vector_ref, swap_ref = refs[3 + 2 * low : 7 + 2 * low]
+        name="arrived",
+    )(first, second)
+
+
+def finish_kernel(low, *refs):
+    place_ref, pair_ref, own_ref = refs[:3]
+    slot_refs, mirror_refs = refs[3:7], refs[7 : 7 + low]
+    up_ref, down_ref, vector_ref, swap_ref = refs[7 + low : 11 + low]
     out_ref, done_ref, sems = refs[-3:]
     run, columns, pair_channels = pair_ref.shape
     half = columns // 2
-    core, z_low, part = place_ref[0], place_ref[1], place_ref[3] ^ other
+    core, z_low, z_high = place_ref[0], place_ref[1], place_ref[3]
     cells = run * run
     gain = vector_ref[:, :pair_channels]
     down_bias = vector_ref[:, pair_channels : 2 * pair_channels]
     up_bias = vector_ref[:, 2 * pair_channels :]
     ones = jnp.full((2 * pair_channels, pair_channels), 1.0 / pair_channels, jnp.bfloat16)
+
+    def chosen(first, second, rows):
+        return jnp.where(core == 0, slot_refs[first][rows], slot_refs[second][rows])
+
     copies = []
-    for dz in range(low):
+    for chunk in range(2 * low):
+        other, dz = divmod(chunk, low)
+        part = z_high ^ other
         middles = []
         begins = []
         for flip in range(2):
@@ -164,13 +178,22 @@
             begin = (core ^ flip) * half + (part * low + (z_low ^ dz)) * run
             begin = pl.multiple_of(begin, run)
             begins.append(begin)
-            piece = mirror_refs[2 * dz + flip][pl.ds(part * run, run)]
+            rows = pl.ds(part * run, run)
+            if flip == 0:
+                piece = chosen(2 * dz, 2 * dz + 1, rows)
+            else:
+                piece = mirror_refs[dz][rows]
             mirrored = jnp.dot(
                 swap_ref[...],
                 piece.reshape(cells, pair_channels),
                 preferred_element_type=jnp.float32,
             )
-            direct = direct_ref[:, pl.ds(local, run), :].reshape(cells, pair_channels)
+            if other == 0:
+                direct = own_ref[:, pl.ds(local, run), :]
+            else:
+                rows = pl.ds((z_low ^ dz) * run, run)
+                direct = chosen(1, 2, rows) if flip == 0 else chosen(3, 0, rows)
+            direct = direct.reshape(cells, pair_channels)
             residual = pair_ref[:, pl.ds(begin, run), :].reshape(cells, pair_channels)
             middles.append(
                 (
@@ -195,7 +218,7 @@
         result = jnp.dot(hidden, down_ref[...], preferred_element_type=jnp.float32)
         result = (values + result + down_bias).astype(jnp.bfloat16)
         for flip in range(2):
-            index = 2 * dz + flip
+            index = 2 * chunk + flip
             done_ref[index] = result[flip * cells : (flip + 1) * cells].reshape(
                 run, run, pair_channels
             )
@@ -273,7 +296,7 @@
     for dy in range(1, cols):
         shares[dy - 1] += [swap(value, "col", cols, dy) for value in fars]
     far_shares = [pair[1] for pair in shares]
-    first_lhs = arrange([lefts[0]] + fars, groups)
+    far_tile = arrived(*fars, 32 * (share_rows * groups * group_len) * groups * group_len // 4)
     data = []
     right_places = {dz: [] for dz in range(groups)}
     order = (0, 1, low + 1, low)
@@ -293,7 +316,7 @@
                 right_places[dz].append((len(data), index * source_rows))
             data.append(value)
         if count < len(order):
-            exchanged = swap(after(values[-1], first_lhs, far_shares), "row", rows, 1)
+            exchanged = swap(after(values[-1], far_tile, far_shares), "row", rows, 1)
             for value in (values[-1], exchanged):
                 right_places[low].append((len(data), 0))
                 data.append(value)
@@ -308,7 +331,7 @@
     share = share_rows // channels
 
     def update_call(last, left_values, extra, out_shape, out_specs, scratch):
-        blocks = max(len(left_values) // 3, 1)
+        blocks = len(left_values) // 3
         row_count = share * blocks
         outer_size = row_count * channels * channels * half
         places = (blocks, len(data), right_places, share_rows, source_rows, group_len, run)
@@ -317,11 +340,11 @@
             out_shape=out_shape,
             in_specs=[smem] + [vmem] * (len(left_values) + len(data) + 2 + len(extra)),
             out_specs=out_specs,
-            scratch_shapes=scratch[:-1]
-            + [
+            scratch_shapes=[
+                pltpu.VMEM((row_count * channels, groups * group_len), bf16),
                 pltpu.VMEM((row_count, channels * channels // 2, 2 * half), bf16),
             ]
-            + scratch[-1:],
+            + scratch,
             compiler_params=params,
             cost_estimate=pl.CostEstimate(
                 flops=2 * outer_size * (groups * group_len + 2 * pair_channels),
@@ -332,62 +355,51 @@
         )(place, *left_values, *data, bias, weight, *extra)
 
     first = update_call(
-        False, [first_lhs], [], jax.ShapeDtypeStruct((share, half, pair_channels), bf16), vmem, []
+        False, [lefts[0]] + fars, [far_tile], jax.ShapeDtypeStruct((share, half, pair_channels), bf16), vmem, []
     )
     outs = update_call(
         True,
         last_lefts,
         [first],
-        [jax.ShapeDtypeStruct((run, half, pair_channels), bf16)] * 2
-        + [jax.ShapeDtypeStruct((2 * run, run, pair_channels), bf16)] * (2 * low),
-        [vmem] * (2 + 2 * low),
-        [
-            pltpu.VMEM(((2 * run - share) * channels, groups * group_len), bf16),
-            pltpu.VMEM((2 * run, half, pair_channels), bf16),
+        [jax.ShapeDtypeStruct((run, half, pair_channels), bf16)]
+        + [jax.ShapeDtypeStruct((2 * run, run, pair_channels), bf16)] * (4 + low),
+        [vmem] * (5 + low),
+        [pltpu.VMEM((2 * run, half, pair_channels), bf16)],
+    )
+
+    def mirrored_place(r, c, q, dz, flip):
+        return ((2 * c + (r % 2 ^ flip)) * cols + r // 2) * groups + (q ^ dz)
+
+    def exchange(slot):
+        pairs = []
+        for r in range(rows):
+            for c in range(cols):
+                for q in range(groups):
+                    source = (r * cols + c) * groups + q
+                    if slot >= 4:
+                        target = mirrored_place(r, c, q, slot - 4, 1)
+                    elif r % 2 == slot % 2:
+                        target = mirrored_place(r, c, q, slot // 2, 0)
+                    else:
+                        target = (r * cols + c) * groups + (q ^ low)
+                    pairs.append((source, target))
+        return lax.ppermute(outs[1 + slot], axes, pairs)
+
+    operands = [place, pair_rep, outs[0]]
+    operands += [exchange(slot) for slot in range(4 + low)]
+    operands += [up_weight, down_weight, vectors, swap_cells]
+    result = pl.pallas_call(
+        functools.partial(finish_kernel, low),
+        out_shape=jax.ShapeDtypeStruct(pair_rep.shape, bf16),
+        in_specs=[smem] + [vmem] * (len(operands) - 1),
+        out_specs=pl.BlockSpec(memory_space=pl.ANY),
+        scratch_shapes=[
+            pltpu.VMEM((4 * low, run, run, pair_channels), bf16),
+            pltpu.SemaphoreType.DMA((4 * low,)),
         ],
-    )
-
-    mirrors = []
-    for dz in range(low):
-        for flip in range(2):
-            pairs = []
-            for r in range(rows):
-                for c in range(cols):
-                    for q in range(groups):
-                        source = (r * cols + c) * groups + q
-                        target = 2 * c + (r % 2 ^ flip)
-                        target = (target * cols + r // 2) * groups + (q ^ dz)
-                        pairs.append((source, target))
-            mirrors.append(lax.ppermute(outs[2 + 2 * dz + flip], axes, pairs))
-    update_other = swap(outs[1], "seq", groups, low)
-
-    anywhere = pl.BlockSpec(memory_space=pl.ANY)
-    result = None
-    for other in range(2):
-        operands = [
-            place,
-            pair_rep,
-            update_other if other else outs[0],
-            *mirrors,
-            up_weight,
-            down_weight,
-            vectors,
-            swap_cells,
-        ]
-        extra = [] if result is None else [result]
-        result = pl.pallas_call(
-            functools.partial(finish_kernel, low, other),
-            out_shape=jax.ShapeDtypeStruct(pair_rep.shape, bf16),
-            in_specs=[smem] + [vmem] * (len(operands) - 1) + [anywhere] * len(extra),
-            out_specs=anywhere,
-            scratch_shapes=[
-                pltpu.VMEM((2 * low, run, run, pair_channels), bf16),
-                pltpu.SemaphoreType.DMA((2 * low,)),
-            ],
-            input_output_aliases={len(operands): 0} if extra else {},
-            compiler_params=params,
-            name="finish",
-        )(*operands, *extra)
+        compiler_params=params,
+        name="finish",
+    )(*operands)
     return result
 
 

time: 67.6 us -> 64.6 us (0.956); the launches traced: 67.3 us -> 63.6 us
  starting transfers between devices: 27.1 us -> 32.8 us
  waiting for transfers between devices: 22.5 us -> 16.9 us
  local copies, waits for them, and re-layouts: 5.2 us -> 2.76 us
  Pallas kernels: 11.5 us -> 10.2 us
    ppermute x4 -> x6, waiting for transfers between devices: 12.1 us -> 6.31 us  [exchange(): return lax.ppermute(outs[1 + slot], axes, pairs)]
    ppermute x4 -> x6, starting transfers between devices: 8.35 us -> 13.6 us  [exchange(): return lax.ppermute(outs[1 + slot], axes, pairs)]
    unnamed x24 -> x20, local copies, waits for them, and re-layouts: 3.67 us -> 1.23 us
    pallas_call x3 -> x2, Pallas kernels: 5.4 us -> 4 us  [the longest x1 4 us: on_device(): pl.pallas_call(functools.partial(finish_kernel, low), out_shape=jax.Shape...]
    ppermute x17 -> x16, starting transfers between devices: 18.8 us -> 19.2 us  [swap(): return lax.ppermute(value, name, [(i, i ^ flip) for i in range(size)])]
    ppermute x17 -> x16, waiting for transfers between devices: 10.4 us -> 10.6 us  [swap(): return lax.ppermute(value, name, [(i, i ^ flip) for i in range(size)])]
  transfers between devices with their start and end apart: 21 -> 22, of which waited for: 7 -> 7; matrix products, arithmetic and copies ran while one was open for 3% -> 3% of each run, Pallas kernels for 9% -> 5%
where the time goes in v3:
time: 64.6 us; the launch traced here: 63.6 us
  starting transfers between devices  32.8 us (51%)
  waiting for transfers between devices  16.9 us (26%)
  Pallas kernels  10.2 us (16%)
  local copies, waits for them, and re-layouts  2.76 us (4%)
  other arithmetic  0.66 us (1%)
    ppermute x16, starting transfers between devices, swap(): return lax.ppermute(value, name, [(i, i ^ flip) for i in range(size)])  19.2 us
    ppermute x6, starting transfers between devices, exchange(): return lax.ppermute(outs[1 + slot], axes, pairs)  13.6 us
    ppermute x16, waiting for transfers between devices, swap(): return lax.ppermute(value, name, [(i, i ^ flip) for i in range(size)])  10.6 us
    ppermute x6, waiting for transfers between devices, exchange(): return lax.ppermute(outs[1 + slot], axes, pairs)  6.31 us
    pallas_call x2, Pallas kernels, update_call(): pl.pallas_call(functools.partial(update_kernel, places, cols, low, last,...  6.09 us
    pallas_call x1, Pallas kernels, on_device(): pl.pallas_call(functools.partial(finish_kernel, low), out_shape=jax.Shape...  4 us
  transfers between devices with their start and end apart: 22, of which 7 were waited for; matrix products, arithmetic and copies ran while one was open for 3% of the time, Pallas kernels for 5%

profile of v3, /device:TPU:3, one launch (start us, length us, event | category | flops | bytes accessed | tf_op | source)
XLA Modules:
  0.0 63.6 jit_solution(5281450420803559246)
XLA Ops:
  0.0 1.1 %copy.18 = bf16[128,8,128]{0,2,1:T(8,128)(2,1)S(1)} copy(bf16[128,8,128]{2,1,0:T(8,128)(2,1)} %param.11) | data formatting | bytes 524288 | tf_op args[1]
  1.2 0.2 copy.19
  1.4 0.1 reshape.55
  1.5 0.0 copy-start.3
  1.5 0.1 copy.20
  1.7 0.1 collective-permute-start.10
  1.7 1.5 %collective-permute-start.6 = (bf16[512,128]{1,0:T(8,128)(2,1)S(1)}, bf16[512,128]{1,0:T(8,128)(2,1)S(1)}, u32[]{:S(2)}, u32[]{:S(2)}) collective-permute-start(bf16[512,128]{1,0:T(8,128)(2,1)S(1)} %bitcast.46), channel_id=1, source_target_pairs={{0,1},{1,0},{2,3},{3,2},{4,5},{5,4},{6,7},{7,6},{8,9},{9,8},{10,11... | collective-permute-start | bytes 393224 | tf_op jit(solution)/shard_map/ppermute | solution.py:263
  3.3 0.3 copy.17
  3.7 0.6 collective-permute-start
  4.3 0.1 copy.21
  4.4 3.0 %collective-permute-start.7 = (bf16[512,128]{1,0:T(8,128)(2,1)S(1)}, bf16[512,128]{1,0:T(8,128)(2,1)S(1)}, u32[]{:S(2)}, u32[]{:S(2)}) collective-permute-start(bf16[512,128]{1,0:T(8,128)(2,1)S(1)} %bitcast.54), channel_id=1, source_target_pairs={{0,3},{1,2},{2,1},{3,0},{4,7},{5,6},{6,5},{7,4},{8,11},{9,10},{10,... | collective-permute-start | bytes 393224 | tf_op jit(solution)/shard_map/ppermute | solution.py:263
  7.4 1.2 %collective-permute-start.11 = (bf16[512,128]{1,0:T(8,128)(2,1)S(1)}, bf16[512,128]{1,0:T(8,128)(2,1)S(1)}, u32[]{:S(2)}, u32[]{:S(2)}) collective-permute-start(bf16[512,128]{1,0:T(8,128)(2,1)S(1)} %collective-permute-done.6.refs_1_), channel_id=1, source_target_pairs={{0,16},{8,24},{16,0},{24,8},{1,17},{9,25},{17,1},{25,9},{2,18},{10... | collective-permute-start | bytes 393224 | tf_op jit(solution)/shard_map/ppermute | solution.py:263
  8.6 1.0 %collective-permute-start.2 = (bf16[512,128]{1,0:T(8,128)(2,1)S(1)}, bf16[512,128]{1,0:T(8,128)(2,1)S(1)}, u32[]{:S(2)}, u32[]{:S(2)}) collective-permute-start(bf16[512,128]{1,0:T(8,128)(2,1)S(1)} %get-tuple-element.28.refs_0_), channel_id=1, source_target_pairs={{0,2},{1,3},{2,0},{3,1},{4,6},{5,7},{6,4},{7,5},{8,10},{9,11},{10,... | collective-permute-start | bytes 393224 | tf_op jit(solution)/shard_map/ppermute | solution.py:263
  9.6 1.3 %collective-permute-start.1 = (bf16[1024,128]{1,0:T(8,128)(2,1)S(1)}, bf16[1024,128]{1,0:T(8,128)(2,1)S(1)}, u32[]{:S(2)}, u32[]{:S(2)}) collective-permute-start(bf16[1024,128]{1,0:T(8,128)(2,1)S(1)} %pack.3.refs_1_), channel_id=1, source_target_pairs={{0,4},{4,0},{1,5},{5,1},{2,6},{6,2},{3,7},{7,3},{8,12},{12,8},{9,1... | collective-permute-start | bytes 786440 | tf_op jit(solution)/shard_map/ppermute | solution.py:263
  10.9 0.2 constant_dynamic-slice_fusion.3
  11.1 2.9 %collective-permute-done.7.refs_2_ = bf16[512,128]{1,0:T(8,128)(2,1)S(1)} collective-permute-done((bf16[512,128]{1,0:T(8,128)(2,1)S(1)}, bf16[512,128]{1,0:T(8,128)(2,1)S(1)}, u32[]{:S(2)}, u32[]{:S(2)}) %collective-permute-start.7) | collective-permute-done | bytes 131104 | tf_op jit(solution)/shard_map/ppermute | solution.py:263
  14.1 1.2 %collective-permute-start.12 = (bf16[512,128]{1,0:T(8,128)(2,1)S(1)}, bf16[512,128]{1,0:T(8,128)(2,1)S(1)}, u32[]{:S(2)}, u32[]{:S(2)}) collective-permute-start(bf16[512,128]{1,0:T(8,128)(2,1)S(1)} %collective-permute-done.7.refs_2_), channel_id=1, source_target_pairs={{0,16},{8,24},{16,0},{24,8},{1,17},{9,25},{17,1},{25,9},{2,18},{10... | collective-permute-start | bytes 393224 | tf_op jit(solution)/shard_map/ppermute | solution.py:263
  15.3 0.1 copy_bitcast_fusion.1
  15.4 0.7 %collective-permute-start.4 = (bf16[512,128]{1,0:T(8,128)(2,1)S(1)}, bf16[512,128]{1,0:T(8,128)(2,1)S(1)}, u32[]{:S(2)}, u32[]{:S(2)}) collective-permute-start(bf16[512,128]{1,0:T(8,128)(2,1)S(1)} %collective-permute-done.refs_1_), channel_id=1, source_target_pairs={{0,2},{1,3},{2,0},{3,1},{4,6},{5,7},{6,4},{7,5},{8,10},{9,11},{10,... | collective-permute-start | bytes 393224 | tf_op jit(solution)/shard_map/ppermute | solution.py:263
  16.1 3.3 %collective-permute-done.2.first_ref.refs_2_ = bf16[512,128]{1,0:T(8,128)(2,1)S(1)} collective-permute-done((bf16[512,128]{1,0:T(8,128)(2,1)S(1)}, bf16[512,128]{1,0:T(8,128)(2,1)S(1)}, u32[]{:S(2)}, u32[]{:S(2)}) %collective-permute-start.2) | collective-permute-done | bytes 131104 | tf_op jit(solution)/shard_map/ppermute | solution.py:263
  19.4 1.2 %collective-permute-start.3 = (bf16[512,128]{1,0:T(8,128)(2,1)S(1)}, bf16[512,128]{1,0:T(8,128)(2,1)S(1)}, u32[]{:S(2)}, u32[]{:S(2)}) collective-permute-start(bf16[512,128]{1,0:T(8,128)(2,1)S(1)} %collective-permute-done.2.first_ref.refs_2_), channel_id=1, source_target_pairs={{0,4},{4,0},{1,5},{5,1},{2,6},{6,2},{3,7},{7,3},{8,12},{12,8},{9,1... | collective-permute-start | bytes 393224 | tf_op jit(solution)/shard_map/ppermute | solution.py:263
  20.7 3.8 %collective-permute-start.9 = (bf16[2048,128]{1,0:T(8,128)(2,1)S(1)}, bf16[2048,128]{1,0:T(8,128)(2,1)S(1)}, u32[]{:S(2)}, u32[]{:S(2)}) collective-permute-start(bf16[2048,128]{1,0:T(8,128)(2,1)S(1)} %pack.4.refs_4_), channel_id=1, source_target_pairs={{0,8},{8,0},{16,24},{24,16},{1,9},{9,1},{17,25},{25,17},{2,10},{10... | collective-permute-start | bytes 1572872 | tf_op jit(solution)/shard_map/ppermute | solution.py:263
  24.5 1.2 %collective-permute-start.14 = (bf16[512,128]{1,0:T(8,128)(2,1)S(1)}, bf16[512,128]{1,0:T(8,128)(2,1)S(1)}, u32[]{:S(2)}, u32[]{:S(2)}) collective-permute-start(bf16[512,128]{1,0:T(8,128)(2,1)S(1)} %collective-permute-done.8.refs_3_), channel_id=1, source_target_pairs={{0,16},{8,24},{16,0},{24,8},{1,17},{9,25},{17,1},{25,9},{2,18},{10... | collective-permute-start | bytes 393224 | tf_op jit(solution)/shard_map/ppermute | solution.py:263
  25.8 0.4 collective-permute-start.13
  26.2 0.1 copy_bitcast_fusion.3
  26.3 3.2 %collective-permute-done.14.refs_8_ = bf16[512,128]{1,0:T(8,128)(2,1)S(1)} collective-permute-done((bf16[512,128]{1,0:T(8,128)(2,1)S(1)}, bf16[512,128]{1,0:T(8,128)(2,1)S(1)}, u32[]{:S(2)}, u32[]{:S(2)}) %collective-permute-start.14) | collective-permute-done | bytes 131104 | tf_op jit(solution)/shard_map/ppermute | solution.py:263
  29.5 0.9 %collective-permute-start.15 = (bf16[512,128]{1,0:T(8,128)(2,1)S(1)}, bf16[512,128]{1,0:T(8,128)(2,1)S(1)}, u32[]{:S(2)}, u32[]{:S(2)}) collective-permute-start(bf16[512,128]{1,0:T(8,128)(2,1)S(1)} %collective-permute-done.14.refs_8_), channel_id=1, source_target_pairs={{0,8},{8,0},{16,24},{24,16},{1,9},{9,1},{17,25},{25,17},{2,10},{10... | collective-permute-start | bytes 393224 | tf_op jit(solution)/shard_map/ppermute | solution.py:263
  30.4 0.5 pad_maximum_fusion
  30.9 0.1 copy.27.refs_11_
  31.1 0.0 copy-start.6
  31.1 0.1 pad_add_fusion.refs_0_
  31.2 1.0 %collective-permute-start.5 = (bf16[512,128]{1,0:T(8,128)(2,1)S(1)}, bf16[512,128]{1,0:T(8,128)(2,1)S(1)}, u32[]{:S(2)}, u32[]{:S(2)}) collective-permute-start(bf16[512,128]{1,0:T(8,128)(2,1)S(1)} %collective-permute-done.4.second_ref.refs_3_), channel_id=1, source_target_pairs={{0,4},{4,0},{1,5},{5,1},{2,6},{6,2},{3,7},{7,3},{8,12},{12,8},{9,1... | collective-permute-start | bytes 393224 | tf_op jit(solution)/shard_map/ppermute | solution.py:263
  32.2 0.1 broadcast_in_dim.2.refs_10_
  32.3 3.0 %update_first.1.refs_12_ = bf16[16,64,128]{2,1,0:T(8,128)(2,1)S(1)} custom-call(s32[4]{0:T(128)S(1)} %pad_add_fusion.refs_0_, bf16[1024,128]{1,0:T(8,128)(2,1)S(1)} %pack.3.refs_1_, bf16[512,128]{1,0:T(8,128)(2,1)S(1)} %collective-permute-done.2.first_ref.refs_2_, bf16[512,128]{1,0:T(8,128)(2,1)S(1)} %collective-permute-done.4.second_ref.refs_3_, ...), custom_call_target="tpu_custom_call" | custom-call | flops 1610612736 | bytes 2097152 | tf_op jit(solution)/shard_map/update_first/pallas_call | solution.py:338
  35.3 0.0 copy-start
  35.3 1.0 %collective-permute-done.5.refs_3_ = bf16[512,128]{1,0:T(8,128)(2,1)S(1)} collective-permute-done((bf16[512,128]{1,0:T(8,128)(2,1)S(1)}, bf16[512,128]{1,0:T(8,128)(2,1)S(1)}, u32[]{:S(2)}, u32[]{:S(2)}) %collective-permute-start.5) | collective-permute-done | bytes 131104 | tf_op jit(solution)/shard_map/ppermute | solution.py:263
  36.3 3.1 %update_last.1 = (bf16[16,64,128]{2,1,0:T(8,128)(2,1)S(1)}, bf16[32,16,128]{2,1,0:T(8,128)(2,1)S(1)}, bf16[32,16,128]{2,1,0:T(8,128)(2,1)S(1)}, bf16[32,16,128]{...) custom-call(s32[4]{0:T(128)S(1)} %pad_add_fusion.refs_0_, ...), custom_call_target="tpu_custom_call" | custom-call | flops 1610612736 | bytes 2097152 | tf_op jit(solution)/shard_map/update_last/pallas_call | solution.py:338
  39.4 0.0 copy-start.1
  39.5 2.1 %collective-permute-start.16 = (bf16[32,16,128]{2,1,0:T(8,128)(2,1)S(1)}, bf16[32,16,128]{2,1,0:T(8,128)(2,1)S(1)}, u32[]{:S(2)}, u32[]{:S(2)}) collective-permute-start(bf16[32,16,128]{2,1,0:T(8,128)(2,1)S(1)} %get-tuple-element.21), channel_id=1, source_target_pairs={{0,0},{1,1},{2,2},{3,3},{4,16},{5,17},{6,18},{7,19},{8,10},{9,11},... | collective-permute-start | bytes 393224 | tf_op jit(solution)/shard_map/ppermute | solution.py:386
  41.6 4.1 %collective-permute-start.17 = (bf16[32,16,128]{2,1,0:T(8,128)(2,1)S(1)}, bf16[32,16,128]{2,1,0:T(8,128)(2,1)S(1)}, u32[]{:S(2)}, u32[]{:S(2)}) collective-permute-start(bf16[32,16,128]{2,1,0:T(8,128)(2,1)S(1)} %get-tuple-element.22), channel_id=1, source_target_pairs={{0,2},{1,3},{2,0},{3,1},{4,6},{5,7},{6,4},{7,5},{8,8},{9,9},{10,10... | collective-permute-start | bytes 393224 | tf_op jit(solution)/shard_map/ppermute | solution.py:386
  45.7 2.4 %collective-permute-start.18 = (bf16[32,16,128]{2,1,0:T(8,128)(2,1)S(1)}, bf16[32,16,128]{2,1,0:T(8,128)(2,1)S(1)}, u32[]{:S(2)}, u32[]{:S(2)}) collective-permute-start(bf16[32,16,128]{2,1,0:T(8,128)(2,1)S(1)} %get-tuple-element.23), channel_id=1, source_target_pairs={{0,1},{1,0},{2,3},{3,2},{4,17},{5,16},{6,19},{7,18},{8,10},{9,11},... | collective-permute-start | bytes 393224 | tf_op jit(solution)/shard_map/ppermute | solution.py:386
  48.1 3.2 %collective-permute-start.20 = (bf16[32,16,128]{2,1,0:T(8,128)(2,1)S(1)}, bf16[32,16,128]{2,1,0:T(8,128)(2,1)S(1)}, u32[]{:S(2)}, u32[]{:S(2)}) collective-permute-start(bf16[32,16,128]{2,1,0:T(8,128)(2,1)S(1)} %get-tuple-element.25), channel_id=1, source_target_pairs={{0,8},{1,9},{2,10},{3,11},{4,24},{5,25},{6,26},{7,27},{8,0},{9,1},... | collective-permute-start | bytes 393224 | tf_op jit(solution)/shard_map/ppermute | solution.py:386
  51.3 1.9 %collective-permute-start.21 = (bf16[32,16,128]{2,1,0:T(8,128)(2,1)S(1)}, bf16[32,16,128]{2,1,0:T(8,128)(2,1)S(1)}, u32[]{:S(2)}, u32[]{:S(2)}) collective-permute-start(bf16[32,16,128]{2,1,0:T(8,128)(2,1)S(1)} %get-tuple-element.26), channel_id=1, source_target_pairs={{0,9},{1,8},{2,11},{3,10},{4,25},{5,24},{6,27},{7,26},{8,1},{9,0},... | collective-permute-start | bytes 393224 | tf_op jit(solution)/shard_map/ppermute | solution.py:386
  53.2 0.1 fusion.refs_12_
  53.3 1.1 %collective-permute-done.18.refs_5_ = bf16[32,16,128]{2,1,0:T(8,128)(2,1)S(1)} collective-permute-done((bf16[32,16,128]{2,1,0:T(8,128)(2,1)S(1)}, bf16[32,16,128]{2,1,0:T(8,128)(2,1)S(1)}, u32[]{:S(2)}, u32[]{:S(2)}) %collective-permute-start.18) | collective-permute-done | bytes 131104 | tf_op jit(solution)/shard_map/ppermute | solution.py:386
  54.4 3.6 %collective-permute-done.19.refs_6_ = bf16[32,16,128]{2,1,0:T(8,128)(2,1)S(1)} collective-permute-done((bf16[32,16,128]{2,1,0:T(8,128)(2,1)S(1)}, bf16[32,16,128]{2,1,0:T(8,128)(2,1)S(1)}, u32[]{:S(2)}, u32[]{:S(2)}) %collective-permute-start.19) | collective-permute-done | bytes 131104 | tf_op jit(solution)/shard_map/ppermute | solution.py:386
  58.1 1.5 %collective-permute-done.21.refs_8_ = bf16[32,16,128]{2,1,0:T(8,128)(2,1)S(1)} collective-permute-done((bf16[32,16,128]{2,1,0:T(8,128)(2,1)S(1)}, bf16[32,16,128]{2,1,0:T(8,128)(2,1)S(1)}, u32[]{:S(2)}, u32[]{:S(2)}) %collective-permute-start.21) | collective-permute-done | bytes 131104 | tf_op jit(solution)/shard_map/ppermute | solution.py:386
  59.6 4.0 %finish.1 = bf16[16,128,128]{2,1,0:T(8,128)(2,1)} custom-call(s32[4]{0:T(128)S(1)} %pad_add_fusion.refs_0_, bf16[16,128,128]{2,1,0:T(8,128)(2,1)S(1)} %copy-done, bf16[16,64,128]{2,1,0:T(8,128)(2,1)S(1)} %get-tuple-element.20.refs_2_, bf16[32,16,128]{2,1,0:T(8,128)(2,1)S(1)} %collective-permute-done.16.refs_3_, ...), custom_call_target="tpu_custom_call" | custom-call | tf_op jit(solution)/shard_map/finish/pallas_call | solution.py:391
  (41 shorter events, 0.3 us)
Async XLA Ops:
  1.5 1.8 %copy-start.3 = (bf16[128,32,64]{0,2,1:T(8,128)(2,1)S(1)}, bf16[128,32,64]{0,2,1:T(8,128)(2,1)}, u32[]{:S(2)}) copy-start(bf16[128,32,64]{0,2,1:T(8,128)(2,1)} %param.10) | copy-start | bytes 1572868
  1.7 5.7 %collective-permute-start.10 = (bf16[512,128]{1,0:T(8,128)(2,1)S(1)}, bf16[512,128]{1,0:T(8,128)(2,1)S(1)}, u32[]{:S(2)}, u32[]{:S(2)}) collective-permute-start(bf16[512,128]{1,0:T(8,128)(2,1)S(1)} %bitcast.45), channel_id=1, source_target_pairs={{0,16},{8,24},{16,0},{24,8},{1,17},{9,25},{17,1},{25,9},{2,18},{10... | collective-permute-start | bytes 393224 | tf_op jit(solution)/shard_map/ppermute | solution.py:263
  1.7 5.7 %collective-permute-start.6 = (bf16[512,128]{1,0:T(8,128)(2,1)S(1)}, bf16[512,128]{1,0:T(8,128)(2,1)S(1)}, u32[]{:S(2)}, u32[]{:S(2)}) collective-permute-start(bf16[512,128]{1,0:T(8,128)(2,1)S(1)} %bitcast.46), channel_id=1, source_target_pairs={{0,1},{1,0},{2,3},{3,2},{4,5},{5,4},{6,7},{7,6},{8,9},{9,8},{10,11... | collective-permute-start | bytes 393224 | tf_op jit(solution)/shard_map/ppermute | solution.py:263
  3.7 6.0 %collective-permute-start = (bf16[512,128]{1,0:T(8,128)(2,1)S(1)}, bf16[512,128]{1,0:T(8,128)(2,1)S(1)}, u32[]{:S(2)}, u32[]{:S(2)}) collective-permute-start(bf16[512,128]{1,0:T(8,128)(2,1)S(1)} %get-tuple-element.27), channel_id=1, source_target_pairs={{0,1},{1,0},{2,3},{3,2},{4,5},{5,4},{6,7},{7,6},{8,9},{9,8},{10,11... | collective-permute-start | bytes 393224 | tf_op jit(solution)/shard_map/ppermute | solution.py:263
  4.4 9.7 %collective-permute-start.7 = (bf16[512,128]{1,0:T(8,128)(2,1)S(1)}, bf16[512,128]{1,0:T(8,128)(2,1)S(1)}, u32[]{:S(2)}, u32[]{:S(2)}) collective-permute-start(bf16[512,128]{1,0:T(8,128)(2,1)S(1)} %bitcast.54), channel_id=1, source_target_pairs={{0,3},{1,2},{2,1},{3,0},{4,7},{5,6},{6,5},{7,4},{8,11},{9,10},{10,... | collective-permute-start | bytes 393224 | tf_op jit(solution)/shard_map/ppermute | solution.py:263
  7.4 6.7 %collective-permute-start.11 = (bf16[512,128]{1,0:T(8,128)(2,1)S(1)}, bf16[512,128]{1,0:T(8,128)(2,1)S(1)}, u32[]{:S(2)}, u32[]{:S(2)}) collective-permute-start(bf16[512,128]{1,0:T(8,128)(2,1)S(1)} %collective-permute-done.6.refs_1_), channel_id=1, source_target_pairs={{0,16},{8,24},{16,0},{24,8},{1,17},{9,25},{17,1},{25,9},{2,18},{10... | collective-permute-start | bytes 393224 | tf_op jit(solution)/shard_map/ppermute | solution.py:263
  8.6 10.8 %collective-permute-start.2 = (bf16[512,128]{1,0:T(8,128)(2,1)S(1)}, bf16[512,128]{1,0:T(8,128)(2,1)S(1)}, u32[]{:S(2)}, u32[]{:S(2)}) collective-permute-start(bf16[512,128]{1,0:T(8,128)(2,1)S(1)} %get-tuple-element.28.refs_0_), channel_id=1, source_target_pairs={{0,2},{1,3},{2,0},{3,1},{4,6},{5,7},{6,4},{7,5},{8,10},{9,11},{10,... | collective-permute-start | bytes 393224 | tf_op jit(solution)/shard_map/ppermute | solution.py:263
  9.6 1.3 %copy-start.4 = (bf16[1024,128]{1,0:T(8,128)(2,1)S(1)}, bf16[1024,128]{1,0:T(8,128)(2,1)}, u32[]{:S(2)}) copy-start(bf16[1024,128]{1,0:T(8,128)(2,1)} %param.12) | copy-start | bytes 786436
  9.6 14.9 %collective-permute-start.1 = (bf16[1024,128]{1,0:T(8,128)(2,1)S(1)}, bf16[1024,128]{1,0:T(8,128)(2,1)S(1)}, u32[]{:S(2)}, u32[]{:S(2)}) collective-permute-start(bf16[1024,128]{1,0:T(8,128)(2,1)S(1)} %pack.3.refs_1_), channel_id=1, source_target_pairs={{0,4},{4,0},{1,5},{5,1},{2,6},{6,2},{3,7},{7,3},{8,12},{12,8},{9,1... | collective-permute-start | bytes 786440 | tf_op jit(solution)/shard_map/ppermute | solution.py:263
  14.1 6.6 %collective-permute-start.8 = (bf16[512,128]{1,0:T(8,128)(2,1)S(1)}, bf16[512,128]{1,0:T(8,128)(2,1)S(1)}, u32[]{:S(2)}, u32[]{:S(2)}) collective-permute-start(bf16[512,128]{1,0:T(8,128)(2,1)S(1)} %collective-permute-done.7.refs_2_), channel_id=1, source_target_pairs={{0,1},{1,0},{2,3},{3,2},{4,5},{5,4},{6,7},{7,6},{8,9},{9,8},{10,11... | collective-permute-start | bytes 393224 | tf_op jit(solution)/shard_map/ppermute | solution.py:263
  14.1 10.4 %collective-permute-start.12 = (bf16[512,128]{1,0:T(8,128)(2,1)S(1)}, bf16[512,128]{1,0:T(8,128)(2,1)S(1)}, u32[]{:S(2)}, u32[]{:S(2)}) collective-permute-start(bf16[512,128]{1,0:T(8,128)(2,1)S(1)} %collective-permute-done.7.refs_2_), channel_id=1, source_target_pairs={{0,16},{8,24},{16,0},{24,8},{1,17},{9,25},{17,1},{25,9},{2,18},{10... | collective-permute-start | bytes 393224 | tf_op jit(solution)/shard_map/ppermute | solution.py:263
  15.4 10.9 %collective-permute-start.4 = (bf16[512,128]{1,0:T(8,128)(2,1)S(1)}, bf16[512,128]{1,0:T(8,128)(2,1)S(1)}, u32[]{:S(2)}, u32[]{:S(2)}) collective-permute-start(bf16[512,128]{1,0:T(8,128)(2,1)S(1)} %collective-permute-done.refs_1_), channel_id=1, source_target_pairs={{0,2},{1,3},{2,0},{3,1},{4,6},{5,7},{6,4},{7,5},{8,10},{9,11},{10,... | collective-permute-start | bytes 393224 | tf_op jit(solution)/shard_map/ppermute | solution.py:263
  19.4 6.9 %collective-permute-start.3 = (bf16[512,128]{1,0:T(8,128)(2,1)S(1)}, bf16[512,128]{1,0:T(8,128)(2,1)S(1)}, u32[]{:S(2)}, u32[]{:S(2)}) collective-permute-start(bf16[512,128]{1,0:T(8,128)(2,1)S(1)} %collective-permute-done.2.first_ref.refs_2_), channel_id=1, source_target_pairs={{0,4},{4,0},{1,5},{5,1},{2,6},{6,2},{3,7},{7,3},{8,12},{12,8},{9,1... | collective-permute-start | bytes 393224 | tf_op jit(solution)/shard_map/ppermute | solution.py:263
  20.7 11.5 %collective-permute-start.9 = (bf16[2048,128]{1,0:T(8,128)(2,1)S(1)}, bf16[2048,128]{1,0:T(8,128)(2,1)S(1)}, u32[]{:S(2)}, u32[]{:S(2)}) collective-permute-start(bf16[2048,128]{1,0:T(8,128)(2,1)S(1)} %pack.4.refs_4_), channel_id=1, source_target_pairs={{0,8},{8,0},{16,24},{24,16},{1,9},{9,1},{17,25},{25,17},{2,10},{10... | collective-permute-start | bytes 1572872 | tf_op jit(solution)/shard_map/ppermute | solution.py:263
  24.5 5.1 %collective-permute-start.14 = (bf16[512,128]{1,0:T(8,128)(2,1)S(1)}, bf16[512,128]{1,0:T(8,128)(2,1)S(1)}, u32[]{:S(2)}, u32[]{:S(2)}) collective-permute-start(bf16[512,128]{1,0:T(8,128)(2,1)S(1)} %collective-permute-done.8.refs_3_), channel_id=1, source_target_pairs={{0,16},{8,24},{16,0},{24,8},{1,17},{9,25},{17,1},{25,9},{2,18},{10... | collective-permute-start | bytes 393224 | tf_op jit(solution)/shard_map/ppermute | solution.py:263
  25.8 6.4 %collective-permute-start.13 = (bf16[1536,128]{1,0:T(8,128)(2,1)S(1)}, bf16[1536,128]{1,0:T(8,128)(2,1)S(1)}, u32[]{:S(2)}, u32[]{:S(2)}) collective-permute-start(bf16[1536,128]{1,0:T(8,128)(2,1)S(1)} %pack.5.refs_6_), channel_id=1, source_target_pairs={{0,8},{8,0},{16,24},{24,16},{1,9},{9,1},{17,25},{25,17},{2,10},{10... | collective-permute-start | bytes 1179656 | tf_op jit(solution)/shard_map/ppermute | solution.py:263
  29.5 2.6 %collective-permute-start.15 = (bf16[512,128]{1,0:T(8,128)(2,1)S(1)}, bf16[512,128]{1,0:T(8,128)(2,1)S(1)}, u32[]{:S(2)}, u32[]{:S(2)}) collective-permute-start(bf16[512,128]{1,0:T(8,128)(2,1)S(1)} %collective-permute-done.14.refs_8_), channel_id=1, source_target_pairs={{0,8},{8,0},{16,24},{24,16},{1,9},{9,1},{17,25},{25,17},{2,10},{10... | collective-permute-start | bytes 393224 | tf_op jit(solution)/shard_map/ppermute | solution.py:263
  31.1 1.1 %copy-start.6 = (f32[128]{0:T(128)S(1)}, f32[128]{0:T(128)}, u32[]{:S(2)}) copy-start(f32[128]{0:T(128)} %param.13) | copy-start | bytes 1540
  31.2 5.1 %collective-permute-start.5 = (bf16[512,128]{1,0:T(8,128)(2,1)S(1)}, bf16[512,128]{1,0:T(8,128)(2,1)S(1)}, u32[]{:S(2)}, u32[]{:S(2)}) collective-permute-start(bf16[512,128]{1,0:T(8,128)(2,1)S(1)} %collective-permute-done.4.second_ref.refs_3_), channel_id=1, source_target_pairs={{0,4},{4,0},{1,5},{5,1},{2,6},{6,2},{3,7},{7,3},{8,12},{12,8},{9,1... | collective-permute-start | bytes 393224 | tf_op jit(solution)/shard_map/ppermute | solution.py:263
  35.3 24.3 %copy-start = (bf16[16,128,128]{2,1,0:T(8,128)(2,1)S(1)}, bf16[16,128,128]{2,1,0:T(8,128)(2,1)}, u32[]{:S(2)}) copy-start(bf16[16,128,128]{2,1,0:T(8,128)(2,1)} %refs_1_.1) | copy-start | bytes 1572868
  36.3 5.2 %copy-start.5 = (f32[512]{0:T(512)S(1)}, f32[512]{0:T(512)}, u32[]{:S(2)}) copy-start(f32[512]{0:T(512)} %param.17) | copy-start | bytes 6148
  36.3 5.2 %copy-start.7 = (f32[128]{0:T(128)S(1)}, f32[128]{0:T(128)}, u32[]{:S(2)}) copy-start(f32[128]{0:T(128)} %param.19) | copy-start | bytes 1540
  36.3 5.2 %copy-start.8 = (f32[128]{0:T(128)S(1)}, f32[128]{0:T(128)}, u32[]{:S(2)}) copy-start(f32[128]{0:T(128)} %param.15) | copy-start | bytes 1540
  36.3 23.3 %copy-start.2 = (bf16[512,128]{1,0:T(8,128)(2,1)S(1)}, bf16[512,128]{1,0:T(8,128)(2,1)}, u32[]{:S(2)}) copy-start(bf16[512,128]{1,0:T(8,128)(2,1)} %refs_10_.1) | copy-start | bytes 393220
  39.4 20.2 %copy-start.1 = (bf16[128,512]{1,0:T(8,128)(2,1)S(1)}, bf16[128,512]{1,0:T(8,128)(2,1)}, u32[]{:S(2)}) copy-start(bf16[128,512]{1,0:T(8,128)(2,1)} %refs_9_.1) | copy-start | bytes 393220
  39.5 11.8 %collective-permute-start.16 = (bf16[32,16,128]{2,1,0:T(8,128)(2,1)S(1)}, bf16[32,16,128]{2,1,0:T(8,128)(2,1)S(1)}, u32[]{:S(2)}, u32[]{:S(2)}) collective-permute-start(bf16[32,16,128]{2,1,0:T(8,128)(2,1)S(1)} %get-tuple-element.21), channel_id=1, source_target_pairs={{0,0},{1,1},{2,2},{3,3},{4,16},{5,17},{6,18},{7,19},{8,10},{9,11},... | collective-permute-start | bytes 393224 | tf_op jit(solution)/shard_map/ppermute | solution.py:386
  41.6 11.7 %collective-permute-start.17 = (bf16[32,16,128]{2,1,0:T(8,128)(2,1)S(1)}, bf16[32,16,128]{2,1,0:T(8,128)(2,1)S(1)}, u32[]{:S(2)}, u32[]{:S(2)}) collective-permute-start(bf16[32,16,128]{2,1,0:T(8,128)(2,1)S(1)} %get-tuple-element.22), channel_id=1, source_target_pairs={{0,2},{1,3},{2,0},{3,1},{4,6},{5,7},{6,4},{7,5},{8,8},{9,9},{10,10... | collective-permute-start | bytes 393224 | tf_op jit(solution)/shard_map/ppermute | solution.py:386
  45.7 8.7 %collective-permute-start.18 = (bf16[32,16,128]{2,1,0:T(8,128)(2,1)S(1)}, bf16[32,16,128]{2,1,0:T(8,128)(2,1)S(1)}, u32[]{:S(2)}, u32[]{:S(2)}) collective-permute-start(bf16[32,16,128]{2,1,0:T(8,128)(2,1)S(1)} %get-tuple-element.23), channel_id=1, source_target_pairs={{0,1},{1,0},{2,3},{3,2},{4,17},{5,16},{6,19},{7,18},{8,10},{9,11},... | collective-permute-start | bytes 393224 | tf_op jit(solution)/shard_map/ppermute | solution.py:386
  48.1 9.9 %collective-permute-start.19 = (bf16[32,16,128]{2,1,0:T(8,128)(2,1)S(1)}, bf16[32,16,128]{2,1,0:T(8,128)(2,1)S(1)}, u32[]{:S(2)}, u32[]{:S(2)}) collective-permute-start(bf16[32,16,128]{2,1,0:T(8,128)(2,1)S(1)} %get-tuple-element.24), channel_id=1, source_target_pairs={{0,2},{1,3},{2,0},{3,1},{4,6},{5,7},{6,4},{7,5},{8,9},{9,8},{10,11... | collective-permute-start | bytes 393224 | tf_op jit(solution)/shard_map/ppermute | solution.py:386
  48.1 9.9 %collective-permute-start.20 = (bf16[32,16,128]{2,1,0:T(8,128)(2,1)S(1)}, bf16[32,16,128]{2,1,0:T(8,128)(2,1)S(1)}, u32[]{:S(2)}, u32[]{:S(2)}) collective-permute-start(bf16[32,16,128]{2,1,0:T(8,128)(2,1)S(1)} %get-tuple-element.25), channel_id=1, source_target_pairs={{0,8},{1,9},{2,10},{3,11},{4,24},{5,25},{6,26},{7,27},{8,0},{9,1},... | collective-permute-start | bytes 393224 | tf_op jit(solution)/shard_map/ppermute | solution.py:386
  51.3 8.3 %collective-permute-start.21 = (bf16[32,16,128]{2,1,0:T(8,128)(2,1)S(1)}, bf16[32,16,128]{2,1,0:T(8,128)(2,1)S(1)}, u32[]{:S(2)}, u32[]{:S(2)}) collective-permute-start(bf16[32,16,128]{2,1,0:T(8,128)(2,1)S(1)} %get-tuple-element.26), channel_id=1, source_target_pairs={{0,9},{1,8},{2,11},{3,10},{4,25},{5,24},{6,27},{7,26},{8,1},{9,0},... | collective-permute-start | bytes 393224 | tf_op jit(solution)/shard_map/ppermute | solution.py:386

commit v4 on v3

--- a/solution.py
+++ b/solution.py
@@ -21,6 +21,7 @@
     data_refs = [refs.pop(0) for _ in range(data_count)]
     bias_ref, weight_ref = refs.pop(0), refs.pop(0)
     first_ref = refs.pop(0)
+    refs = refs[1:] if last else refs
     update_ref = refs.pop() if last else refs[0]
     outer_ref = refs.pop()
     lhs_ref = refs.pop()
@@ -161,7 +162,6 @@
     gain = vector_ref[:, :pair_channels]
     down_bias = vector_ref[:, pair_channels : 2 * pair_channels]
     up_bias = vector_ref[:, 2 * pair_channels :]
-    ones = jnp.full((2 * pair_channels, pair_channels), 1.0 / pair_channels, jnp.bfloat16)
 
     def chosen(first, second, rows):
         return jnp.where(core == 0, slot_refs[first][rows], slot_refs[second][rows])
@@ -202,14 +202,9 @@
             )
         middle = jnp.concatenate(middles, axis=0)
         values = middle.astype(jnp.float32)
-        center = jnp.dot(middle, ones[:pair_channels], preferred_element_type=jnp.float32)
+        center = jnp.mean(values, axis=1, keepdims=True)
         moved = values - center
-        square = jnp.square(moved)
-        high = square.astype(jnp.bfloat16)
-        rest = (square - high.astype(jnp.float32)).astype(jnp.bfloat16)
-        spread = jnp.dot(
-            jnp.concatenate([high, rest], axis=1), ones, preferred_element_type=jnp.float32
-        )
+        spread = jnp.mean(jnp.square(moved), axis=1, keepdims=True)
         normed = moved * lax.rsqrt(spread + epsilon) * gain
         hidden = jnp.dot(
             normed.astype(jnp.bfloat16), up_ref[...], preferred_element_type=jnp.float32
@@ -296,7 +291,8 @@
     for dy in range(1, cols):
         shares[dy - 1] += [swap(value, "col", cols, dy) for value in fars]
     far_shares = [pair[1] for pair in shares]
-    far_tile = arrived(*fars, 32 * (share_rows * groups * group_len) * groups * group_len // 4)
+    far_tile = arrived(*fars, 10 * (share_rows * groups * group_len) * groups * group_len)
+    share_tile = arrived(shares[0][1], shares[0][-1], 4 * (share_rows * groups * group_len) * groups * group_len)
     data = []
     right_places = {dz: [] for dz in range(groups)}
     order = (0, 1, low + 1, low)
@@ -304,7 +300,7 @@
     last = ()
     for dz in order:
         for dx in range(1, xs):
-            behind = last + ((near_shares,) if dz == low else ())
+            behind = last + ((near_shares, weight) if dz == low else ())
             crosses[dz].append(swap(after(blocks[dz], *behind), "row", rows, 2 * dx))
             last = (crosses[dz][-1],)
     for position in range(xs):
@@ -360,7 +356,7 @@
     outs = update_call(
         True,
         last_lefts,
-        [first],
+        [first, share_tile],
         [jax.ShapeDtypeStruct((run, half, pair_channels), bf16)]
         + [jax.ShapeDtypeStruct((2 * run, run, pair_channels), bf16)] * (4 + low),
         [vmem] * (5 + low),

time: 64.6 us -> 66.5 us (1.029); the launches traced: 63.6 us -> 66.3 us
  local copies, waits for them, and re-layouts: 2.76 us -> 4.41 us
    ppermute x6, waiting for transfers between devices: 6.31 us -> 7.58 us  [exchange(): return lax.ppermute(outs[1 + slot], axes, pairs)]
    reshape x1, local copies, waits for them, and re-layouts: 0.14 us -> 1.09 us  [on_device(): weight = weight.reshape(2 * pair_channels, channels * channels // 2)]
    ppermute x16, waiting for transfers between devices: 10.6 us -> 9.69 us  [swap(): return lax.ppermute(value, name, [(i, i ^ flip) for i in range(size)])]
    unnamed x20, local copies, waits for them, and re-layouts: 1.23 us -> 1.94 us
  transfers between devices with their start and end apart: 22 -> 22, of which waited for: 7 -> 8; matrix products, arithmetic and copies ran while one was open for 3% -> 5% of each run, Pallas kernels for 5% -> 0%
where the time goes in v4:
time: 66.5 us; the launch traced here: 66.3 us
  starting transfers between devices  33 us (50%)
  waiting for transfers between devices  17.3 us (26%)
  Pallas kernels  10.6 us (16%)
  local copies, waits for them, and re-layouts  4.41 us (7%)
    ppermute x16, starting transfers between devices, swap(): return lax.ppermute(value, name, [(i, i ^ flip) for i in range(size)])  18.8 us
    ppermute x6, starting transfers between devices, exchange(): return lax.ppermute(outs[1 + slot], axes, pairs)  14.3 us
    ppermute x16, waiting for transfers between devices, swap(): return lax.ppermute(value, name, [(i, i ^ flip) for i in range(size)])  9.69 us
    ppermute x6, waiting for transfers between devices, exchange(): return lax.ppermute(outs[1 + slot], axes, pairs)  7.58 us
    pallas_call x2, Pallas kernels, update_call(): pl.pallas_call(functools.partial(update_kernel, places, cols, low, last,...  6.09 us
    pallas_call x1, Pallas kernels, on_device(): pl.pallas_call(functools.partial(finish_kernel, low), out_shape=jax.Shape...  4.42 us
    unnamed x20, local copies, waits for them, and re-layouts  1.94 us
  transfers between devices with their start and end apart: 22, of which 8 were waited for; matrix products, arithmetic and copies ran while one was open for 5% of the time, Pallas kernels for 0%

profile of v4, /device:TPU:3, one launch (start us, length us, event | category | flops | bytes accessed | tf_op | source)
XLA Modules:
  0.0 66.3 jit_solution(898618962717434961)
XLA Ops:
  0.0 1.1 %copy.18 = bf16[128,8,128]{0,2,1:T(8,128)(2,1)S(1)} copy(bf16[128,8,128]{2,1,0:T(8,128)(2,1)} %param.11) | data formatting | bytes 524288 | tf_op args[1]
  1.2 0.2 copy.19
  1.4 0.1 reshape.55
  1.5 0.0 copy-start.3
  1.5 0.1 copy.20
  1.7 0.1 collective-permute-start.10
  1.7 1.5 %collective-permute-start.6 = (bf16[512,128]{1,0:T(8,128)(2,1)S(1)}, bf16[512,128]{1,0:T(8,128)(2,1)S(1)}, u32[]{:S(2)}, u32[]{:S(2)}) collective-permute-start(bf16[512,128]{1,0:T(8,128)(2,1)S(1)} %bitcast.46), channel_id=1, source_target_pairs={{0,1},{1,0},{2,3},{3,2},{4,5},{5,4},{6,7},{7,6},{8,9},{9,8},{10,11... | collective-permute-start | bytes 393224 | tf_op jit(solution)/shard_map/ppermute | solution.py:258
  3.3 0.1 copy.21
  3.4 2.3 %collective-permute-start.7 = (bf16[512,128]{1,0:T(8,128)(2,1)S(1)}, bf16[512,128]{1,0:T(8,128)(2,1)S(1)}, u32[]{:S(2)}, u32[]{:S(2)}) collective-permute-start(bf16[512,128]{1,0:T(8,128)(2,1)S(1)} %bitcast.54), channel_id=1, source_target_pairs={{0,3},{1,2},{2,1},{3,0},{4,7},{5,6},{6,5},{7,4},{8,11},{9,10},{10,... | collective-permute-start | bytes 393224 | tf_op jit(solution)/shard_map/ppermute | solution.py:258
  5.7 0.3 copy.17
  6.0 0.5 collective-permute-start
  6.5 1.0 %collective-permute-start.2 = (bf16[512,128]{1,0:T(8,128)(2,1)S(1)}, bf16[512,128]{1,0:T(8,128)(2,1)S(1)}, u32[]{:S(2)}, u32[]{:S(2)}) collective-permute-start(bf16[512,128]{1,0:T(8,128)(2,1)S(1)} %get-tuple-element.28.refs_0_), channel_id=1, source_target_pairs={{0,2},{1,3},{2,0},{3,1},{4,6},{5,7},{6,4},{7,5},{8,10},{9,11},{10,... | collective-permute-start | bytes 393224 | tf_op jit(solution)/shard_map/ppermute | solution.py:258
  7.5 0.2 constant_dynamic-slice_fusion.3
  7.7 1.3 %collective-permute-start.11 = (bf16[512,128]{1,0:T(8,128)(2,1)S(1)}, bf16[512,128]{1,0:T(8,128)(2,1)S(1)}, u32[]{:S(2)}, u32[]{:S(2)}) collective-permute-start(bf16[512,128]{1,0:T(8,128)(2,1)S(1)} %collective-permute-done.6.refs_1_), channel_id=1, source_target_pairs={{0,16},{8,24},{16,0},{24,8},{1,17},{9,25},{17,1},{25,9},{2,18},{10... | collective-permute-start | bytes 393224 | tf_op jit(solution)/shard_map/ppermute | solution.py:258
  9.0 1.6 %collective-permute-done.7.refs_2_ = bf16[512,128]{1,0:T(8,128)(2,1)S(1)} collective-permute-done((bf16[512,128]{1,0:T(8,128)(2,1)S(1)}, bf16[512,128]{1,0:T(8,128)(2,1)S(1)}, u32[]{:S(2)}, u32[]{:S(2)}) %collective-permute-start.7) | collective-permute-done | bytes 131104 | tf_op jit(solution)/shard_map/ppermute | solution.py:258
  10.6 0.1 copy_bitcast_fusion.1
  10.7 4.0 %collective-permute-done.refs_1_ = bf16[512,128]{1,0:T(8,128)(2,1)S(1)} collective-permute-done((bf16[512,128]{1,0:T(8,128)(2,1)S(1)}, bf16[512,128]{1,0:T(8,128)(2,1)S(1)}, u32[]{:S(2)}, u32[]{:S(2)}) %collective-permute-start) | collective-permute-done | bytes 131104 | tf_op jit(solution)/shard_map/ppermute | solution.py:258
  14.7 1.3 %collective-permute-start.1 = (bf16[1024,128]{1,0:T(8,128)(2,1)S(1)}, bf16[1024,128]{1,0:T(8,128)(2,1)S(1)}, u32[]{:S(2)}, u32[]{:S(2)}) collective-permute-start(bf16[1024,128]{1,0:T(8,128)(2,1)S(1)} %pack.3.refs_1_), channel_id=1, source_target_pairs={{0,4},{4,0},{1,5},{5,1},{2,6},{6,2},{3,7},{7,3},{8,12},{12,8},{9,1... | collective-permute-start | bytes 786440 | tf_op jit(solution)/shard_map/ppermute | solution.py:258
  16.0 1.2 %collective-permute-start.12 = (bf16[512,128]{1,0:T(8,128)(2,1)S(1)}, bf16[512,128]{1,0:T(8,128)(2,1)S(1)}, u32[]{:S(2)}, u32[]{:S(2)}) collective-permute-start(bf16[512,128]{1,0:T(8,128)(2,1)S(1)} %collective-permute-done.7.refs_2_), channel_id=1, source_target_pairs={{0,16},{8,24},{16,0},{24,8},{1,17},{9,25},{17,1},{25,9},{2,18},{10... | collective-permute-start | bytes 393224 | tf_op jit(solution)/shard_map/ppermute | solution.py:258
  17.2 1.5 %collective-permute-done.8.refs_3_ = bf16[512,128]{1,0:T(8,128)(2,1)S(1)} collective-permute-done((bf16[512,128]{1,0:T(8,128)(2,1)S(1)}, bf16[512,128]{1,0:T(8,128)(2,1)S(1)}, u32[]{:S(2)}, u32[]{:S(2)}) %collective-permute-start.8) | collective-permute-done | bytes 131104 | tf_op jit(solution)/shard_map/ppermute | solution.py:258
  18.8 2.6 %collective-permute-start.9 = (bf16[2048,128]{1,0:T(8,128)(2,1)S(1)}, bf16[2048,128]{1,0:T(8,128)(2,1)S(1)}, u32[]{:S(2)}, u32[]{:S(2)}) collective-permute-start(bf16[2048,128]{1,0:T(8,128)(2,1)S(1)} %pack.4.refs_4_), channel_id=1, source_target_pairs={{0,8},{8,0},{16,24},{24,16},{1,9},{9,1},{17,25},{25,17},{2,10},{10... | collective-permute-start | bytes 1572872 | tf_op jit(solution)/shard_map/ppermute | solution.py:258
  21.4 0.1 copy_bitcast_fusion.3
  21.5 3.3 %collective-permute-start.13 = (bf16[1536,128]{1,0:T(8,128)(2,1)S(1)}, bf16[1536,128]{1,0:T(8,128)(2,1)S(1)}, u32[]{:S(2)}, u32[]{:S(2)}) collective-permute-start(bf16[1536,128]{1,0:T(8,128)(2,1)S(1)} %pack.5.refs_6_), channel_id=1, source_target_pairs={{0,8},{8,0},{16,24},{24,16},{1,9},{9,1},{17,25},{25,17},{2,10},{10... | collective-permute-start | bytes 1179656 | tf_op jit(solution)/shard_map/ppermute | solution.py:258
  24.9 0.5 pad_maximum_fusion
  25.3 0.7 %copy.38 = bf16[64,8,2,128]{3,1,2,0:T(8,128)(2,1)} copy(bf16[64,8,2,128]{3,2,1,0:T(2,128)(2,1)S(1)} %bitcast.50) | data formatting | bytes 524288
  26.1 0.2 collective-permute-start.3
  26.3 1.2 %collective-permute-start.14 = (bf16[512,128]{1,0:T(8,128)(2,1)S(1)}, bf16[512,128]{1,0:T(8,128)(2,1)S(1)}, u32[]{:S(2)}, u32[]{:S(2)}) collective-permute-start(bf16[512,128]{1,0:T(8,128)(2,1)S(1)} %collective-permute-done.8.refs_3_), channel_id=1, source_target_pairs={{0,16},{8,24},{16,0},{24,8},{1,17},{9,25},{17,1},{25,9},{2,18},{10... | collective-permute-start | bytes 393224 | tf_op jit(solution)/shard_map/ppermute | solution.py:258
  27.5 1.1 %copy.27.refs_11_ = bf16[256,512]{1,0:T(8,128)(2,1)S(1)} copy(bf16[256,512]{0,1:T(8,128)(2,1)} %bitcast.49) | data formatting | bytes 524288 | tf_op jit(solution)/shard_map/reshape | solution.py:281
  28.6 1.3 %collective-permute-start.5 = (bf16[512,128]{1,0:T(8,128)(2,1)S(1)}, bf16[512,128]{1,0:T(8,128)(2,1)S(1)}, u32[]{:S(2)}, u32[]{:S(2)}) collective-permute-start(bf16[512,128]{1,0:T(8,128)(2,1)S(1)} %collective-permute-done.4.second_ref.refs_3_), channel_id=1, source_target_pairs={{0,4},{4,0},{1,5},{5,1},{2,6},{6,2},{3,7},{7,3},{8,12},{12,8},{9,1... | collective-permute-start | bytes 393224 | tf_op jit(solution)/shard_map/ppermute | solution.py:258
  29.9 1.3 %collective-permute-done.3.first_ref.refs_2_ = bf16[512,128]{1,0:T(8,128)(2,1)S(1)} collective-permute-done((bf16[512,128]{1,0:T(8,128)(2,1)S(1)}, bf16[512,128]{1,0:T(8,128)(2,1)S(1)}, u32[]{:S(2)}, u32[]{:S(2)}) %collective-permute-start.3) | collective-permute-done | bytes 131104 | tf_op jit(solution)/shard_map/ppermute | solution.py:258
  31.2 1.0 %collective-permute-start.15 = (bf16[512,128]{1,0:T(8,128)(2,1)S(1)}, bf16[512,128]{1,0:T(8,128)(2,1)S(1)}, u32[]{:S(2)}, u32[]{:S(2)}) collective-permute-start(bf16[512,128]{1,0:T(8,128)(2,1)S(1)} %collective-permute-done.14.refs_8_), channel_id=1, source_target_pairs={{0,8},{8,0},{16,24},{24,16},{1,9},{9,1},{17,25},{25,17},{2,10},{10... | collective-permute-start | bytes 393224 | tf_op jit(solution)/shard_map/ppermute | solution.py:258
  32.2 0.1 pad_add_fusion.refs_0_
  32.3 1.3 %collective-permute-done.5.second_ref.refs_3_ = bf16[512,128]{1,0:T(8,128)(2,1)S(1)} collective-permute-done((bf16[512,128]{1,0:T(8,128)(2,1)S(1)}, bf16[512,128]{1,0:T(8,128)(2,1)S(1)}, u32[]{:S(2)}, u32[]{:S(2)}) %collective-permute-start.5) | collective-permute-done | bytes 131104 | tf_op jit(solution)/shard_map/ppermute | solution.py:258
  33.6 0.1 broadcast_in_dim.2.refs_10_
  33.7 3.0 %update_first.1.refs_12_ = bf16[16,64,128]{2,1,0:T(8,128)(2,1)S(1)} custom-call(s32[4]{0:T(128)S(1)} %pad_add_fusion.refs_0_, bf16[1024,128]{1,0:T(8,128)(2,1)S(1)} %pack.3.refs_1_, bf16[512,128]{1,0:T(8,128)(2,1)S(1)} %collective-permute-done.2.first_ref.refs_2_, bf16[512,128]{1,0:T(8,128)(2,1)S(1)} %collective-permute-done.4.second_ref.refs_3_, ...), custom_call_target="tpu_custom_call" | custom-call | flops 1610612736 | bytes 2097152 | tf_op jit(solution)/shard_map/update_first/pallas_call | solution.py:334
  36.7 0.0 copy-start.8
  36.7 0.0 copy-start
  36.7 3.1 %update_last.1 = (bf16[16,64,128]{2,1,0:T(8,128)(2,1)S(1)}, bf16[32,16,128]{2,1,0:T(8,128)(2,1)S(1)}, bf16[32,16,128]{2,1,0:T(8,128)(2,1)S(1)}, bf16[32,16,128]{...) custom-call(s32[4]{0:T(128)S(1)} %pad_add_fusion.refs_0_, ...), custom_call_target="tpu_custom_call" | custom-call | flops 1610612736 | bytes 2097152 | tf_op jit(solution)/shard_map/update_last/pallas_call | solution.py:334
  39.8 4.7 %collective-permute-start.16 = (bf16[32,16,128]{2,1,0:T(8,128)(2,1)S(1)}, bf16[32,16,128]{2,1,0:T(8,128)(2,1)S(1)}, u32[]{:S(2)}, u32[]{:S(2)}) collective-permute-start(bf16[32,16,128]{2,1,0:T(8,128)(2,1)S(1)} %get-tuple-element.21), channel_id=1, source_target_pairs={{0,0},{1,1},{2,2},{3,3},{4,16},{5,17},{6,18},{7,19},{8,10},{9,11},... | collective-permute-start | bytes 393224 | tf_op jit(solution)/shard_map/ppermute | solution.py:382
  44.6 3.7 %collective-permute-start.17 = (bf16[32,16,128]{2,1,0:T(8,128)(2,1)S(1)}, bf16[32,16,128]{2,1,0:T(8,128)(2,1)S(1)}, u32[]{:S(2)}, u32[]{:S(2)}) collective-permute-start(bf16[32,16,128]{2,1,0:T(8,128)(2,1)S(1)} %get-tuple-element.22), channel_id=1, source_target_pairs={{0,2},{1,3},{2,0},{3,1},{4,6},{5,7},{6,4},{7,5},{8,8},{9,9},{10,10... | collective-permute-start | bytes 393224 | tf_op jit(solution)/shard_map/ppermute | solution.py:382
  48.3 0.1 collective-permute-start.18
  48.4 2.4 %collective-permute-start.19 = (bf16[32,16,128]{2,1,0:T(8,128)(2,1)S(1)}, bf16[32,16,128]{2,1,0:T(8,128)(2,1)S(1)}, u32[]{:S(2)}, u32[]{:S(2)}) collective-permute-start(bf16[32,16,128]{2,1,0:T(8,128)(2,1)S(1)} %get-tuple-element.24), channel_id=1, source_target_pairs={{0,2},{1,3},{2,0},{3,1},{4,6},{5,7},{6,4},{7,5},{8,9},{9,8},{10,11... | collective-permute-start | bytes 393224 | tf_op jit(solution)/shard_map/ppermute | solution.py:382
  50.8 3.4 %collective-permute-start.20 = (bf16[32,16,128]{2,1,0:T(8,128)(2,1)S(1)}, bf16[32,16,128]{2,1,0:T(8,128)(2,1)S(1)}, u32[]{:S(2)}, u32[]{:S(2)}) collective-permute-start(bf16[32,16,128]{2,1,0:T(8,128)(2,1)S(1)} %get-tuple-element.25), channel_id=1, source_target_pairs={{0,8},{1,9},{2,10},{3,11},{4,24},{5,25},{6,26},{7,27},{8,0},{9,1},... | collective-permute-start | bytes 393224 | tf_op jit(solution)/shard_map/ppermute | solution.py:382
  54.2 0.1 fusion.refs_12_
  54.3 2.7 %collective-permute-done.18.refs_5_ = bf16[32,16,128]{2,1,0:T(8,128)(2,1)S(1)} collective-permute-done((bf16[32,16,128]{2,1,0:T(8,128)(2,1)S(1)}, bf16[32,16,128]{2,1,0:T(8,128)(2,1)S(1)}, u32[]{:S(2)}, u32[]{:S(2)}) %collective-permute-start.18) | collective-permute-done | bytes 131104 | tf_op jit(solution)/shard_map/ppermute | solution.py:382
  57.1 2.9 %collective-permute-done.20.refs_7_ = bf16[32,16,128]{2,1,0:T(8,128)(2,1)S(1)} collective-permute-done((bf16[32,16,128]{2,1,0:T(8,128)(2,1)S(1)}, bf16[32,16,128]{2,1,0:T(8,128)(2,1)S(1)}, u32[]{:S(2)}, u32[]{:S(2)}) %collective-permute-start.20) | collective-permute-done | bytes 131104 | tf_op jit(solution)/shard_map/ppermute | solution.py:382
  59.9 2.0 %collective-permute-done.21.refs_8_ = bf16[32,16,128]{2,1,0:T(8,128)(2,1)S(1)} collective-permute-done((bf16[32,16,128]{2,1,0:T(8,128)(2,1)S(1)}, bf16[32,16,128]{2,1,0:T(8,128)(2,1)S(1)}, u32[]{:S(2)}, u32[]{:S(2)}) %collective-permute-start.21) | collective-permute-done | bytes 131104 | tf_op jit(solution)/shard_map/ppermute | solution.py:382
  61.9 4.4 %finish.1 = bf16[16,128,128]{2,1,0:T(8,128)(2,1)} custom-call(s32[4]{0:T(128)S(1)} %pad_add_fusion.refs_0_, bf16[16,128,128]{2,1,0:T(8,128)(2,1)S(1)} %copy-done, bf16[16,64,128]{2,1,0:T(8,128)(2,1)S(1)} %get-tuple-element.20.refs_2_, bf16[32,16,128]{2,1,0:T(8,128)(2,1)S(1)} %collective-permute-done.16.refs_3_, ...), custom_call_target="tpu_custom_call" | custom-call | tf_op jit(solution)/shard_map/finish/pallas_call | solution.py:387
  (42 shorter events, 0.2 us)
Async XLA Ops:
  1.5 4.2 %copy-start.3 = (bf16[128,32,64]{0,2,1:T(8,128)(2,1)S(1)}, bf16[128,32,64]{0,2,1:T(8,128)(2,1)}, u32[]{:S(2)}) copy-start(bf16[128,32,64]{0,2,1:T(8,128)(2,1)} %param.10) | copy-start | bytes 1572868
  1.7 6.0 %collective-permute-start.10 = (bf16[512,128]{1,0:T(8,128)(2,1)S(1)}, bf16[512,128]{1,0:T(8,128)(2,1)S(1)}, u32[]{:S(2)}, u32[]{:S(2)}) collective-permute-start(bf16[512,128]{1,0:T(8,128)(2,1)S(1)} %bitcast.45), channel_id=1, source_target_pairs={{0,16},{8,24},{16,0},{24,8},{1,17},{9,25},{17,1},{25,9},{2,18},{10... | collective-permute-start | bytes 393224 | tf_op jit(solution)/shard_map/ppermute | solution.py:258
  1.7 5.9 %collective-permute-start.6 = (bf16[512,128]{1,0:T(8,128)(2,1)S(1)}, bf16[512,128]{1,0:T(8,128)(2,1)S(1)}, u32[]{:S(2)}, u32[]{:S(2)}) collective-permute-start(bf16[512,128]{1,0:T(8,128)(2,1)S(1)} %bitcast.46), channel_id=1, source_target_pairs={{0,1},{1,0},{2,3},{3,2},{4,5},{5,4},{6,7},{7,6},{8,9},{9,8},{10,11... | collective-permute-start | bytes 393224 | tf_op jit(solution)/shard_map/ppermute | solution.py:258
  3.4 7.2 %collective-permute-start.7 = (bf16[512,128]{1,0:T(8,128)(2,1)S(1)}, bf16[512,128]{1,0:T(8,128)(2,1)S(1)}, u32[]{:S(2)}, u32[]{:S(2)}) collective-permute-start(bf16[512,128]{1,0:T(8,128)(2,1)S(1)} %bitcast.54), channel_id=1, source_target_pairs={{0,3},{1,2},{2,1},{3,0},{4,7},{5,6},{6,5},{7,4},{8,11},{9,10},{10,... | collective-permute-start | bytes 393224 | tf_op jit(solution)/shard_map/ppermute | solution.py:258
  6.0 1.5 %copy-start.4 = (bf16[1024,128]{1,0:T(8,128)(2,1)S(1)}, bf16[1024,128]{1,0:T(8,128)(2,1)}, u32[]{:S(2)}) copy-start(bf16[1024,128]{1,0:T(8,128)(2,1)} %param.12) | copy-start | bytes 786436
  6.0 8.6 %collective-permute-start = (bf16[512,128]{1,0:T(8,128)(2,1)S(1)}, bf16[512,128]{1,0:T(8,128)(2,1)S(1)}, u32[]{:S(2)}, u32[]{:S(2)}) collective-permute-start(bf16[512,128]{1,0:T(8,128)(2,1)S(1)} %get-tuple-element.27), channel_id=1, source_target_pairs={{0,1},{1,0},{2,3},{3,2},{4,5},{5,4},{6,7},{7,6},{8,9},{9,8},{10,11... | collective-permute-start | bytes 393224 | tf_op jit(solution)/shard_map/ppermute | solution.py:258
  6.5 19.6 %collective-permute-start.2 = (bf16[512,128]{1,0:T(8,128)(2,1)S(1)}, bf16[512,128]{1,0:T(8,128)(2,1)S(1)}, u32[]{:S(2)}, u32[]{:S(2)}) collective-permute-start(bf16[512,128]{1,0:T(8,128)(2,1)S(1)} %get-tuple-element.28.refs_0_), channel_id=1, source_target_pairs={{0,2},{1,3},{2,0},{3,1},{4,6},{5,7},{6,4},{7,5},{8,10},{9,11},{10,... | collective-permute-start | bytes 393224 | tf_op jit(solution)/shard_map/ppermute | solution.py:258
  7.7 8.3 %collective-permute-start.11 = (bf16[512,128]{1,0:T(8,128)(2,1)S(1)}, bf16[512,128]{1,0:T(8,128)(2,1)S(1)}, u32[]{:S(2)}, u32[]{:S(2)}) collective-permute-start(bf16[512,128]{1,0:T(8,128)(2,1)S(1)} %collective-permute-done.6.refs_1_), channel_id=1, source_target_pairs={{0,16},{8,24},{16,0},{24,8},{1,17},{9,25},{17,1},{25,9},{2,18},{10... | collective-permute-start | bytes 393224 | tf_op jit(solution)/shard_map/ppermute | solution.py:258
  10.6 8.2 %collective-permute-start.8 = (bf16[512,128]{1,0:T(8,128)(2,1)S(1)}, bf16[512,128]{1,0:T(8,128)(2,1)S(1)}, u32[]{:S(2)}, u32[]{:S(2)}) collective-permute-start(bf16[512,128]{1,0:T(8,128)(2,1)S(1)} %collective-permute-done.7.refs_2_), channel_id=1, source_target_pairs={{0,1},{1,0},{2,3},{3,2},{4,5},{5,4},{6,7},{7,6},{8,9},{9,8},{10,11... | collective-permute-start | bytes 393224 | tf_op jit(solution)/shard_map/ppermute | solution.py:258
  14.7 11.6 %collective-permute-start.1 = (bf16[1024,128]{1,0:T(8,128)(2,1)S(1)}, bf16[1024,128]{1,0:T(8,128)(2,1)S(1)}, u32[]{:S(2)}, u32[]{:S(2)}) collective-permute-start(bf16[1024,128]{1,0:T(8,128)(2,1)S(1)} %pack.3.refs_1_), channel_id=1, source_target_pairs={{0,4},{4,0},{1,5},{5,1},{2,6},{6,2},{3,7},{7,3},{8,12},{12,8},{9,1... | collective-permute-start | bytes 786440 | tf_op jit(solution)/shard_map/ppermute | solution.py:258
  16.0 12.6 %collective-permute-start.4 = (bf16[512,128]{1,0:T(8,128)(2,1)S(1)}, bf16[512,128]{1,0:T(8,128)(2,1)S(1)}, u32[]{:S(2)}, u32[]{:S(2)}) collective-permute-start(bf16[512,128]{1,0:T(8,128)(2,1)S(1)} %collective-permute-done.refs_1_), channel_id=1, source_target_pairs={{0,2},{1,3},{2,0},{3,1},{4,6},{5,7},{6,4},{7,5},{8,10},{9,11},{10,... | collective-permute-start | bytes 393224 | tf_op jit(solution)/shard_map/ppermute | solution.py:258
  16.0 5.5 %collective-permute-start.12 = (bf16[512,128]{1,0:T(8,128)(2,1)S(1)}, bf16[512,128]{1,0:T(8,128)(2,1)S(1)}, u32[]{:S(2)}, u32[]{:S(2)}) collective-permute-start(bf16[512,128]{1,0:T(8,128)(2,1)S(1)} %collective-permute-done.7.refs_2_), channel_id=1, source_target_pairs={{0,16},{8,24},{16,0},{24,8},{1,17},{9,25},{17,1},{25,9},{2,18},{10... | collective-permute-start | bytes 393224 | tf_op jit(solution)/shard_map/ppermute | solution.py:258
  18.8 14.8 %collective-permute-start.9 = (bf16[2048,128]{1,0:T(8,128)(2,1)S(1)}, bf16[2048,128]{1,0:T(8,128)(2,1)S(1)}, u32[]{:S(2)}, u32[]{:S(2)}) collective-permute-start(bf16[2048,128]{1,0:T(8,128)(2,1)S(1)} %pack.4.refs_4_), channel_id=1, source_target_pairs={{0,8},{8,0},{16,24},{24,16},{1,9},{9,1},{17,25},{25,17},{2,10},{10... | collective-permute-start | bytes 1572872 | tf_op jit(solution)/shard_map/ppermute | solution.py:258
  21.5 12.0 %collective-permute-start.13 = (bf16[1536,128]{1,0:T(8,128)(2,1)S(1)}, bf16[1536,128]{1,0:T(8,128)(2,1)S(1)}, u32[]{:S(2)}, u32[]{:S(2)}) collective-permute-start(bf16[1536,128]{1,0:T(8,128)(2,1)S(1)} %pack.5.refs_6_), channel_id=1, source_target_pairs={{0,8},{8,0},{16,24},{24,16},{1,9},{9,1},{17,25},{25,17},{2,10},{10... | collective-permute-start | bytes 1179656 | tf_op jit(solution)/shard_map/ppermute | solution.py:258
  26.1 5.1 %collective-permute-start.3 = (bf16[512,128]{1,0:T(8,128)(2,1)S(1)}, bf16[512,128]{1,0:T(8,128)(2,1)S(1)}, u32[]{:S(2)}, u32[]{:S(2)}) collective-permute-start(bf16[512,128]{1,0:T(8,128)(2,1)S(1)} %collective-permute-done.2.first_ref.refs_2_), channel_id=1, source_target_pairs={{0,4},{4,0},{1,5},{5,1},{2,6},{6,2},{3,7},{7,3},{8,12},{12,8},{9,1... | collective-permute-start | bytes 393224 | tf_op jit(solution)/shard_map/ppermute | solution.py:258
  26.3 4.9 %collective-permute-start.14 = (bf16[512,128]{1,0:T(8,128)(2,1)S(1)}, bf16[512,128]{1,0:T(8,128)(2,1)S(1)}, u32[]{:S(2)}, u32[]{:S(2)}) collective-permute-start(bf16[512,128]{1,0:T(8,128)(2,1)S(1)} %collective-permute-done.8.refs_3_), channel_id=1, source_target_pairs={{0,16},{8,24},{16,0},{24,8},{1,17},{9,25},{17,1},{25,9},{2,18},{10... | collective-permute-start | bytes 393224 | tf_op jit(solution)/shard_map/ppermute | solution.py:258
  28.6 4.9 %collective-permute-start.5 = (bf16[512,128]{1,0:T(8,128)(2,1)S(1)}, bf16[512,128]{1,0:T(8,128)(2,1)S(1)}, u32[]{:S(2)}, u32[]{:S(2)}) collective-permute-start(bf16[512,128]{1,0:T(8,128)(2,1)S(1)} %collective-permute-done.4.second_ref.refs_3_), channel_id=1, source_target_pairs={{0,4},{4,0},{1,5},{5,1},{2,6},{6,2},{3,7},{7,3},{8,12},{12,8},{9,1... | collective-permute-start | bytes 393224 | tf_op jit(solution)/shard_map/ppermute | solution.py:258
  31.2 2.4 %collective-permute-start.15 = (bf16[512,128]{1,0:T(8,128)(2,1)S(1)}, bf16[512,128]{1,0:T(8,128)(2,1)S(1)}, u32[]{:S(2)}, u32[]{:S(2)}) collective-permute-start(bf16[512,128]{1,0:T(8,128)(2,1)S(1)} %collective-permute-done.14.refs_8_), channel_id=1, source_target_pairs={{0,8},{8,0},{16,24},{24,16},{1,9},{9,1},{17,25},{25,17},{2,10},{10... | collective-permute-start | bytes 393224 | tf_op jit(solution)/shard_map/ppermute | solution.py:258
  32.3 1.3 %copy-start.6 = (f32[128]{0:T(128)S(1)}, f32[128]{0:T(128)}, u32[]{:S(2)}) copy-start(f32[128]{0:T(128)} %param.13) | copy-start | bytes 1540
  36.6 7.9 %copy-start.5 = (f32[512]{0:T(512)S(1)}, f32[512]{0:T(512)}, u32[]{:S(2)}) copy-start(f32[512]{0:T(512)} %param.17) | copy-start | bytes 6148
  36.7 7.9 %copy-start.7 = (f32[128]{0:T(128)S(1)}, f32[128]{0:T(128)}, u32[]{:S(2)}) copy-start(f32[128]{0:T(128)} %param.19) | copy-start | bytes 1540
  36.7 7.9 %copy-start.8 = (f32[128]{0:T(128)S(1)}, f32[128]{0:T(128)}, u32[]{:S(2)}) copy-start(f32[128]{0:T(128)} %param.15) | copy-start | bytes 1540
  36.7 25.2 %copy-start = (bf16[16,128,128]{2,1,0:T(8,128)(2,1)S(1)}, bf16[16,128,128]{2,1,0:T(8,128)(2,1)}, u32[]{:S(2)}) copy-start(bf16[16,128,128]{2,1,0:T(8,128)(2,1)} %refs_1_.1) | copy-start | bytes 1572868
  36.7 25.2 %copy-start.2 = (bf16[512,128]{1,0:T(8,128)(2,1)S(1)}, bf16[512,128]{1,0:T(8,128)(2,1)}, u32[]{:S(2)}) copy-start(bf16[512,128]{1,0:T(8,128)(2,1)} %refs_10_.1) | copy-start | bytes 393220
  39.8 22.1 %copy-start.1 = (bf16[128,512]{1,0:T(8,128)(2,1)S(1)}, bf16[128,512]{1,0:T(8,128)(2,1)}, u32[]{:S(2)}) copy-start(bf16[128,512]{1,0:T(8,128)(2,1)} %refs_9_.1) | copy-start | bytes 393220
  39.8 14.4 %collective-permute-start.16 = (bf16[32,16,128]{2,1,0:T(8,128)(2,1)S(1)}, bf16[32,16,128]{2,1,0:T(8,128)(2,1)S(1)}, u32[]{:S(2)}, u32[]{:S(2)}) collective-permute-start(bf16[32,16,128]{2,1,0:T(8,128)(2,1)S(1)} %get-tuple-element.21), channel_id=1, source_target_pairs={{0,0},{1,1},{2,2},{3,3},{4,16},{5,17},{6,18},{7,19},{8,10},{9,11},... | collective-permute-start | bytes 393224 | tf_op jit(solution)/shard_map/ppermute | solution.py:382
  44.6 9.7 %collective-permute-start.17 = (bf16[32,16,128]{2,1,0:T(8,128)(2,1)S(1)}, bf16[32,16,128]{2,1,0:T(8,128)(2,1)S(1)}, u32[]{:S(2)}, u32[]{:S(2)}) collective-permute-start(bf16[32,16,128]{2,1,0:T(8,128)(2,1)S(1)} %get-tuple-element.22), channel_id=1, source_target_pairs={{0,2},{1,3},{2,0},{3,1},{4,6},{5,7},{6,4},{7,5},{8,8},{9,9},{10,10... | collective-permute-start | bytes 393224 | tf_op jit(solution)/shard_map/ppermute | solution.py:382
  48.3 8.8 %collective-permute-start.18 = (bf16[32,16,128]{2,1,0:T(8,128)(2,1)S(1)}, bf16[32,16,128]{2,1,0:T(8,128)(2,1)S(1)}, u32[]{:S(2)}, u32[]{:S(2)}) collective-permute-start(bf16[32,16,128]{2,1,0:T(8,128)(2,1)S(1)} %get-tuple-element.23), channel_id=1, source_target_pairs={{0,1},{1,0},{2,3},{3,2},{4,17},{5,16},{6,19},{7,18},{8,10},{9,11},... | collective-permute-start | bytes 393224 | tf_op jit(solution)/shard_map/ppermute | solution.py:382
  48.4 8.7 %collective-permute-start.19 = (bf16[32,16,128]{2,1,0:T(8,128)(2,1)S(1)}, bf16[32,16,128]{2,1,0:T(8,128)(2,1)S(1)}, u32[]{:S(2)}, u32[]{:S(2)}) collective-permute-start(bf16[32,16,128]{2,1,0:T(8,128)(2,1)S(1)} %get-tuple-element.24), channel_id=1, source_target_pairs={{0,2},{1,3},{2,0},{3,1},{4,6},{5,7},{6,4},{7,5},{8,9},{9,8},{10,11... | collective-permute-start | bytes 393224 | tf_op jit(solution)/shard_map/ppermute | solution.py:382
  50.8 9.1 %collective-permute-start.20 = (bf16[32,16,128]{2,1,0:T(8,128)(2,1)S(1)}, bf16[32,16,128]{2,1,0:T(8,128)(2,1)S(1)}, u32[]{:S(2)}, u32[]{:S(2)}) collective-permute-start(bf16[32,16,128]{2,1,0:T(8,128)(2,1)S(1)} %get-tuple-element.25), channel_id=1, source_target_pairs={{0,8},{1,9},{2,10},{3,11},{4,24},{5,25},{6,26},{7,27},{8,0},{9,1},... | collective-permute-start | bytes 393224 | tf_op jit(solution)/shard_map/ppermute | solution.py:382
  54.2 7.7 %collective-permute-start.21 = (bf16[32,16,128]{2,1,0:T(8,128)(2,1)S(1)}, bf16[32,16,128]{2,1,0:T(8,128)(2,1)S(1)}, u32[]{:S(2)}, u32[]{:S(2)}) collective-permute-start(bf16[32,16,128]{2,1,0:T(8,128)(2,1)S(1)} %get-tuple-element.26), channel_id=1, source_target_pairs={{0,9},{1,8},{2,11},{3,10},{4,25},{5,24},{6,27},{7,26},{8,1},{9,0},... | collective-permute-start | bytes 393224 | tf_op jit(solution)/shard_map/ppermute | solution.py:382

commit v5 on v3

--- a/solution.py
+++ b/solution.py
@@ -21,6 +21,7 @@
     data_refs = [refs.pop(0) for _ in range(data_count)]
     bias_ref, weight_ref = refs.pop(0), refs.pop(0)
     first_ref = refs.pop(0)
+    refs = refs[1:] if last else refs
     update_ref = refs.pop() if last else refs[0]
     outer_ref = refs.pop()
     lhs_ref = refs.pop()
@@ -296,7 +297,8 @@
     for dy in range(1, cols):
         shares[dy - 1] += [swap(value, "col", cols, dy) for value in fars]
     far_shares = [pair[1] for pair in shares]
-    far_tile = arrived(*fars, 32 * (share_rows * groups * group_len) * groups * group_len // 4)
+    far_tile = arrived(*fars, 10 * (share_rows * groups * group_len) * groups * group_len)
+    share_tile = arrived(shares[0][1], shares[0][-1], 4 * (share_rows * groups * group_len) * groups * group_len)
     data = []
     right_places = {dz: [] for dz in range(groups)}
     order = (0, 1, low + 1, low)
@@ -360,7 +362,7 @@
     outs = update_call(
         True,
         last_lefts,
-        [first],
+        [first, share_tile],
         [jax.ShapeDtypeStruct((run, half, pair_channels), bf16)]
         + [jax.ShapeDtypeStruct((2 * run, run, pair_channels), bf16)] * (4 + low),
         [vmem] * (5 + low),

time: 64.6 us -> 66.6 us (1.031)
  local copies, waits for them, and re-layouts: 2.76 us -> 4.41 us
    ppermute x16, starting transfers between devices: 19.2 us -> 21.1 us  [swap(): return lax.ppermute(value, name, [(i, i ^ flip) for i in range(size)])]
    ppermute x6, starting transfers between devices: 13.6 us -> 12.3 us  [exchange(): return lax.ppermute(outs[1 + slot], axes, pairs)]
    ppermute x16, waiting for transfers between devices: 10.6 us -> 9.43 us  [swap(): return lax.ppermute(value, name, [(i, i ^ flip) for i in range(size)])]
    reshape x1, local copies, waits for them, and re-layouts: 0.14 us -> 1.09 us  [on_device(): weight = weight.reshape(2 * pair_channels, channels * channels // 2)]
    ppermute x6, waiting for transfers between devices: 6.31 us -> 7.16 us  [exchange(): return lax.ppermute(outs[1 + slot], axes, pairs)]
    unnamed x20, local copies, waits for them, and re-layouts: 1.23 us -> 1.94 us
  transfers between devices with their start and end apart: 22 -> 22, of which waited for: 7 -> 9; matrix products, arithmetic and copies ran while one was open for 3% -> 5% of each run, Pallas kernels for 5% -> 0%
where the time goes in v5:
time: 66.6 us; the launch traced here: 65.6 us
  starting transfers between devices  33.4 us (50%)
  waiting for transfers between devices  16.6 us (25%)
  Pallas kernels  10.2 us (15%)
  local copies, waits for them, and re-layouts  4.41 us (7%)
    ppermute x16, starting transfers between devices, swap(): return lax.ppermute(value, name, [(i, i ^ flip) for i in range(size)])  21.1 us
    ppermute x6, starting transfers between devices, exchange(): return lax.ppermute(outs[1 + slot], axes, pairs)  12.3 us
    ppermute x16, waiting for transfers between devices, swap(): return lax.ppermute(value, name, [(i, i ^ flip) for i in range(size)])  9.43 us
    ppermute x6, waiting for transfers between devices, exchange(): return lax.ppermute(outs[1 + slot], axes, pairs)  7.16 us
    pallas_call x2, Pallas kernels, update_call(): pl.pallas_call(functools.partial(update_kernel, places, cols, low, last,...  6.09 us
    pallas_call x1, Pallas kernels, on_device(): pl.pallas_call(functools.partial(finish_kernel, low), out_shape=jax.Shape...  3.99 us
    unnamed x20, local copies, waits for them, and re-layouts  1.94 us
  transfers between devices with their start and end apart: 22, of which 9 were waited for; matrix products, arithmetic and copies ran while one was open for 5% of the time, Pallas kernels for 0%

profile of v5, /device:TPU:3, one launch (start us, length us, event | category | flops | bytes accessed | tf_op | source)
XLA Modules:
  0.0 65.6 jit_solution(9186866346133134341)
XLA Ops:
  0.0 1.1 %copy.18 = bf16[128,8,128]{0,2,1:T(8,128)(2,1)S(1)} copy(bf16[128,8,128]{2,1,0:T(8,128)(2,1)} %param.11) | data formatting | bytes 524288 | tf_op args[1]
  1.2 0.2 copy.19
  1.4 0.1 reshape.55
  1.5 0.1 copy.20
  1.7 0.1 collective-permute-start.10
  1.7 1.5 %collective-permute-start.6 = (bf16[512,128]{1,0:T(8,128)(2,1)S(1)}, bf16[512,128]{1,0:T(8,128)(2,1)S(1)}, u32[]{:S(2)}, u32[]{:S(2)}) collective-permute-start(bf16[512,128]{1,0:T(8,128)(2,1)S(1)} %bitcast.46), channel_id=1, source_target_pairs={{0,1},{1,0},{2,3},{3,2},{4,5},{5,4},{6,7},{7,6},{8,9},{9,8},{10,11... | collective-permute-start | bytes 393224 | tf_op jit(solution)/shard_map/ppermute | solution.py:264
  3.3 0.3 copy.17
  3.7 0.6 collective-permute-start
  4.3 0.1 copy.21
  4.4 3.0 %collective-permute-start.7 = (bf16[512,128]{1,0:T(8,128)(2,1)S(1)}, bf16[512,128]{1,0:T(8,128)(2,1)S(1)}, u32[]{:S(2)}, u32[]{:S(2)}) collective-permute-start(bf16[512,128]{1,0:T(8,128)(2,1)S(1)} %bitcast.54), channel_id=1, source_target_pairs={{0,3},{1,2},{2,1},{3,0},{4,7},{5,6},{6,5},{7,4},{8,11},{9,10},{10,... | collective-permute-start | bytes 393224 | tf_op jit(solution)/shard_map/ppermute | solution.py:264
  7.4 0.2 constant_dynamic-slice_fusion.3
  7.6 1.3 %collective-permute-start.11 = (bf16[512,128]{1,0:T(8,128)(2,1)S(1)}, bf16[512,128]{1,0:T(8,128)(2,1)S(1)}, u32[]{:S(2)}, u32[]{:S(2)}) collective-permute-start(bf16[512,128]{1,0:T(8,128)(2,1)S(1)} %collective-permute-done.6.refs_1_), channel_id=1, source_target_pairs={{0,16},{8,24},{16,0},{24,8},{1,17},{9,25},{17,1},{25,9},{2,18},{10... | collective-permute-start | bytes 393224 | tf_op jit(solution)/shard_map/ppermute | solution.py:264
  8.9 0.3 collective-permute-done.refs_1_
  9.2 1.3 %collective-permute-start.1 = (bf16[1024,128]{1,0:T(8,128)(2,1)S(1)}, bf16[1024,128]{1,0:T(8,128)(2,1)S(1)}, u32[]{:S(2)}, u32[]{:S(2)}) collective-permute-start(bf16[1024,128]{1,0:T(8,128)(2,1)S(1)} %pack.3.refs_1_), channel_id=1, source_target_pairs={{0,4},{4,0},{1,5},{5,1},{2,6},{6,2},{3,7},{7,3},{8,12},{12,8},{9,1... | collective-permute-start | bytes 786440 | tf_op jit(solution)/shard_map/ppermute | solution.py:264
  10.6 3.5 %collective-permute-done.7.refs_2_ = bf16[512,128]{1,0:T(8,128)(2,1)S(1)} collective-permute-done((bf16[512,128]{1,0:T(8,128)(2,1)S(1)}, bf16[512,128]{1,0:T(8,128)(2,1)S(1)}, u32[]{:S(2)}, u32[]{:S(2)}) %collective-permute-start.7) | collective-permute-done | bytes 131104 | tf_op jit(solution)/shard_map/ppermute | solution.py:264
  14.1 0.1 copy_bitcast_fusion.1
  14.2 1.2 %collective-permute-start.4 = (bf16[512,128]{1,0:T(8,128)(2,1)S(1)}, bf16[512,128]{1,0:T(8,128)(2,1)S(1)}, u32[]{:S(2)}, u32[]{:S(2)}) collective-permute-start(bf16[512,128]{1,0:T(8,128)(2,1)S(1)} %collective-permute-done.refs_1_), channel_id=1, source_target_pairs={{0,2},{1,3},{2,0},{3,1},{4,6},{5,7},{6,4},{7,5},{8,10},{9,11},{10,... | collective-permute-start | bytes 393224 | tf_op jit(solution)/shard_map/ppermute | solution.py:264
  15.4 2.5 %collective-permute-start.12 = (bf16[512,128]{1,0:T(8,128)(2,1)S(1)}, bf16[512,128]{1,0:T(8,128)(2,1)S(1)}, u32[]{:S(2)}, u32[]{:S(2)}) collective-permute-start(bf16[512,128]{1,0:T(8,128)(2,1)S(1)} %collective-permute-done.7.refs_2_), channel_id=1, source_target_pairs={{0,16},{8,24},{16,0},{24,8},{1,17},{9,25},{17,1},{25,9},{2,18},{10... | collective-permute-start | bytes 393224 | tf_op jit(solution)/shard_map/ppermute | solution.py:264
  17.8 1.7 %collective-permute-done.8.refs_3_ = bf16[512,128]{1,0:T(8,128)(2,1)S(1)} collective-permute-done((bf16[512,128]{1,0:T(8,128)(2,1)S(1)}, bf16[512,128]{1,0:T(8,128)(2,1)S(1)}, u32[]{:S(2)}, u32[]{:S(2)}) %collective-permute-start.8) | collective-permute-done | bytes 131104 | tf_op jit(solution)/shard_map/ppermute | solution.py:264
  19.6 5.2 %collective-permute-start.9 = (bf16[2048,128]{1,0:T(8,128)(2,1)S(1)}, bf16[2048,128]{1,0:T(8,128)(2,1)S(1)}, u32[]{:S(2)}, u32[]{:S(2)}) collective-permute-start(bf16[2048,128]{1,0:T(8,128)(2,1)S(1)} %pack.4.refs_4_), channel_id=1, source_target_pairs={{0,8},{8,0},{16,24},{24,16},{1,9},{9,1},{17,25},{25,17},{2,10},{10... | collective-permute-start | bytes 1572872 | tf_op jit(solution)/shard_map/ppermute | solution.py:264
  24.8 0.1 copy_bitcast_fusion.3
  24.9 1.3 %collective-permute-start.3 = (bf16[512,128]{1,0:T(8,128)(2,1)S(1)}, bf16[512,128]{1,0:T(8,128)(2,1)S(1)}, u32[]{:S(2)}, u32[]{:S(2)}) collective-permute-start(bf16[512,128]{1,0:T(8,128)(2,1)S(1)} %collective-permute-done.2.first_ref.refs_2_), channel_id=1, source_target_pairs={{0,4},{4,0},{1,5},{5,1},{2,6},{6,2},{3,7},{7,3},{8,12},{12,8},{9,1... | collective-permute-start | bytes 393224 | tf_op jit(solution)/shard_map/ppermute | solution.py:264
  26.2 1.2 %collective-permute-start.14 = (bf16[512,128]{1,0:T(8,128)(2,1)S(1)}, bf16[512,128]{1,0:T(8,128)(2,1)S(1)}, u32[]{:S(2)}, u32[]{:S(2)}) collective-permute-start(bf16[512,128]{1,0:T(8,128)(2,1)S(1)} %collective-permute-done.8.refs_3_), channel_id=1, source_target_pairs={{0,16},{8,24},{16,0},{24,8},{1,17},{9,25},{17,1},{25,9},{2,18},{10... | collective-permute-start | bytes 393224 | tf_op jit(solution)/shard_map/ppermute | solution.py:264
  27.5 0.6 collective-permute-start.13
  28.1 0.5 pad_maximum_fusion
  28.6 0.7 %copy.38 = bf16[64,8,2,128]{3,1,2,0:T(8,128)(2,1)} copy(bf16[64,8,2,128]{3,2,1,0:T(2,128)(2,1)S(1)} %bitcast.49) | data formatting | bytes 524288
  29.3 1.1 %copy.27.refs_11_ = bf16[256,512]{1,0:T(8,128)(2,1)S(1)} copy(bf16[256,512]{0,1:T(8,128)(2,1)} %bitcast.50) | data formatting | bytes 524288 | tf_op jit(solution)/shard_map/reshape | solution.py:287
  30.4 0.1 collective-permute-start.5
  30.5 0.5 collective-permute-done.14.refs_8_
  31.0 1.1 %collective-permute-start.15 = (bf16[512,128]{1,0:T(8,128)(2,1)S(1)}, bf16[512,128]{1,0:T(8,128)(2,1)S(1)}, u32[]{:S(2)}, u32[]{:S(2)}) collective-permute-start(bf16[512,128]{1,0:T(8,128)(2,1)S(1)} %collective-permute-done.14.refs_8_), channel_id=1, source_target_pairs={{0,8},{8,0},{16,24},{24,16},{1,9},{9,1},{17,25},{25,17},{2,10},{10... | collective-permute-start | bytes 393224 | tf_op jit(solution)/shard_map/ppermute | solution.py:264
  32.1 0.1 pad_add_fusion.refs_0_
  32.2 3.4 %collective-permute-done.5.second_ref.refs_3_ = bf16[512,128]{1,0:T(8,128)(2,1)S(1)} collective-permute-done((bf16[512,128]{1,0:T(8,128)(2,1)S(1)}, bf16[512,128]{1,0:T(8,128)(2,1)S(1)}, u32[]{:S(2)}, u32[]{:S(2)}) %collective-permute-start.5) | collective-permute-done | bytes 131104 | tf_op jit(solution)/shard_map/ppermute | solution.py:264
  35.6 0.1 broadcast_in_dim.2.refs_10_
  35.7 3.0 %update_first.1.refs_12_ = bf16[16,64,128]{2,1,0:T(8,128)(2,1)S(1)} custom-call(s32[4]{0:T(128)S(1)} %pad_add_fusion.refs_0_, bf16[1024,128]{1,0:T(8,128)(2,1)S(1)} %pack.3.refs_1_, bf16[512,128]{1,0:T(8,128)(2,1)S(1)} %collective-permute-done.2.first_ref.refs_2_, bf16[512,128]{1,0:T(8,128)(2,1)S(1)} %collective-permute-done.4.second_ref.refs_3_, ...), custom_call_target="tpu_custom_call" | custom-call | flops 1610612736 | bytes 2097152 | tf_op jit(solution)/shard_map/update_first/pallas_call | solution.py:340
  38.7 0.0 copy-start.7
  38.8 3.1 %update_last.1 = (bf16[16,64,128]{2,1,0:T(8,128)(2,1)S(1)}, bf16[32,16,128]{2,1,0:T(8,128)(2,1)S(1)}, bf16[32,16,128]{2,1,0:T(8,128)(2,1)S(1)}, bf16[32,16,128]{...) custom-call(s32[4]{0:T(128)S(1)} %pad_add_fusion.refs_0_, ...), custom_call_target="tpu_custom_call" | custom-call | flops 1610612736 | bytes 2097152 | tf_op jit(solution)/shard_map/update_last/pallas_call | solution.py:340
  41.9 2.2 %collective-permute-start.16 = (bf16[32,16,128]{2,1,0:T(8,128)(2,1)S(1)}, bf16[32,16,128]{2,1,0:T(8,128)(2,1)S(1)}, u32[]{:S(2)}, u32[]{:S(2)}) collective-permute-start(bf16[32,16,128]{2,1,0:T(8,128)(2,1)S(1)} %get-tuple-element.21), channel_id=1, source_target_pairs={{0,0},{1,1},{2,2},{3,3},{4,16},{5,17},{6,18},{7,19},{8,10},{9,11},... | collective-permute-start | bytes 393224 | tf_op jit(solution)/shard_map/ppermute | solution.py:388
  44.1 2.6 %collective-permute-start.17 = (bf16[32,16,128]{2,1,0:T(8,128)(2,1)S(1)}, bf16[32,16,128]{2,1,0:T(8,128)(2,1)S(1)}, u32[]{:S(2)}, u32[]{:S(2)}) collective-permute-start(bf16[32,16,128]{2,1,0:T(8,128)(2,1)S(1)} %get-tuple-element.22), channel_id=1, source_target_pairs={{0,2},{1,3},{2,0},{3,1},{4,6},{5,7},{6,4},{7,5},{8,8},{9,9},{10,10... | collective-permute-start | bytes 393224 | tf_op jit(solution)/shard_map/ppermute | solution.py:388
  46.7 1.8 %collective-permute-start.18 = (bf16[32,16,128]{2,1,0:T(8,128)(2,1)S(1)}, bf16[32,16,128]{2,1,0:T(8,128)(2,1)S(1)}, u32[]{:S(2)}, u32[]{:S(2)}) collective-permute-start(bf16[32,16,128]{2,1,0:T(8,128)(2,1)S(1)} %get-tuple-element.23), channel_id=1, source_target_pairs={{0,1},{1,0},{2,3},{3,2},{4,17},{5,16},{6,19},{7,18},{8,10},{9,11},... | collective-permute-start | bytes 393224 | tf_op jit(solution)/shard_map/ppermute | solution.py:388
  48.6 2.4 %collective-permute-start.19 = (bf16[32,16,128]{2,1,0:T(8,128)(2,1)S(1)}, bf16[32,16,128]{2,1,0:T(8,128)(2,1)S(1)}, u32[]{:S(2)}, u32[]{:S(2)}) collective-permute-start(bf16[32,16,128]{2,1,0:T(8,128)(2,1)S(1)} %get-tuple-element.24), channel_id=1, source_target_pairs={{0,2},{1,3},{2,0},{3,1},{4,6},{5,7},{6,4},{7,5},{8,9},{9,8},{10,11... | collective-permute-start | bytes 393224 | tf_op jit(solution)/shard_map/ppermute | solution.py:388
  50.9 3.1 %collective-permute-start.20 = (bf16[32,16,128]{2,1,0:T(8,128)(2,1)S(1)}, bf16[32,16,128]{2,1,0:T(8,128)(2,1)S(1)}, u32[]{:S(2)}, u32[]{:S(2)}) collective-permute-start(bf16[32,16,128]{2,1,0:T(8,128)(2,1)S(1)} %get-tuple-element.25), channel_id=1, source_target_pairs={{0,8},{1,9},{2,10},{3,11},{4,24},{5,25},{6,26},{7,27},{8,0},{9,1},... | collective-permute-start | bytes 393224 | tf_op jit(solution)/shard_map/ppermute | solution.py:388
  54.1 0.2 collective-permute-start.21
  54.3 0.1 fusion.refs_12_
  54.4 0.5 collective-permute-done.18.refs_5_
  54.9 1.2 %collective-permute-done.19.refs_6_ = bf16[32,16,128]{2,1,0:T(8,128)(2,1)S(1)} collective-permute-done((bf16[32,16,128]{2,1,0:T(8,128)(2,1)S(1)}, bf16[32,16,128]{2,1,0:T(8,128)(2,1)S(1)}, u32[]{:S(2)}, u32[]{:S(2)}) %collective-permute-start.19) | collective-permute-done | bytes 131104 | tf_op jit(solution)/shard_map/ppermute | solution.py:388
  56.1 2.3 %collective-permute-done.20.refs_7_ = bf16[32,16,128]{2,1,0:T(8,128)(2,1)S(1)} collective-permute-done((bf16[32,16,128]{2,1,0:T(8,128)(2,1)S(1)}, bf16[32,16,128]{2,1,0:T(8,128)(2,1)S(1)}, u32[]{:S(2)}, u32[]{:S(2)}) %collective-permute-start.20) | collective-permute-done | bytes 131104 | tf_op jit(solution)/shard_map/ppermute | solution.py:388
  58.4 3.1 %collective-permute-done.21.refs_8_ = bf16[32,16,128]{2,1,0:T(8,128)(2,1)S(1)} collective-permute-done((bf16[32,16,128]{2,1,0:T(8,128)(2,1)S(1)}, bf16[32,16,128]{2,1,0:T(8,128)(2,1)S(1)}, u32[]{:S(2)}, u32[]{:S(2)}) %collective-permute-start.21) | collective-permute-done | bytes 131104 | tf_op jit(solution)/shard_map/ppermute | solution.py:388
  61.6 4.0 %finish.1 = bf16[16,128,128]{2,1,0:T(8,128)(2,1)} custom-call(s32[4]{0:T(128)S(1)} %pad_add_fusion.refs_0_, bf16[16,128,128]{2,1,0:T(8,128)(2,1)S(1)} %copy-done, bf16[16,64,128]{2,1,0:T(8,128)(2,1)S(1)} %get-tuple-element.20.refs_2_, bf16[32,16,128]{2,1,0:T(8,128)(2,1)S(1)} %collective-permute-done.16.refs_3_, ...), custom_call_target="tpu_custom_call" | custom-call | tf_op jit(solution)/shard_map/finish/pallas_call | solution.py:393
  (42 shorter events, 0.2 us)
Async XLA Ops:
  1.5 1.8 %copy-start.3 = (bf16[128,32,64]{0,2,1:T(8,128)(2,1)S(1)}, bf16[128,32,64]{0,2,1:T(8,128)(2,1)}, u32[]{:S(2)}) copy-start(bf16[128,32,64]{0,2,1:T(8,128)(2,1)} %param.10) | copy-start | bytes 1572868
  1.7 6.0 %collective-permute-start.10 = (bf16[512,128]{1,0:T(8,128)(2,1)S(1)}, bf16[512,128]{1,0:T(8,128)(2,1)S(1)}, u32[]{:S(2)}, u32[]{:S(2)}) collective-permute-start(bf16[512,128]{1,0:T(8,128)(2,1)S(1)} %bitcast.45), channel_id=1, source_target_pairs={{0,16},{8,24},{16,0},{24,8},{1,17},{9,25},{17,1},{25,9},{2,18},{10... | collective-permute-start | bytes 393224 | tf_op jit(solution)/shard_map/ppermute | solution.py:264
  1.7 5.9 %collective-permute-start.6 = (bf16[512,128]{1,0:T(8,128)(2,1)S(1)}, bf16[512,128]{1,0:T(8,128)(2,1)S(1)}, u32[]{:S(2)}, u32[]{:S(2)}) collective-permute-start(bf16[512,128]{1,0:T(8,128)(2,1)S(1)} %bitcast.46), channel_id=1, source_target_pairs={{0,1},{1,0},{2,3},{3,2},{4,5},{5,4},{6,7},{7,6},{8,9},{9,8},{10,11... | collective-permute-start | bytes 393224 | tf_op jit(solution)/shard_map/ppermute | solution.py:264
  3.7 3.8 %copy-start.4 = (bf16[1024,128]{1,0:T(8,128)(2,1)S(1)}, bf16[1024,128]{1,0:T(8,128)(2,1)}, u32[]{:S(2)}) copy-start(bf16[1024,128]{1,0:T(8,128)(2,1)} %param.12) | copy-start | bytes 786436
  3.7 5.5 %collective-permute-start = (bf16[512,128]{1,0:T(8,128)(2,1)S(1)}, bf16[512,128]{1,0:T(8,128)(2,1)S(1)}, u32[]{:S(2)}, u32[]{:S(2)}) collective-permute-start(bf16[512,128]{1,0:T(8,128)(2,1)S(1)} %get-tuple-element.27), channel_id=1, source_target_pairs={{0,1},{1,0},{2,3},{3,2},{4,5},{5,4},{6,7},{7,6},{8,9},{9,8},{10,11... | collective-permute-start | bytes 393224 | tf_op jit(solution)/shard_map/ppermute | solution.py:264
  4.4 9.7 %collective-permute-start.7 = (bf16[512,128]{1,0:T(8,128)(2,1)S(1)}, bf16[512,128]{1,0:T(8,128)(2,1)S(1)}, u32[]{:S(2)}, u32[]{:S(2)}) collective-permute-start(bf16[512,128]{1,0:T(8,128)(2,1)S(1)} %bitcast.54), channel_id=1, source_target_pairs={{0,3},{1,2},{2,1},{3,0},{4,7},{5,6},{6,5},{7,4},{8,11},{9,10},{10,... | collective-permute-start | bytes 393224 | tf_op jit(solution)/shard_map/ppermute | solution.py:264
  7.4 17.5 %collective-permute-start.2 = (bf16[512,128]{1,0:T(8,128)(2,1)S(1)}, bf16[512,128]{1,0:T(8,128)(2,1)S(1)}, u32[]{:S(2)}, u32[]{:S(2)}) collective-permute-start(bf16[512,128]{1,0:T(8,128)(2,1)S(1)} %get-tuple-element.28.refs_0_), channel_id=1, source_target_pairs={{0,2},{1,3},{2,0},{3,1},{4,6},{5,7},{6,4},{7,5},{8,10},{9,11},{10,... | collective-permute-start | bytes 393224 | tf_op jit(solution)/shard_map/ppermute | solution.py:264
  7.6 7.7 %collective-permute-start.11 = (bf16[512,128]{1,0:T(8,128)(2,1)S(1)}, bf16[512,128]{1,0:T(8,128)(2,1)S(1)}, u32[]{:S(2)}, u32[]{:S(2)}) collective-permute-start(bf16[512,128]{1,0:T(8,128)(2,1)S(1)} %collective-permute-done.6.refs_1_), channel_id=1, source_target_pairs={{0,16},{8,24},{16,0},{24,8},{1,17},{9,25},{17,1},{25,9},{2,18},{10... | collective-permute-start | bytes 393224 | tf_op jit(solution)/shard_map/ppermute | solution.py:264
  9.2 17.0 %collective-permute-start.1 = (bf16[1024,128]{1,0:T(8,128)(2,1)S(1)}, bf16[1024,128]{1,0:T(8,128)(2,1)S(1)}, u32[]{:S(2)}, u32[]{:S(2)}) collective-permute-start(bf16[1024,128]{1,0:T(8,128)(2,1)S(1)} %pack.3.refs_1_), channel_id=1, source_target_pairs={{0,4},{4,0},{1,5},{5,1},{2,6},{6,2},{3,7},{7,3},{8,12},{12,8},{9,1... | collective-permute-start | bytes 786440 | tf_op jit(solution)/shard_map/ppermute | solution.py:264
  14.1 5.5 %collective-permute-start.8 = (bf16[512,128]{1,0:T(8,128)(2,1)S(1)}, bf16[512,128]{1,0:T(8,128)(2,1)S(1)}, u32[]{:S(2)}, u32[]{:S(2)}) collective-permute-start(bf16[512,128]{1,0:T(8,128)(2,1)S(1)} %collective-permute-done.7.refs_2_), channel_id=1, source_target_pairs={{0,1},{1,0},{2,3},{3,2},{4,5},{5,4},{6,7},{7,6},{8,9},{9,8},{10,11... | collective-permute-start | bytes 393224 | tf_op jit(solution)/shard_map/ppermute | solution.py:264
  14.2 16.2 %collective-permute-start.4 = (bf16[512,128]{1,0:T(8,128)(2,1)S(1)}, bf16[512,128]{1,0:T(8,128)(2,1)S(1)}, u32[]{:S(2)}, u32[]{:S(2)}) collective-permute-start(bf16[512,128]{1,0:T(8,128)(2,1)S(1)} %collective-permute-done.refs_1_), channel_id=1, source_target_pairs={{0,2},{1,3},{2,0},{3,1},{4,6},{5,7},{6,4},{7,5},{8,10},{9,11},{10,... | collective-permute-start | bytes 393224 | tf_op jit(solution)/shard_map/ppermute | solution.py:264
  15.4 10.9 %collective-permute-start.12 = (bf16[512,128]{1,0:T(8,128)(2,1)S(1)}, bf16[512,128]{1,0:T(8,128)(2,1)S(1)}, u32[]{:S(2)}, u32[]{:S(2)}) collective-permute-start(bf16[512,128]{1,0:T(8,128)(2,1)S(1)} %collective-permute-done.7.refs_2_), channel_id=1, source_target_pairs={{0,16},{8,24},{16,0},{24,8},{1,17},{9,25},{17,1},{25,9},{2,18},{10... | collective-permute-start | bytes 393224 | tf_op jit(solution)/shard_map/ppermute | solution.py:264
  19.6 16.0 %collective-permute-start.9 = (bf16[2048,128]{1,0:T(8,128)(2,1)S(1)}, bf16[2048,128]{1,0:T(8,128)(2,1)S(1)}, u32[]{:S(2)}, u32[]{:S(2)}) collective-permute-start(bf16[2048,128]{1,0:T(8,128)(2,1)S(1)} %pack.4.refs_4_), channel_id=1, source_target_pairs={{0,8},{8,0},{16,24},{24,16},{1,9},{9,1},{17,25},{25,17},{2,10},{10... | collective-permute-start | bytes 1572872 | tf_op jit(solution)/shard_map/ppermute | solution.py:264
  24.9 5.6 %collective-permute-start.3 = (bf16[512,128]{1,0:T(8,128)(2,1)S(1)}, bf16[512,128]{1,0:T(8,128)(2,1)S(1)}, u32[]{:S(2)}, u32[]{:S(2)}) collective-permute-start(bf16[512,128]{1,0:T(8,128)(2,1)S(1)} %collective-permute-done.2.first_ref.refs_2_), channel_id=1, source_target_pairs={{0,4},{4,0},{1,5},{5,1},{2,6},{6,2},{3,7},{7,3},{8,12},{12,8},{9,1... | collective-permute-start | bytes 393224 | tf_op jit(solution)/shard_map/ppermute | solution.py:264
  26.2 4.8 %collective-permute-start.14 = (bf16[512,128]{1,0:T(8,128)(2,1)S(1)}, bf16[512,128]{1,0:T(8,128)(2,1)S(1)}, u32[]{:S(2)}, u32[]{:S(2)}) collective-permute-start(bf16[512,128]{1,0:T(8,128)(2,1)S(1)} %collective-permute-done.8.refs_3_), channel_id=1, source_target_pairs={{0,16},{8,24},{16,0},{24,8},{1,17},{9,25},{17,1},{25,9},{2,18},{10... | collective-permute-start | bytes 393224 | tf_op jit(solution)/shard_map/ppermute | solution.py:264
  27.5 8.2 %collective-permute-start.13 = (bf16[1536,128]{1,0:T(8,128)(2,1)S(1)}, bf16[1536,128]{1,0:T(8,128)(2,1)S(1)}, u32[]{:S(2)}, u32[]{:S(2)}) collective-permute-start(bf16[1536,128]{1,0:T(8,128)(2,1)S(1)} %pack.5.refs_6_), channel_id=1, source_target_pairs={{0,8},{8,0},{16,24},{24,16},{1,9},{9,1},{17,25},{25,17},{2,10},{10... | collective-permute-start | bytes 1179656 | tf_op jit(solution)/shard_map/ppermute | solution.py:264
  30.4 5.2 %collective-permute-start.5 = (bf16[512,128]{1,0:T(8,128)(2,1)S(1)}, bf16[512,128]{1,0:T(8,128)(2,1)S(1)}, u32[]{:S(2)}, u32[]{:S(2)}) collective-permute-start(bf16[512,128]{1,0:T(8,128)(2,1)S(1)} %collective-permute-done.4.second_ref.refs_3_), channel_id=1, source_target_pairs={{0,4},{4,0},{1,5},{5,1},{2,6},{6,2},{3,7},{7,3},{8,12},{12,8},{9,1... | collective-permute-start | bytes 393224 | tf_op jit(solution)/shard_map/ppermute | solution.py:264
  31.0 4.6 %collective-permute-start.15 = (bf16[512,128]{1,0:T(8,128)(2,1)S(1)}, bf16[512,128]{1,0:T(8,128)(2,1)S(1)}, u32[]{:S(2)}, u32[]{:S(2)}) collective-permute-start(bf16[512,128]{1,0:T(8,128)(2,1)S(1)} %collective-permute-done.14.refs_8_), channel_id=1, source_target_pairs={{0,8},{8,0},{16,24},{24,16},{1,9},{9,1},{17,25},{25,17},{2,10},{10... | collective-permute-start | bytes 393224 | tf_op jit(solution)/shard_map/ppermute | solution.py:264
  32.2 3.4 %copy-start.6 = (f32[128]{0:T(128)S(1)}, f32[128]{0:T(128)}, u32[]{:S(2)}) copy-start(f32[128]{0:T(128)} %param.13) | copy-start | bytes 1540
  38.7 5.4 %copy-start.5 = (f32[512]{0:T(512)S(1)}, f32[512]{0:T(512)}, u32[]{:S(2)}) copy-start(f32[512]{0:T(512)} %param.17) | copy-start | bytes 6148
  38.7 5.4 %copy-start.7 = (f32[128]{0:T(128)S(1)}, f32[128]{0:T(128)}, u32[]{:S(2)}) copy-start(f32[128]{0:T(128)} %param.19) | copy-start | bytes 1540
  38.7 5.4 %copy-start.8 = (f32[128]{0:T(128)S(1)}, f32[128]{0:T(128)}, u32[]{:S(2)}) copy-start(f32[128]{0:T(128)} %param.15) | copy-start | bytes 1540
  38.7 22.8 %copy-start = (bf16[16,128,128]{2,1,0:T(8,128)(2,1)S(1)}, bf16[16,128,128]{2,1,0:T(8,128)(2,1)}, u32[]{:S(2)}) copy-start(bf16[16,128,128]{2,1,0:T(8,128)(2,1)} %refs_1_.1) | copy-start | bytes 1572868
  38.8 22.8 %copy-start.2 = (bf16[512,128]{1,0:T(8,128)(2,1)S(1)}, bf16[512,128]{1,0:T(8,128)(2,1)}, u32[]{:S(2)}) copy-start(bf16[512,128]{1,0:T(8,128)(2,1)} %refs_10_.1) | copy-start | bytes 393220
  41.9 19.7 %copy-start.1 = (bf16[128,512]{1,0:T(8,128)(2,1)S(1)}, bf16[128,512]{1,0:T(8,128)(2,1)}, u32[]{:S(2)}) copy-start(bf16[128,512]{1,0:T(8,128)(2,1)} %refs_9_.1) | copy-start | bytes 393220
  41.9 12.2 %collective-permute-start.16 = (bf16[32,16,128]{2,1,0:T(8,128)(2,1)S(1)}, bf16[32,16,128]{2,1,0:T(8,128)(2,1)S(1)}, u32[]{:S(2)}, u32[]{:S(2)}) collective-permute-start(bf16[32,16,128]{2,1,0:T(8,128)(2,1)S(1)} %get-tuple-element.21), channel_id=1, source_target_pairs={{0,0},{1,1},{2,2},{3,3},{4,16},{5,17},{6,18},{7,19},{8,10},{9,11},... | collective-permute-start | bytes 393224 | tf_op jit(solution)/shard_map/ppermute | solution.py:388
  44.1 10.2 %collective-permute-start.17 = (bf16[32,16,128]{2,1,0:T(8,128)(2,1)S(1)}, bf16[32,16,128]{2,1,0:T(8,128)(2,1)S(1)}, u32[]{:S(2)}, u32[]{:S(2)}) collective-permute-start(bf16[32,16,128]{2,1,0:T(8,128)(2,1)S(1)} %get-tuple-element.22), channel_id=1, source_target_pairs={{0,2},{1,3},{2,0},{3,1},{4,6},{5,7},{6,4},{7,5},{8,8},{9,9},{10,10... | collective-permute-start | bytes 393224 | tf_op jit(solution)/shard_map/ppermute | solution.py:388
  46.7 8.2 %collective-permute-start.18 = (bf16[32,16,128]{2,1,0:T(8,128)(2,1)S(1)}, bf16[32,16,128]{2,1,0:T(8,128)(2,1)S(1)}, u32[]{:S(2)}, u32[]{:S(2)}) collective-permute-start(bf16[32,16,128]{2,1,0:T(8,128)(2,1)S(1)} %get-tuple-element.23), channel_id=1, source_target_pairs={{0,1},{1,0},{2,3},{3,2},{4,17},{5,16},{6,19},{7,18},{8,10},{9,11},... | collective-permute-start | bytes 393224 | tf_op jit(solution)/shard_map/ppermute | solution.py:388
  48.6 7.5 %collective-permute-start.19 = (bf16[32,16,128]{2,1,0:T(8,128)(2,1)S(1)}, bf16[32,16,128]{2,1,0:T(8,128)(2,1)S(1)}, u32[]{:S(2)}, u32[]{:S(2)}) collective-permute-start(bf16[32,16,128]{2,1,0:T(8,128)(2,1)S(1)} %get-tuple-element.24), channel_id=1, source_target_pairs={{0,2},{1,3},{2,0},{3,1},{4,6},{5,7},{6,4},{7,5},{8,9},{9,8},{10,11... | collective-permute-start | bytes 393224 | tf_op jit(solution)/shard_map/ppermute | solution.py:388
  50.9 7.5 %collective-permute-start.20 = (bf16[32,16,128]{2,1,0:T(8,128)(2,1)S(1)}, bf16[32,16,128]{2,1,0:T(8,128)(2,1)S(1)}, u32[]{:S(2)}, u32[]{:S(2)}) collective-permute-start(bf16[32,16,128]{2,1,0:T(8,128)(2,1)S(1)} %get-tuple-element.25), channel_id=1, source_target_pairs={{0,8},{1,9},{2,10},{3,11},{4,24},{5,25},{6,26},{7,27},{8,0},{9,1},... | collective-permute-start | bytes 393224 | tf_op jit(solution)/shard_map/ppermute | solution.py:388
  54.1 7.5 %collective-permute-start.21 = (bf16[32,16,128]{2,1,0:T(8,128)(2,1)S(1)}, bf16[32,16,128]{2,1,0:T(8,128)(2,1)S(1)}, u32[]{:S(2)}, u32[]{:S(2)}) collective-permute-start(bf16[32,16,128]{2,1,0:T(8,128)(2,1)S(1)} %get-tuple-element.26), channel_id=1, source_target_pairs={{0,9},{1,8},{2,11},{3,10},{4,25},{5,24},{6,27},{7,26},{8,1},{9,0},... | collective-permute-start | bytes 393224 | tf_op jit(solution)/shard_map/ppermute | solution.py:388

commit v6 on v3

--- a/solution.py
+++ b/solution.py
@@ -304,7 +304,7 @@
     last = ()
     for dz in order:
         for dx in range(1, xs):
-            behind = last + ((near_shares,) if dz == low else ())
+            behind = last + ((near_shares, bias) if dz == low else ())
             crosses[dz].append(swap(after(blocks[dz], *behind), "row", rows, 2 * dx))
             last = (crosses[dz][-1],)
     for position in range(xs):

time: 64.6 us -> 66.3 us (1.026)
  local copies, waits for them, and re-layouts: 2.76 us -> 4.4 us
    reshape x1, local copies, waits for them, and re-layouts: 0.14 us -> 1.09 us  [on_device(): weight = weight.reshape(2 * pair_channels, channels * channels // 2)]
    unnamed x20, local copies, waits for them, and re-layouts: 1.23 us -> 1.93 us
  transfers between devices with their start and end apart: 22 -> 22, of which waited for: 7 -> 7; matrix products, arithmetic and copies ran while one was open for 3% -> 5% of each run, Pallas kernels for 5% -> 5%
where the time goes in v6:
time: 66.3 us; the launch traced here: 65.3 us
  starting transfers between devices  32.8 us (49%)
  waiting for transfers between devices  17 us (26%)
  Pallas kernels  10.2 us (15%)
  local copies, waits for them, and re-layouts  4.4 us (7%)
    ppermute x16, starting transfers between devices, swap(): return lax.ppermute(value, name, [(i, i ^ flip) for i in range(size)])  19.2 us
    ppermute x6, starting transfers between devices, exchange(): return lax.ppermute(outs[1 + slot], axes, pairs)  13.6 us
    ppermute x16, waiting for transfers between devices, swap(): return lax.ppermute(value, name, [(i, i ^ flip) for i in range(size)])  10.7 us
    ppermute x6, waiting for transfers between devices, exchange(): return lax.ppermute(outs[1 + slot], axes, pairs)  6.29 us
    pallas_call x2, Pallas kernels, update_call(): pl.pallas_call(functools.partial(update_kernel, places, cols, low, last,...  6.08 us
    pallas_call x1, Pallas kernels, on_device(): pl.pallas_call(functools.partial(finish_kernel, low), out_shape=jax.Shape...  3.99 us
    unnamed x20, local copies, waits for them, and re-layouts  1.93 us
  transfers between devices with their start and end apart: 22, of which 7 were waited for; matrix products, arithmetic and copies ran while one was open for 5% of the time, Pallas kernels for 5%

profile of v6, /device:TPU:3, one launch (start us, length us, event | category | flops | bytes accessed | tf_op | source)
XLA Modules:
  0.0 65.3 jit_solution(9080516610531213982)
XLA Ops:
  0.0 1.1 %copy.18 = bf16[128,8,128]{0,2,1:T(8,128)(2,1)S(1)} copy(bf16[128,8,128]{2,1,0:T(8,128)(2,1)} %param.11) | data formatting | bytes 524288 | tf_op args[1]
  1.2 0.2 copy.19
  1.4 0.1 reshape.55
  1.5 0.0 copy-start.3
  1.5 0.1 copy.20
  1.7 0.1 collective-permute-start.10
  1.7 1.5 %collective-permute-start.6 = (bf16[512,128]{1,0:T(8,128)(2,1)S(1)}, bf16[512,128]{1,0:T(8,128)(2,1)S(1)}, u32[]{:S(2)}, u32[]{:S(2)}) collective-permute-start(bf16[512,128]{1,0:T(8,128)(2,1)S(1)} %bitcast.46), channel_id=1, source_target_pairs={{0,1},{1,0},{2,3},{3,2},{4,5},{5,4},{6,7},{7,6},{8,9},{9,8},{10,11... | collective-permute-start | bytes 393224 | tf_op jit(solution)/shard_map/ppermute | solution.py:263
  3.3 0.3 copy.17
  3.7 0.6 collective-permute-start
  4.3 0.1 copy.21
  4.4 3.0 %collective-permute-start.7 = (bf16[512,128]{1,0:T(8,128)(2,1)S(1)}, bf16[512,128]{1,0:T(8,128)(2,1)S(1)}, u32[]{:S(2)}, u32[]{:S(2)}) collective-permute-start(bf16[512,128]{1,0:T(8,128)(2,1)S(1)} %bitcast.54), channel_id=1, source_target_pairs={{0,3},{1,2},{2,1},{3,0},{4,7},{5,6},{6,5},{7,4},{8,11},{9,10},{10,... | collective-permute-start | bytes 393224 | tf_op jit(solution)/shard_map/ppermute | solution.py:263
  7.4 1.2 %collective-permute-start.11 = (bf16[512,128]{1,0:T(8,128)(2,1)S(1)}, bf16[512,128]{1,0:T(8,128)(2,1)S(1)}, u32[]{:S(2)}, u32[]{:S(2)}) collective-permute-start(bf16[512,128]{1,0:T(8,128)(2,1)S(1)} %collective-permute-done.6.refs_1_), channel_id=1, source_target_pairs={{0,16},{8,24},{16,0},{24,8},{1,17},{9,25},{17,1},{25,9},{2,18},{10... | collective-permute-start | bytes 393224 | tf_op jit(solution)/shard_map/ppermute | solution.py:263
  8.6 1.0 %collective-permute-start.2 = (bf16[512,128]{1,0:T(8,128)(2,1)S(1)}, bf16[512,128]{1,0:T(8,128)(2,1)S(1)}, u32[]{:S(2)}, u32[]{:S(2)}) collective-permute-start(bf16[512,128]{1,0:T(8,128)(2,1)S(1)} %get-tuple-element.28.refs_0_), channel_id=1, source_target_pairs={{0,2},{1,3},{2,0},{3,1},{4,6},{5,7},{6,4},{7,5},{8,10},{9,11},{10,... | collective-permute-start | bytes 393224 | tf_op jit(solution)/shard_map/ppermute | solution.py:263
  9.6 1.3 %collective-permute-start.1 = (bf16[1024,128]{1,0:T(8,128)(2,1)S(1)}, bf16[1024,128]{1,0:T(8,128)(2,1)S(1)}, u32[]{:S(2)}, u32[]{:S(2)}) collective-permute-start(bf16[1024,128]{1,0:T(8,128)(2,1)S(1)} %pack.3.refs_1_), channel_id=1, source_target_pairs={{0,4},{4,0},{1,5},{5,1},{2,6},{6,2},{3,7},{7,3},{8,12},{12,8},{9,1... | collective-permute-start | bytes 786440 | tf_op jit(solution)/shard_map/ppermute | solution.py:263
  10.9 0.2 constant_dynamic-slice_fusion.3
  11.1 2.9 %collective-permute-done.7.refs_2_ = bf16[512,128]{1,0:T(8,128)(2,1)S(1)} collective-permute-done((bf16[512,128]{1,0:T(8,128)(2,1)S(1)}, bf16[512,128]{1,0:T(8,128)(2,1)S(1)}, u32[]{:S(2)}, u32[]{:S(2)}) %collective-permute-start.7) | collective-permute-done | bytes 131104 | tf_op jit(solution)/shard_map/ppermute | solution.py:263
  14.1 1.2 %collective-permute-start.12 = (bf16[512,128]{1,0:T(8,128)(2,1)S(1)}, bf16[512,128]{1,0:T(8,128)(2,1)S(1)}, u32[]{:S(2)}, u32[]{:S(2)}) collective-permute-start(bf16[512,128]{1,0:T(8,128)(2,1)S(1)} %collective-permute-done.7.refs_2_), channel_id=1, source_target_pairs={{0,16},{8,24},{16,0},{24,8},{1,17},{9,25},{17,1},{25,9},{2,18},{10... | collective-permute-start | bytes 393224 | tf_op jit(solution)/shard_map/ppermute | solution.py:263
  15.3 0.1 copy_bitcast_fusion.1
  15.4 0.0 copy-start.6
  15.4 0.7 %collective-permute-start.4 = (bf16[512,128]{1,0:T(8,128)(2,1)S(1)}, bf16[512,128]{1,0:T(8,128)(2,1)S(1)}, u32[]{:S(2)}, u32[]{:S(2)}) collective-permute-start(bf16[512,128]{1,0:T(8,128)(2,1)S(1)} %collective-permute-done.refs_1_), channel_id=1, source_target_pairs={{0,2},{1,3},{2,0},{3,1},{4,6},{5,7},{6,4},{7,5},{8,10},{9,11},{10,... | collective-permute-start | bytes 393224 | tf_op jit(solution)/shard_map/ppermute | solution.py:263
  16.1 3.3 %collective-permute-done.2.first_ref.refs_2_ = bf16[512,128]{1,0:T(8,128)(2,1)S(1)} collective-permute-done((bf16[512,128]{1,0:T(8,128)(2,1)S(1)}, bf16[512,128]{1,0:T(8,128)(2,1)S(1)}, u32[]{:S(2)}, u32[]{:S(2)}) %collective-permute-start.2) | collective-permute-done | bytes 131104 | tf_op jit(solution)/shard_map/ppermute | solution.py:263
  19.4 1.2 %collective-permute-start.3 = (bf16[512,128]{1,0:T(8,128)(2,1)S(1)}, bf16[512,128]{1,0:T(8,128)(2,1)S(1)}, u32[]{:S(2)}, u32[]{:S(2)}) collective-permute-start(bf16[512,128]{1,0:T(8,128)(2,1)S(1)} %collective-permute-done.2.first_ref.refs_2_), channel_id=1, source_target_pairs={{0,4},{4,0},{1,5},{5,1},{2,6},{6,2},{3,7},{7,3},{8,12},{12,8},{9,1... | collective-permute-start | bytes 393224 | tf_op jit(solution)/shard_map/ppermute | solution.py:263
  20.7 3.8 %collective-permute-start.9 = (bf16[2048,128]{1,0:T(8,128)(2,1)S(1)}, bf16[2048,128]{1,0:T(8,128)(2,1)S(1)}, u32[]{:S(2)}, u32[]{:S(2)}) collective-permute-start(bf16[2048,128]{1,0:T(8,128)(2,1)S(1)} %pack.4.refs_4_), channel_id=1, source_target_pairs={{0,8},{8,0},{16,24},{24,16},{1,9},{9,1},{17,25},{25,17},{2,10},{10... | collective-permute-start | bytes 1572872 | tf_op jit(solution)/shard_map/ppermute | solution.py:263
  24.5 0.1 broadcast_in_dim.2.refs_10_
  24.6 1.3 %collective-permute-start.14 = (bf16[512,128]{1,0:T(8,128)(2,1)S(1)}, bf16[512,128]{1,0:T(8,128)(2,1)S(1)}, u32[]{:S(2)}, u32[]{:S(2)}) collective-permute-start(bf16[512,128]{1,0:T(8,128)(2,1)S(1)} %collective-permute-done.8.refs_3_), channel_id=1, source_target_pairs={{0,16},{8,24},{16,0},{24,8},{1,17},{9,25},{17,1},{25,9},{2,18},{10... | collective-permute-start | bytes 393224 | tf_op jit(solution)/shard_map/ppermute | solution.py:263
  25.9 0.4 collective-permute-start.13
  26.2 0.1 copy_bitcast_fusion.3
  26.4 3.3 %collective-permute-done.14.refs_8_ = bf16[512,128]{1,0:T(8,128)(2,1)S(1)} collective-permute-done((bf16[512,128]{1,0:T(8,128)(2,1)S(1)}, bf16[512,128]{1,0:T(8,128)(2,1)S(1)}, u32[]{:S(2)}, u32[]{:S(2)}) %collective-permute-start.14) | collective-permute-done | bytes 131104 | tf_op jit(solution)/shard_map/ppermute | solution.py:263
  29.7 0.8 %collective-permute-start.15 = (bf16[512,128]{1,0:T(8,128)(2,1)S(1)}, bf16[512,128]{1,0:T(8,128)(2,1)S(1)}, u32[]{:S(2)}, u32[]{:S(2)}) collective-permute-start(bf16[512,128]{1,0:T(8,128)(2,1)S(1)} %collective-permute-done.14.refs_8_), channel_id=1, source_target_pairs={{0,8},{8,0},{16,24},{24,16},{1,9},{9,1},{17,25},{25,17},{2,10},{10... | collective-permute-start | bytes 393224 | tf_op jit(solution)/shard_map/ppermute | solution.py:263
  30.5 0.5 pad_maximum_fusion
  31.0 0.7 %copy.38 = bf16[64,8,2,128]{3,1,2,0:T(8,128)(2,1)} copy(bf16[64,8,2,128]{3,2,1,0:T(2,128)(2,1)S(1)} %bitcast.49) | data formatting | bytes 524288
  31.7 1.1 %copy.27.refs_11_ = bf16[256,512]{1,0:T(8,128)(2,1)S(1)} copy(bf16[256,512]{0,1:T(8,128)(2,1)} %bitcast.50) | data formatting | bytes 524288 | tf_op jit(solution)/shard_map/reshape | solution.py:286
  32.8 0.1 pad_add_fusion.refs_0_
  32.9 1.0 %collective-permute-start.5 = (bf16[512,128]{1,0:T(8,128)(2,1)S(1)}, bf16[512,128]{1,0:T(8,128)(2,1)S(1)}, u32[]{:S(2)}, u32[]{:S(2)}) collective-permute-start(bf16[512,128]{1,0:T(8,128)(2,1)S(1)} %collective-permute-done.4.second_ref.refs_3_), channel_id=1, source_target_pairs={{0,4},{4,0},{1,5},{5,1},{2,6},{6,2},{3,7},{7,3},{8,12},{12,8},{9,1... | collective-permute-start | bytes 393224 | tf_op jit(solution)/shard_map/ppermute | solution.py:263
  33.9 3.0 %update_first.1.refs_12_ = bf16[16,64,128]{2,1,0:T(8,128)(2,1)S(1)} custom-call(s32[4]{0:T(128)S(1)} %pad_add_fusion.refs_0_, bf16[1024,128]{1,0:T(8,128)(2,1)S(1)} %pack.3.refs_1_, bf16[512,128]{1,0:T(8,128)(2,1)S(1)} %collective-permute-done.2.first_ref.refs_2_, bf16[512,128]{1,0:T(8,128)(2,1)S(1)} %collective-permute-done.4.second_ref.refs_3_, ...), custom_call_target="tpu_custom_call" | custom-call | flops 1610612736 | bytes 2097152 | tf_op jit(solution)/shard_map/update_first/pallas_call | solution.py:338
  36.9 1.1 %collective-permute-done.5.refs_3_ = bf16[512,128]{1,0:T(8,128)(2,1)S(1)} collective-permute-done((bf16[512,128]{1,0:T(8,128)(2,1)S(1)}, bf16[512,128]{1,0:T(8,128)(2,1)S(1)}, u32[]{:S(2)}, u32[]{:S(2)}) %collective-permute-start.5) | collective-permute-done | bytes 131104 | tf_op jit(solution)/shard_map/ppermute | solution.py:263
  38.1 3.1 %update_last.1 = (bf16[16,64,128]{2,1,0:T(8,128)(2,1)S(1)}, bf16[32,16,128]{2,1,0:T(8,128)(2,1)S(1)}, bf16[32,16,128]{2,1,0:T(8,128)(2,1)S(1)}, bf16[32,16,128]{...) custom-call(s32[4]{0:T(128)S(1)} %pad_add_fusion.refs_0_, ...), custom_call_target="tpu_custom_call" | custom-call | flops 1610612736 | bytes 2097152 | tf_op jit(solution)/shard_map/update_last/pallas_call | solution.py:338
  41.2 0.0 copy-start.1
  41.2 2.1 %collective-permute-start.16 = (bf16[32,16,128]{2,1,0:T(8,128)(2,1)S(1)}, bf16[32,16,128]{2,1,0:T(8,128)(2,1)S(1)}, u32[]{:S(2)}, u32[]{:S(2)}) collective-permute-start(bf16[32,16,128]{2,1,0:T(8,128)(2,1)S(1)} %get-tuple-element.21), channel_id=1, source_target_pairs={{0,0},{1,1},{2,2},{3,3},{4,16},{5,17},{6,18},{7,19},{8,10},{9,11},... | collective-permute-start | bytes 393224 | tf_op jit(solution)/shard_map/ppermute | solution.py:386
  43.3 4.1 %collective-permute-start.17 = (bf16[32,16,128]{2,1,0:T(8,128)(2,1)S(1)}, bf16[32,16,128]{2,1,0:T(8,128)(2,1)S(1)}, u32[]{:S(2)}, u32[]{:S(2)}) collective-permute-start(bf16[32,16,128]{2,1,0:T(8,128)(2,1)S(1)} %get-tuple-element.22), channel_id=1, source_target_pairs={{0,2},{1,3},{2,0},{3,1},{4,6},{5,7},{6,4},{7,5},{8,8},{9,9},{10,10... | collective-permute-start | bytes 393224 | tf_op jit(solution)/shard_map/ppermute | solution.py:386
  47.4 2.4 %collective-permute-start.18 = (bf16[32,16,128]{2,1,0:T(8,128)(2,1)S(1)}, bf16[32,16,128]{2,1,0:T(8,128)(2,1)S(1)}, u32[]{:S(2)}, u32[]{:S(2)}) collective-permute-start(bf16[32,16,128]{2,1,0:T(8,128)(2,1)S(1)} %get-tuple-element.23), channel_id=1, source_target_pairs={{0,1},{1,0},{2,3},{3,2},{4,17},{5,16},{6,19},{7,18},{8,10},{9,11},... | collective-permute-start | bytes 393224 | tf_op jit(solution)/shard_map/ppermute | solution.py:386
  49.8 3.2 %collective-permute-start.20 = (bf16[32,16,128]{2,1,0:T(8,128)(2,1)S(1)}, bf16[32,16,128]{2,1,0:T(8,128)(2,1)S(1)}, u32[]{:S(2)}, u32[]{:S(2)}) collective-permute-start(bf16[32,16,128]{2,1,0:T(8,128)(2,1)S(1)} %get-tuple-element.25), channel_id=1, source_target_pairs={{0,8},{1,9},{2,10},{3,11},{4,24},{5,25},{6,26},{7,27},{8,0},{9,1},... | collective-permute-start | bytes 393224 | tf_op jit(solution)/shard_map/ppermute | solution.py:386
  53.0 1.9 %collective-permute-start.21 = (bf16[32,16,128]{2,1,0:T(8,128)(2,1)S(1)}, bf16[32,16,128]{2,1,0:T(8,128)(2,1)S(1)}, u32[]{:S(2)}, u32[]{:S(2)}) collective-permute-start(bf16[32,16,128]{2,1,0:T(8,128)(2,1)S(1)} %get-tuple-element.26), channel_id=1, source_target_pairs={{0,9},{1,8},{2,11},{3,10},{4,25},{5,24},{6,27},{7,26},{8,1},{9,0},... | collective-permute-start | bytes 393224 | tf_op jit(solution)/shard_map/ppermute | solution.py:386
  54.9 0.1 fusion.refs_12_
  55.0 1.1 %collective-permute-done.18.refs_5_ = bf16[32,16,128]{2,1,0:T(8,128)(2,1)S(1)} collective-permute-done((bf16[32,16,128]{2,1,0:T(8,128)(2,1)S(1)}, bf16[32,16,128]{2,1,0:T(8,128)(2,1)S(1)}, u32[]{:S(2)}, u32[]{:S(2)}) %collective-permute-start.18) | collective-permute-done | bytes 131104 | tf_op jit(solution)/shard_map/ppermute | solution.py:386
  56.2 3.6 %collective-permute-done.19.refs_6_ = bf16[32,16,128]{2,1,0:T(8,128)(2,1)S(1)} collective-permute-done((bf16[32,16,128]{2,1,0:T(8,128)(2,1)S(1)}, bf16[32,16,128]{2,1,0:T(8,128)(2,1)S(1)}, u32[]{:S(2)}, u32[]{:S(2)}) %collective-permute-start.19) | collective-permute-done | bytes 131104 | tf_op jit(solution)/shard_map/ppermute | solution.py:386
  59.8 1.5 %collective-permute-done.21.refs_8_ = bf16[32,16,128]{2,1,0:T(8,128)(2,1)S(1)} collective-permute-done((bf16[32,16,128]{2,1,0:T(8,128)(2,1)S(1)}, bf16[32,16,128]{2,1,0:T(8,128)(2,1)S(1)}, u32[]{:S(2)}, u32[]{:S(2)}) %collective-permute-start.21) | collective-permute-done | bytes 131104 | tf_op jit(solution)/shard_map/ppermute | solution.py:386
  61.3 4.0 %finish.1 = bf16[16,128,128]{2,1,0:T(8,128)(2,1)} custom-call(s32[4]{0:T(128)S(1)} %pad_add_fusion.refs_0_, bf16[16,128,128]{2,1,0:T(8,128)(2,1)S(1)} %copy-done, bf16[16,64,128]{2,1,0:T(8,128)(2,1)S(1)} %get-tuple-element.20.refs_2_, bf16[32,16,128]{2,1,0:T(8,128)(2,1)S(1)} %collective-permute-done.16.refs_3_, ...), custom_call_target="tpu_custom_call" | custom-call | tf_op jit(solution)/shard_map/finish/pallas_call | solution.py:391
  (41 shorter events, 0.2 us)
Async XLA Ops:
  1.5 1.8 %copy-start.3 = (bf16[128,32,64]{0,2,1:T(8,128)(2,1)S(1)}, bf16[128,32,64]{0,2,1:T(8,128)(2,1)}, u32[]{:S(2)}) copy-start(bf16[128,32,64]{0,2,1:T(8,128)(2,1)} %param.10) | copy-start | bytes 1572868
  1.7 5.7 %collective-permute-start.10 = (bf16[512,128]{1,0:T(8,128)(2,1)S(1)}, bf16[512,128]{1,0:T(8,128)(2,1)S(1)}, u32[]{:S(2)}, u32[]{:S(2)}) collective-permute-start(bf16[512,128]{1,0:T(8,128)(2,1)S(1)} %bitcast.45), channel_id=1, source_target_pairs={{0,16},{8,24},{16,0},{24,8},{1,17},{9,25},{17,1},{25,9},{2,18},{10... | collective-permute-start | bytes 393224 | tf_op jit(solution)/shard_map/ppermute | solution.py:263
  1.7 5.7 %collective-permute-start.6 = (bf16[512,128]{1,0:T(8,128)(2,1)S(1)}, bf16[512,128]{1,0:T(8,128)(2,1)S(1)}, u32[]{:S(2)}, u32[]{:S(2)}) collective-permute-start(bf16[512,128]{1,0:T(8,128)(2,1)S(1)} %bitcast.46), channel_id=1, source_target_pairs={{0,1},{1,0},{2,3},{3,2},{4,5},{5,4},{6,7},{7,6},{8,9},{9,8},{10,11... | collective-permute-start | bytes 393224 | tf_op jit(solution)/shard_map/ppermute | solution.py:263
  3.7 6.0 %collective-permute-start = (bf16[512,128]{1,0:T(8,128)(2,1)S(1)}, bf16[512,128]{1,0:T(8,128)(2,1)S(1)}, u32[]{:S(2)}, u32[]{:S(2)}) collective-permute-start(bf16[512,128]{1,0:T(8,128)(2,1)S(1)} %get-tuple-element.27), channel_id=1, source_target_pairs={{0,1},{1,0},{2,3},{3,2},{4,5},{5,4},{6,7},{7,6},{8,9},{9,8},{10,11... | collective-permute-start | bytes 393224 | tf_op jit(solution)/shard_map/ppermute | solution.py:263
  4.4 9.7 %collective-permute-start.7 = (bf16[512,128]{1,0:T(8,128)(2,1)S(1)}, bf16[512,128]{1,0:T(8,128)(2,1)S(1)}, u32[]{:S(2)}, u32[]{:S(2)}) collective-permute-start(bf16[512,128]{1,0:T(8,128)(2,1)S(1)} %bitcast.54), channel_id=1, source_target_pairs={{0,3},{1,2},{2,1},{3,0},{4,7},{5,6},{6,5},{7,4},{8,11},{9,10},{10,... | collective-permute-start | bytes 393224 | tf_op jit(solution)/shard_map/ppermute | solution.py:263
  7.4 6.7 %collective-permute-start.11 = (bf16[512,128]{1,0:T(8,128)(2,1)S(1)}, bf16[512,128]{1,0:T(8,128)(2,1)S(1)}, u32[]{:S(2)}, u32[]{:S(2)}) collective-permute-start(bf16[512,128]{1,0:T(8,128)(2,1)S(1)} %collective-permute-done.6.refs_1_), channel_id=1, source_target_pairs={{0,16},{8,24},{16,0},{24,8},{1,17},{9,25},{17,1},{25,9},{2,18},{10... | collective-permute-start | bytes 393224 | tf_op jit(solution)/shard_map/ppermute | solution.py:263
  8.6 10.8 %collective-permute-start.2 = (bf16[512,128]{1,0:T(8,128)(2,1)S(1)}, bf16[512,128]{1,0:T(8,128)(2,1)S(1)}, u32[]{:S(2)}, u32[]{:S(2)}) collective-permute-start(bf16[512,128]{1,0:T(8,128)(2,1)S(1)} %get-tuple-element.28.refs_0_), channel_id=1, source_target_pairs={{0,2},{1,3},{2,0},{3,1},{4,6},{5,7},{6,4},{7,5},{8,10},{9,11},{10,... | collective-permute-start | bytes 393224 | tf_op jit(solution)/shard_map/ppermute | solution.py:263
  9.6 1.3 %copy-start.4 = (bf16[1024,128]{1,0:T(8,128)(2,1)S(1)}, bf16[1024,128]{1,0:T(8,128)(2,1)}, u32[]{:S(2)}) copy-start(bf16[1024,128]{1,0:T(8,128)(2,1)} %param.12) | copy-start | bytes 786436
  9.6 14.9 %collective-permute-start.1 = (bf16[1024,128]{1,0:T(8,128)(2,1)S(1)}, bf16[1024,128]{1,0:T(8,128)(2,1)S(1)}, u32[]{:S(2)}, u32[]{:S(2)}) collective-permute-start(bf16[1024,128]{1,0:T(8,128)(2,1)S(1)} %pack.3.refs_1_), channel_id=1, source_target_pairs={{0,4},{4,0},{1,5},{5,1},{2,6},{6,2},{3,7},{7,3},{8,12},{12,8},{9,1... | collective-permute-start | bytes 786440 | tf_op jit(solution)/shard_map/ppermute | solution.py:263
  14.1 6.6 %collective-permute-start.8 = (bf16[512,128]{1,0:T(8,128)(2,1)S(1)}, bf16[512,128]{1,0:T(8,128)(2,1)S(1)}, u32[]{:S(2)}, u32[]{:S(2)}) collective-permute-start(bf16[512,128]{1,0:T(8,128)(2,1)S(1)} %collective-permute-done.7.refs_2_), channel_id=1, source_target_pairs={{0,1},{1,0},{2,3},{3,2},{4,5},{5,4},{6,7},{7,6},{8,9},{9,8},{10,11... | collective-permute-start | bytes 393224 | tf_op jit(solution)/shard_map/ppermute | solution.py:263
  14.1 10.4 %collective-permute-start.12 = (bf16[512,128]{1,0:T(8,128)(2,1)S(1)}, bf16[512,128]{1,0:T(8,128)(2,1)S(1)}, u32[]{:S(2)}, u32[]{:S(2)}) collective-permute-start(bf16[512,128]{1,0:T(8,128)(2,1)S(1)} %collective-permute-done.7.refs_2_), channel_id=1, source_target_pairs={{0,16},{8,24},{16,0},{24,8},{1,17},{9,25},{17,1},{25,9},{2,18},{10... | collective-permute-start | bytes 393224 | tf_op jit(solution)/shard_map/ppermute | solution.py:263
  15.4 9.1 %copy-start.6 = (f32[128]{0:T(128)S(1)}, f32[128]{0:T(128)}, u32[]{:S(2)}) copy-start(f32[128]{0:T(128)} %param.13) | copy-start | bytes 1540
  15.4 10.9 %collective-permute-start.4 = (bf16[512,128]{1,0:T(8,128)(2,1)S(1)}, bf16[512,128]{1,0:T(8,128)(2,1)S(1)}, u32[]{:S(2)}, u32[]{:S(2)}) collective-permute-start(bf16[512,128]{1,0:T(8,128)(2,1)S(1)} %collective-permute-done.refs_1_), channel_id=1, source_target_pairs={{0,2},{1,3},{2,0},{3,1},{4,6},{5,7},{6,4},{7,5},{8,10},{9,11},{10,... | collective-permute-start | bytes 393224 | tf_op jit(solution)/shard_map/ppermute | solution.py:263
  19.4 6.9 %collective-permute-start.3 = (bf16[512,128]{1,0:T(8,128)(2,1)S(1)}, bf16[512,128]{1,0:T(8,128)(2,1)S(1)}, u32[]{:S(2)}, u32[]{:S(2)}) collective-permute-start(bf16[512,128]{1,0:T(8,128)(2,1)S(1)} %collective-permute-done.2.first_ref.refs_2_), channel_id=1, source_target_pairs={{0,4},{4,0},{1,5},{5,1},{2,6},{6,2},{3,7},{7,3},{8,12},{12,8},{9,1... | collective-permute-start | bytes 393224 | tf_op jit(solution)/shard_map/ppermute | solution.py:263
  20.7 13.2 %collective-permute-start.9 = (bf16[2048,128]{1,0:T(8,128)(2,1)S(1)}, bf16[2048,128]{1,0:T(8,128)(2,1)S(1)}, u32[]{:S(2)}, u32[]{:S(2)}) collective-permute-start(bf16[2048,128]{1,0:T(8,128)(2,1)S(1)} %pack.4.refs_4_), channel_id=1, source_target_pairs={{0,8},{8,0},{16,24},{24,16},{1,9},{9,1},{17,25},{25,17},{2,10},{10... | collective-permute-start | bytes 1572872 | tf_op jit(solution)/shard_map/ppermute | solution.py:263
  24.6 5.1 %collective-permute-start.14 = (bf16[512,128]{1,0:T(8,128)(2,1)S(1)}, bf16[512,128]{1,0:T(8,128)(2,1)S(1)}, u32[]{:S(2)}, u32[]{:S(2)}) collective-permute-start(bf16[512,128]{1,0:T(8,128)(2,1)S(1)} %collective-permute-done.8.refs_3_), channel_id=1, source_target_pairs={{0,16},{8,24},{16,0},{24,8},{1,17},{9,25},{17,1},{25,9},{2,18},{10... | collective-permute-start | bytes 393224 | tf_op jit(solution)/shard_map/ppermute | solution.py:263
  25.9 8.1 %collective-permute-start.13 = (bf16[1536,128]{1,0:T(8,128)(2,1)S(1)}, bf16[1536,128]{1,0:T(8,128)(2,1)S(1)}, u32[]{:S(2)}, u32[]{:S(2)}) collective-permute-start(bf16[1536,128]{1,0:T(8,128)(2,1)S(1)} %pack.5.refs_6_), channel_id=1, source_target_pairs={{0,8},{8,0},{16,24},{24,16},{1,9},{9,1},{17,25},{25,17},{2,10},{10... | collective-permute-start | bytes 1179656 | tf_op jit(solution)/shard_map/ppermute | solution.py:263
  29.7 4.2 %collective-permute-start.15 = (bf16[512,128]{1,0:T(8,128)(2,1)S(1)}, bf16[512,128]{1,0:T(8,128)(2,1)S(1)}, u32[]{:S(2)}, u32[]{:S(2)}) collective-permute-start(bf16[512,128]{1,0:T(8,128)(2,1)S(1)} %collective-permute-done.14.refs_8_), channel_id=1, source_target_pairs={{0,8},{8,0},{16,24},{24,16},{1,9},{9,1},{17,25},{25,17},{2,10},{10... | collective-permute-start | bytes 393224 | tf_op jit(solution)/shard_map/ppermute | solution.py:263
  32.9 5.1 %collective-permute-start.5 = (bf16[512,128]{1,0:T(8,128)(2,1)S(1)}, bf16[512,128]{1,0:T(8,128)(2,1)S(1)}, u32[]{:S(2)}, u32[]{:S(2)}) collective-permute-start(bf16[512,128]{1,0:T(8,128)(2,1)S(1)} %collective-permute-done.4.second_ref.refs_3_), channel_id=1, source_target_pairs={{0,4},{4,0},{1,5},{5,1},{2,6},{6,2},{3,7},{7,3},{8,12},{12,8},{9,1... | collective-permute-start | bytes 393224 | tf_op jit(solution)/shard_map/ppermute | solution.py:263
  36.9 24.4 %copy-start = (bf16[16,128,128]{2,1,0:T(8,128)(2,1)S(1)}, bf16[16,128,128]{2,1,0:T(8,128)(2,1)}, u32[]{:S(2)}) copy-start(bf16[16,128,128]{2,1,0:T(8,128)(2,1)} %refs_1_.1) | copy-start | bytes 1572868
  38.1 5.2 %copy-start.5 = (f32[512]{0:T(512)S(1)}, f32[512]{0:T(512)}, u32[]{:S(2)}) copy-start(f32[512]{0:T(512)} %param.17) | copy-start | bytes 6148
  38.1 5.2 %copy-start.7 = (f32[128]{0:T(128)S(1)}, f32[128]{0:T(128)}, u32[]{:S(2)}) copy-start(f32[128]{0:T(128)} %param.19) | copy-start | bytes 1540
  38.1 5.2 %copy-start.8 = (f32[128]{0:T(128)S(1)}, f32[128]{0:T(128)}, u32[]{:S(2)}) copy-start(f32[128]{0:T(128)} %param.15) | copy-start | bytes 1540
  38.1 23.3 %copy-start.2 = (bf16[512,128]{1,0:T(8,128)(2,1)S(1)}, bf16[512,128]{1,0:T(8,128)(2,1)}, u32[]{:S(2)}) copy-start(bf16[512,128]{1,0:T(8,128)(2,1)} %refs_10_.1) | copy-start | bytes 393220
  41.2 20.1 %copy-start.1 = (bf16[128,512]{1,0:T(8,128)(2,1)S(1)}, bf16[128,512]{1,0:T(8,128)(2,1)}, u32[]{:S(2)}) copy-start(bf16[128,512]{1,0:T(8,128)(2,1)} %refs_9_.1) | copy-start | bytes 393220
  41.2 11.8 %collective-permute-start.16 = (bf16[32,16,128]{2,1,0:T(8,128)(2,1)S(1)}, bf16[32,16,128]{2,1,0:T(8,128)(2,1)S(1)}, u32[]{:S(2)}, u32[]{:S(2)}) collective-permute-start(bf16[32,16,128]{2,1,0:T(8,128)(2,1)S(1)} %get-tuple-element.21), channel_id=1, source_target_pairs={{0,0},{1,1},{2,2},{3,3},{4,16},{5,17},{6,18},{7,19},{8,10},{9,11},... | collective-permute-start | bytes 393224 | tf_op jit(solution)/shard_map/ppermute | solution.py:386
  43.3 11.7 %collective-permute-start.17 = (bf16[32,16,128]{2,1,0:T(8,128)(2,1)S(1)}, bf16[32,16,128]{2,1,0:T(8,128)(2,1)S(1)}, u32[]{:S(2)}, u32[]{:S(2)}) collective-permute-start(bf16[32,16,128]{2,1,0:T(8,128)(2,1)S(1)} %get-tuple-element.22), channel_id=1, source_target_pairs={{0,2},{1,3},{2,0},{3,1},{4,6},{5,7},{6,4},{7,5},{8,8},{9,9},{10,10... | collective-permute-start | bytes 393224 | tf_op jit(solution)/shard_map/ppermute | solution.py:386
  47.4 8.7 %collective-permute-start.18 = (bf16[32,16,128]{2,1,0:T(8,128)(2,1)S(1)}, bf16[32,16,128]{2,1,0:T(8,128)(2,1)S(1)}, u32[]{:S(2)}, u32[]{:S(2)}) collective-permute-start(bf16[32,16,128]{2,1,0:T(8,128)(2,1)S(1)} %get-tuple-element.23), channel_id=1, source_target_pairs={{0,1},{1,0},{2,3},{3,2},{4,17},{5,16},{6,19},{7,18},{8,10},{9,11},... | collective-permute-start | bytes 393224 | tf_op jit(solution)/shard_map/ppermute | solution.py:386
  49.8 9.9 %collective-permute-start.19 = (bf16[32,16,128]{2,1,0:T(8,128)(2,1)S(1)}, bf16[32,16,128]{2,1,0:T(8,128)(2,1)S(1)}, u32[]{:S(2)}, u32[]{:S(2)}) collective-permute-start(bf16[32,16,128]{2,1,0:T(8,128)(2,1)S(1)} %get-tuple-element.24), channel_id=1, source_target_pairs={{0,2},{1,3},{2,0},{3,1},{4,6},{5,7},{6,4},{7,5},{8,9},{9,8},{10,11... | collective-permute-start | bytes 393224 | tf_op jit(solution)/shard_map/ppermute | solution.py:386
  49.8 9.9 %collective-permute-start.20 = (bf16[32,16,128]{2,1,0:T(8,128)(2,1)S(1)}, bf16[32,16,128]{2,1,0:T(8,128)(2,1)S(1)}, u32[]{:S(2)}, u32[]{:S(2)}) collective-permute-start(bf16[32,16,128]{2,1,0:T(8,128)(2,1)S(1)} %get-tuple-element.25), channel_id=1, source_target_pairs={{0,8},{1,9},{2,10},{3,11},{4,24},{5,25},{6,26},{7,27},{8,0},{9,1},... | collective-permute-start | bytes 393224 | tf_op jit(solution)/shard_map/ppermute | solution.py:386
  53.0 8.3 %collective-permute-start.21 = (bf16[32,16,128]{2,1,0:T(8,128)(2,1)S(1)}, bf16[32,16,128]{2,1,0:T(8,128)(2,1)S(1)}, u32[]{:S(2)}, u32[]{:S(2)}) collective-permute-start(bf16[32,16,128]{2,1,0:T(8,128)(2,1)S(1)} %get-tuple-element.26), channel_id=1, source_target_pairs={{0,9},{1,8},{2,11},{3,10},{4,25},{5,24},{6,27},{7,26},{8,1},{9,0},... | collective-permute-start | bytes 393224 | tf_op jit(solution)/shard_map/ppermute | solution.py:386
